TPU v7x, 32 devices: a whole 2x2x4 slice. The times are simulated.
32 devices in a mesh: tok: 4 (over x, core), feat: 8 (over z, y).
Axes of the slice: x: 2, y: 2, z: 4, core: 2. Of those that a mesh axis runs over, the one named last changes fastest.
Arguments:
- inputs: bfloat16 [9248, 1024], P(('tok', 'feat')), may hold values from -6 to 6
- valid: int32 [16], P('tok'), may hold values 0 or 1
- cotangent: bfloat16 [9248, 1024], P(('tok', 'feat')), may hold values from -6 to 6
- w_query: bfloat16 [1024, 1024], P('feat'), may hold values from -0.1875 to 0.1875
- w_key: bfloat16 [1024, 1024], P('feat'), may hold values from -0.1875 to 0.1875
- w_value: bfloat16 [1024, 1024], P('feat'), may hold values from -0.1875 to 0.1875
- b_query: bfloat16 [1024], P('feat'), may hold values from -3 to 3
- b_value: bfloat16 [1024], P('feat'), may hold values from -0.59765625 to 0.59765625
- w_attn_out: bfloat16 [1024, 1024], P('feat'), may hold values from -2 to 2
- b_attn_out: bfloat16 [1024], replicated, may hold values from -0.59765625 to 0.59765625
- w_mlp_in: bfloat16 [1024, 4096], P(None, 'feat'), may hold values from -0.1875 to 0.1875
- b_mlp_in: bfloat16 [4096], P('feat'), may hold values from -3 to 3
- w_mlp_out: bfloat16 [4096, 1024], P('feat'), may hold values from -0.1875 to 0.1875
- b_mlp_out: bfloat16 [1024], replicated, may hold values from -0.59765625 to 0.59765625
- attention_norm_gain: bfloat16 [1024], replicated, may hold values from 0.5 to 1.5
- attention_norm_shift: bfloat16 [1024], replicated, may hold values from -0.59765625 to 0.59765625
- feedforward_norm_gain: bfloat16 [1024], replicated, may hold values from 0.5 to 1.5
- feedforward_norm_shift: bfloat16 [1024], replicated, may hold values from -0.59765625 to 0.59765625
Outputs:
- output: float32 [9248, 1024], P(('tok', 'feat'))
- layer_input_gradient: float32 [9248, 1024], P(('tok', 'feat'))
- grad_w_query: float32 [1024, 1024], P('feat')
- grad_w_key: float32 [1024, 1024], P('feat')
- grad_w_value: float32 [1024, 1024], P('feat')
- grad_b_query: float32 [1024], P('feat')
- grad_b_value: float32 [1024], P('feat')
- grad_w_attn_out: float32 [1024, 1024], P('feat')
- grad_b_attn_out: float32 [1024], replicated
- grad_w_mlp_in: float32 [1024, 4096], P(None, 'feat')
- grad_b_mlp_in: float32 [4096], P('feat')
- grad_w_mlp_out: float32 [4096, 1024], P('feat')
- grad_b_mlp_out: float32 [1024], replicated
- attention_gain_gradient: float32 [1024], replicated
- grad_s_attn: float32 [1024], replicated
- feedforward_gain_gradient: float32 [1024], replicated
- grad_s_mlp: float32 [1024], replicated
- stream_rms: float32 [4], replicated
Inputs may be any that keep to these rules, and one draw needn't show every extreme that they name: `valid`: 1 marks a real image, 0 a padded one.
All inputs are finite; a program needn't handle non-finite values. No bound on the sum of `valid` on one device may be relied on, other than what follows from the above.
Results may differ from a plain program's by a relative error of at most 0.017.
Values may be sent and summed in bfloat16 or wider, within the bound.
No kernel may reach another device: no remote copies, remote signals or barrier semaphores. Data moves between devices by JAX's collectives and lax.ppermute only.
A program may use at most 128 MiB of HBM per device.

v0:
```python
import jax
import jax.numpy as jnp
from jax import lax
from jax.sharding import PartitionSpec as P

D = 1024
DH = 64
SEQ = 577


EPSILON = 1e-05
SLOPE = 1.702


def gelu_slope(values):
    sigmoid = jax.nn.sigmoid(SLOPE * values)
    return sigmoid + SLOPE * values * sigmoid * (1.0 - sigmoid)


def column_sums(values):
    return jnp.sum(values.astype(jnp.float32), axis=0)


def split_heads(values):
    return values.reshape(values.shape[0], values.shape[1] // DH, DH)


def apply_layer_norm(values):
    center = jnp.mean(values, axis=1, keepdims=True)
    spread = jnp.mean(values * values, axis=1, keepdims=True) - center * center
    inverse_deviation = lax.rsqrt(spread + EPSILON)
    return ((values - center) * inverse_deviation, inverse_deviation)


def layer_norm_backward(normalized_gradient, centered_scaled, inverse_deviation, norm_gain):
    scaled_output = normalized_gradient * norm_gain.astype(jnp.float32)
    plain_output = jnp.mean(scaled_output, axis=1, keepdims=True)
    cross_term = jnp.mean(scaled_output * centered_scaled, axis=1, keepdims=True)
    return inverse_deviation * (scaled_output - plain_output - centered_scaled * cross_term)


def image_forward(blocks):
    query_img, key_img, value_img = blocks
    scale = DH ** (-0.5)
    query_heads = split_heads(query_img)
    key_heads = split_heads(key_img)
    value_heads = split_heads(value_img)
    scores = (
        jnp.einsum("qhd,khd->hqk", query_heads, key_heads, preferred_element_type=jnp.float32)
        * scale
    )
    top_score = jnp.max(scores, axis=-1, keepdims=True)
    weights = jnp.exp(scores - top_score)
    total = jnp.sum(weights, axis=-1, keepdims=True)
    probs = (weights / total).astype(jnp.bfloat16)
    mixed = jnp.einsum("hqk,khd->qhd", probs, value_heads, preferred_element_type=jnp.float32)
    log_total = top_score[..., 0] + jnp.log(total[..., 0])
    return (mixed.reshape(query_img.shape).astype(jnp.bfloat16), log_total)


def image_backward(blocks):
    query_img, key_img, value_img, grad_img, log_total = blocks
    scale = DH ** (-0.5)
    query_heads = split_heads(query_img)
    key_heads = split_heads(key_img)
    value_heads = split_heads(value_img)
    grad_heads = split_heads(grad_img)
    scores = (
        jnp.einsum("qhd,khd->hqk", query_heads, key_heads, preferred_element_type=jnp.float32)
        * scale
    )
    probs = jnp.exp(scores - log_total[..., None])
    probs_low = probs.astype(jnp.bfloat16)
    grad_probs = jnp.einsum(
        "qhd,khd->hqk", grad_heads, value_heads, preferred_element_type=jnp.float32
    )
    grad_value = jnp.einsum(
        "hqk,qhd->khd", probs_low, grad_heads, preferred_element_type=jnp.float32
    )
    inner = jnp.sum(probs * grad_probs, axis=-1, keepdims=True)
    grad_scores = (probs * (grad_probs - inner)).astype(jnp.bfloat16)
    grad_query = (
        jnp.einsum("hqk,khd->qhd", grad_scores, key_heads, preferred_element_type=jnp.float32)
        * scale
    )
    grad_key = (
        jnp.einsum("hqk,qhd->khd", grad_scores, query_heads, preferred_element_type=jnp.float32)
        * scale
    )
    shape_img = query_img.shape
    return (
        grad_query.reshape(shape_img).astype(jnp.bfloat16),
        grad_key.reshape(shape_img).astype(jnp.bfloat16),
        grad_value.reshape(shape_img).astype(jnp.bfloat16),
    )


def by_image(values, images):
    return values.reshape(images, values.shape[0] // images, values.shape[1])


def on_device(
    inputs,
    valid,
    cotangent,
    w_query,
    w_key,
    w_value,
    b_query,
    b_value,
    w_attn_out,
    b_attn_out,
    w_mlp_in,
    b_mlp_in,
    w_mlp_out,
    b_mlp_out,
    attention_norm_gain,
    attention_norm_shift,
    feedforward_norm_gain,
    feedforward_norm_shift,
):
    row_count, width = inputs.shape
    images = valid.shape[0]
    group_rows = images * SEQ
    parts = lax.axis_size("feat")
    extra = row_count * parts - group_rows
    width_local = w_query.shape[0]
    hidden_local = w_mlp_out.shape[0]
    global_rows = lax.axis_index("feat") * row_count + jnp.arange(row_count, dtype=jnp.int32)
    owner = global_rows // SEQ
    matches = (owner[:, None] == jnp.arange(images, dtype=jnp.int32)[None, :]).astype(jnp.float32)
    row_mask = jnp.sum(matches * valid.astype(jnp.float32)[None, :], axis=1)
    live = (global_rows < group_rows).astype(jnp.float32)[:, None]

    def padded(values):
        return jnp.pad(values, ((0, extra), (0, 0)))

    local_input_rows = inputs.astype(jnp.float32)
    first_centered_scaled, first_inverse_deviation = apply_layer_norm(local_input_rows)
    normalized_first = (
        first_centered_scaled * attention_norm_gain.astype(jnp.float32)
        + attention_norm_shift.astype(jnp.float32)
    ).astype(jnp.bfloat16)
    normed_full = lax.all_gather(normalized_first, "feat", axis=0, tiled=True)[:group_rows]
    w_qkv = jnp.concatenate([w_query, w_key, w_value], axis=0)
    projected = jnp.einsum("rd,cd->rc", normed_full, w_qkv, preferred_element_type=jnp.float32)
    queries = (projected[:, :width_local] + b_query.astype(jnp.float32)).astype(jnp.bfloat16)
    key_rows = projected[:, width_local : 2 * width_local].astype(jnp.bfloat16)
    value_rows = (projected[:, 2 * width_local :] + b_value.astype(jnp.float32)).astype(
        jnp.bfloat16
    )
    mixed, log_totals = lax.map(
        image_forward,
        (by_image(queries, images), by_image(key_rows, images), by_image(value_rows, images)),
    )
    mixed = mixed.reshape(group_rows, width_local)
    partial_out = jnp.dot(mixed, w_attn_out, preferred_element_type=jnp.float32)
    attn = lax.psum_scatter(
        padded(partial_out), "feat", scatter_dimension=0, tiled=True
    ) + b_attn_out.astype(jnp.float32)
    middle_state = local_input_rows + attn
    second_centered_scaled, second_inverse_deviation = apply_layer_norm(middle_state)
    normalized_middle = (
        second_centered_scaled * feedforward_norm_gain.astype(jnp.float32)
        + feedforward_norm_shift.astype(jnp.float32)
    ).astype(jnp.bfloat16)
    mid_full = lax.all_gather(normalized_middle, "feat", axis=0, tiled=True)[:group_rows]
    hidden = jnp.dot(mid_full, w_mlp_in, preferred_element_type=jnp.float32) + b_mlp_in.astype(
        jnp.float32
    )
    active = (hidden * jax.nn.sigmoid(SLOPE * hidden)).astype(jnp.bfloat16)
    partial_mlp = jnp.dot(active, w_mlp_out, preferred_element_type=jnp.float32)
    branch = lax.psum_scatter(
        padded(partial_mlp).astype(jnp.bfloat16), "feat", scatter_dimension=0, tiled=True
    ).astype(jnp.float32) + b_mlp_out.astype(jnp.float32)
    output = (middle_state + branch) * live
    output_gradient = cotangent.astype(jnp.float32) * row_mask[:, None]
    grad_branch = output_gradient.astype(jnp.bfloat16)
    grad_b_mlp_out = column_sums(grad_branch)
    branch_full = lax.all_gather(grad_branch, "feat", axis=0, tiled=True)[:group_rows]
    grad_w_mlp_out = jnp.einsum(
        "rf,rd->fd", active, branch_full, preferred_element_type=jnp.float32
    )
    grad_active = jnp.einsum(
        "rd,fd->rf", branch_full, w_mlp_out, preferred_element_type=jnp.float32
    )
    grad_hidden = (grad_active * gelu_slope(hidden)).astype(jnp.bfloat16)
    grad_b_mlp_in = column_sums(grad_hidden)
    grad_mlp_in_rows = jnp.einsum(
        "rf,rd->fd", grad_hidden, mid_full, preferred_element_type=jnp.float32
    )
    partial_mid = jnp.einsum("rf,df->rd", grad_hidden, w_mlp_in, preferred_element_type=jnp.float32)
    midpoint_gradient = lax.psum_scatter(
        padded(partial_mid), "feat", scatter_dimension=0, tiled=True
    )
    feedforward_gain_gradient = jnp.sum(midpoint_gradient * second_centered_scaled, axis=0)
    grad_s_mlp = jnp.sum(midpoint_gradient, axis=0)
    middle_state_gradient = output_gradient + layer_norm_backward(
        midpoint_gradient, second_centered_scaled, second_inverse_deviation, feedforward_norm_gain
    )
    grad_attn = middle_state_gradient.astype(jnp.bfloat16)
    grad_b_attn_out = column_sums(grad_attn)
    attn_full = lax.all_gather(grad_attn, "feat", axis=0, tiled=True)[:group_rows]
    grad_w_attn_out = jnp.einsum("rh,rd->hd", mixed, attn_full, preferred_element_type=jnp.float32)
    grad_mixed = jnp.einsum(
        "rd,hd->rh", attn_full, w_attn_out, preferred_element_type=jnp.float32
    ).astype(jnp.bfloat16)
    grad_query, grad_key, grad_value = lax.map(
        image_backward,
        (
            by_image(queries, images),
            by_image(key_rows, images),
            by_image(value_rows, images),
            by_image(grad_mixed, images),
            log_totals,
        ),
    )
    grad_query = grad_query.reshape(group_rows, width_local)
    grad_key = grad_key.reshape(group_rows, width_local)
    grad_value = grad_value.reshape(group_rows, width_local)
    grad_b_query = column_sums(grad_query)
    grad_b_value = column_sums(grad_value)
    grad_qkv = jnp.concatenate([grad_query, grad_key, grad_value], axis=1)
    grad_w_qkv = jnp.einsum("rc,rd->cd", grad_qkv, normed_full, preferred_element_type=jnp.float32)
    partial_in = jnp.einsum("rc,cd->rd", grad_qkv, w_qkv, preferred_element_type=jnp.float32)
    normalized_gradient = lax.psum_scatter(
        padded(partial_in).astype(jnp.bfloat16), "feat", scatter_dimension=0, tiled=True
    ).astype(jnp.float32)
    attention_gain_gradient = jnp.sum(normalized_gradient * first_centered_scaled, axis=0)
    grad_s_attn = jnp.sum(normalized_gradient, axis=0)
    layer_input_gradient = middle_state_gradient + layer_norm_backward(
        normalized_gradient, first_centered_scaled, first_inverse_deviation, attention_norm_gain
    )
    local_powers = jnp.stack(
        [
            jnp.sum(row_mask[:, None] * local_input_rows * local_input_rows),
            jnp.sum(row_mask[:, None] * attn * attn),
            jnp.sum(row_mask[:, None] * branch * branch),
            jnp.sum(row_mask[:, None] * output * output),
        ]
    )
    local_count = jnp.sum(row_mask)
    bias_entries = jnp.concatenate([grad_b_query, grad_b_value, grad_b_mlp_in])
    bias_row = jnp.pad(bias_entries, (0, width - bias_entries.shape[0]))[None, :]
    packed = jnp.concatenate(
        [grad_w_qkv, grad_w_attn_out, grad_mlp_in_rows, grad_w_mlp_out, bias_row], axis=0
    )
    packed_rows = packed.shape[0]
    tok_parts = lax.axis_size("tok")
    fill_rows = (tok_parts - packed_rows % tok_parts) % tok_parts
    packed = jnp.pad(packed, ((0, fill_rows), (0, 0)))
    shares = lax.psum_scatter(
        packed.astype(jnp.bfloat16), "tok", scatter_dimension=0, tiled=True
    ).astype(jnp.float32)
    summed = lax.all_gather(shares.astype(jnp.bfloat16), "tok", axis=0, tiled=True).astype(
        shares.dtype
    )[:packed_rows]
    offset = 0
    grad_w_query = summed[offset : offset + width_local]
    offset += width_local
    grad_w_key = summed[offset : offset + width_local]
    offset += width_local
    grad_w_value = summed[offset : offset + width_local]
    offset += width_local
    grad_w_attn_out = summed[offset : offset + width_local]
    offset += width_local
    grad_w_mlp_in = summed[offset : offset + hidden_local].T
    offset += hidden_local
    grad_w_mlp_out = summed[offset : offset + hidden_local]
    offset += hidden_local
    bias_sums = summed[offset]
    grad_b_query = bias_sums[:width_local]
    grad_b_value = bias_sums[width_local : 2 * width_local]
    grad_b_mlp_in = bias_sums[2 * width_local : 2 * width_local + hidden_local]
    (
        grad_b_attn_out,
        grad_b_mlp_out,
        attention_gain_gradient,
        grad_s_attn,
        feedforward_gain_gradient,
        grad_s_mlp,
        powers,
        counted,
    ) = lax.psum(
        (
            grad_b_attn_out,
            grad_b_mlp_out,
            attention_gain_gradient,
            grad_s_attn,
            feedforward_gain_gradient,
            grad_s_mlp,
            local_powers,
            local_count,
        ),
        ("tok", "feat"),
    )
    stream_rms = jnp.sqrt(powers / (jnp.maximum(counted, 1.0) * D))
    return (
        output,
        layer_input_gradient,
        grad_w_query,
        grad_w_key,
        grad_w_value,
        grad_b_query,
        grad_b_value,
        grad_w_attn_out,
        grad_b_attn_out,
        grad_w_mlp_in,
        grad_b_mlp_in,
        grad_w_mlp_out,
        grad_b_mlp_out,
        attention_gain_gradient,
        grad_s_attn,
        feedforward_gain_gradient,
        grad_s_mlp,
        stream_rms,
    )


def solution(mesh):
    in_specs = (
        P(("tok", "feat"), None),
        P("tok"),
        P(("tok", "feat"), None),
        P("feat", None),
        P("feat", None),
        P("feat", None),
        P("feat"),
        P("feat"),
        P("feat", None),
        P(),
        P(None, "feat"),
        P("feat"),
        P("feat", None),
        P(),
        P(),
        P(),
        P(),
        P(),
    )
    out_specs = (
        P(("tok", "feat"), None),
        P(("tok", "feat"), None),
        P("feat", None),
        P("feat", None),
        P("feat", None),
        P("feat"),
        P("feat"),
        P("feat", None),
        P(),
        P(None, "feat"),
        P("feat"),
        P("feat", None),
        P(),
        P(),
        P(),
        P(),
        P(),
        P(),
    )
    return jax.shard_map(
        on_device, mesh=mesh, in_specs=in_specs, out_specs=out_specs, check_vma=False
    )
```

profile of v0, /device:TPU:0, one launch (start us, length us, event | category | flops | bytes accessed | tf_op | source)
XLA Modules:
  0.0 1217.8 jit_solution(6162602981668325185)
XLA Ops:
  16.1 80.6 %all-gather.11.cloned.1.call-done = bf16[8,289,1024]{2,1,0:T(8,128)(2,1)} async-done(((bf16[1,289,1024]{2,1,0:T(8,128)(2,1)}), bf16[8,289,1024]{2,1,0:T(8,128)(2,1)}) %all-gather.11.cloned.1.call-update) | async-done | bytes 4734992 | tf_op jit(solution)/shard_map/all_gather | solution.py:144
  96.7 5.9 reshape.251
  102.6 4.6 fusion.33
  113.5 12.9 %while.26 = (s32[]{:T(128)}, bf16[4,577,128]{2,1,0:T(8,128)(2,1)S(1)}, f32[4,2,577]{2,1,0:T(2,128)S(1)}, bf16[4,577,128]{1,2,0:T(8,128)(2,1)S(1)}, bf16[4,577,12...) while((s32[]{:T(128)}, bf16[4,577,128]{2,1,0:T(8,128)(2,1)S(1)}, ...), condition=%wide.region_5.6_spmd, body=%wide.region_2.0_spmd.sunk | while | flops 176525056 | bytes 10100381 | solution.py:152
  131.4 4.7 pad.25
  136.1 215.9 %fusion = f32[296,1024]{1,0:T(8,128)S(1)} fusion(f32[2312,1024]{1,0:T(8,128)} %pad.25), kind=kCustom, calls=%all-reduce-scatter | all-reduce-scatter fusion | flops 2424833 | bytes 10682880
  357.8 4.4 concatenate.18
  365.0 10.5 all-gather.17.cloned.1.call-start
  375.6 6.2 reshape.255
  381.8 66.8 %all-gather.13.cloned.1.call-done = bf16[8,289,1024]{2,1,0:T(8,128)(2,1)} async-done(((bf16[1,289,1024]{2,1,0:T(8,128)(2,1)}), bf16[8,289,1024]{2,1,0:T(8,128)(2,1)}) %all-gather.13.cloned.1.call-update) | async-done | bytes 4734992 | tf_op jit(solution)/shard_map/all_gather | solution.py:167
  448.6 5.9 reshape.253
  454.5 4.9 convolution_add_fusion
  459.5 4.9 fusion.98
  467.1 4.5 pad.27
  471.6 191.4 %fusion.2 = f32[296,1024]{1,0:T(8,128)} fusion(f32[2312,1024]{1,0:T(8,128)} %pad.27), kind=kCustom, calls=%all-reduce-scatter.2 | all-reduce-scatter fusion | flops 2424833 | bytes 10682880
  665.3 4.8 collective-permute-done.2
  670.1 5.2 concatenate.20
  681.6 83.8 %all-gather.17.cloned.1.call-done = bf16[8,289,1024]{2,1,0:T(8,128)(2,1)} async-done(((bf16[1,289,1024]{2,1,0:T(8,128)(2,1)}), bf16[8,289,1024]{2,1,0:T(8,128)(2,1)}) %all-gather.17.cloned.1.call-update) | async-done | bytes 4734992 | tf_op jit(solution)/shard_map/all_gather | solution.py:203
  765.4 6.0 reshape.257
  771.4 4.6 fusion.35
  779.0 51.9 %while.27 = (s32[]{:T(128)}, bf16[4,577,128]{1,2,0:T(8,128)(2,1)}, bf16[4,577,128]{2,1,0:T(8,128)(2,1)}, bf16[4,577,128]{1,2,0:T(8,128)(2,1)}, bf16[4,577,128]{1...) while((s32[]{:T(128)}, bf16[4,577,128]{1,2,0:T(8,128)(2,1)}, ...), condition=%wide.region_16.17_spmd, body=%wide.region_14.16_spmd.sunk | while | flops 434507520 | bytes 34832936 | solution.py:208
  849.8 5.2 fusion.56
  856.4 5.9 fusion.44
  867.5 32.7 %fusion.4 = bf16[392,1024]{1,0:T(8,128)(2,1)} fusion(bf16[1540,1024]{1,0:T(8,128)(2,1)} %pad.30), kind=kCustom, calls=%all-reduce-scatter.4 | all-reduce-scatter fusion | flops 1605633 | bytes 3957248
  903.5 5.9 concatenate.22
  911.7 5.1 convolution_convert_fusion.1
  925.1 197.6 %fusion.95 = (bf16[296,1024]{1,0:T(8,128)(2,1)}, bf16[296,1024]{1,0:T(8,128)(2,1)}) fusion(bf16[2312,1024]{1,0:T(8,128)(2,1)} %pad.26, bf16[2312,1024]{1,0:T(8,128)(2,1)} %pad.28), kind=kCustom, calls=%all-reduce-scatter.5 | all-reduce-scatter fusion | flops 4849665 | bytes 10682880
  1128.7 5.0 concatenate.19
  1133.7 4.9 concatenate.21
  1145.5 43.0 %all-reduce.16 = (f32[1024]{0:T(1024)}, f32[1024]{0:T(1024)}, f32[1024]{0:T(1024)}, f32[1024]{0:T(1024)}, f32[1024]{0:T(1024)}, /*index=5*/f32[1024]{0:T(1024)}, f32[4]{0:T(128)S(1)}, f32[]{:T(128)}) all-reduce(f32[1024]{0:T(1024)S(1)} %copy-done.24, ...), channel_id=1, replica_groups=mesh['tok'=4,'feat'=8] {'tok','feat'}, use_global_device_ids=true, to_apply=%region_25.26 | all-reduce | flops 6149 | bytes 49192 | tf_op jit(solution)/shard_map/psum | solution.py:284
  1192.7 5.3 reshape.260
  1198.0 4.8 fusion.96
  (291 shorter events, 169.2 us)
Async XLA Ops:
  7.2 452.2 %copy-start = (bf16[512,1024]{1,0:T(8,128)(2,1)S(1)}, bf16[512,1024]{1,0:T(8,128)(2,1)}, u32[]{:S(2)}) copy-start(bf16[512,1024]{1,0:T(8,128)(2,1)} %param.34) | copy-start | bytes 3145732
  7.2 8.7 copy-start.34
  7.2 8.7 copy-start.35
  7.2 8.8 copy-start.13
  7.2 8.8 copy-start.14
  7.3 89.4 %all-gather.11.cloned.1.call-start = ((), (), s32[]{:S(2)}) async-start(), calls=%async_computation | async-start | bytes 5455872 | tf_op jit(solution)/shard_map/all_gather | solution.py:144
  9.4 93.2 %copy-start.18 = (f32[1024]{0:T(1024)}, f32[1024]{0:T(1024)S(1)}, u32[]{:S(2)}) copy-start(f32[1024]{0:T(1024)S(1)} %convert_element_type.188) | copy-start | bytes 12292
  10.1 92.5 %copy-start.20 = (f32[289]{0:T(512)}, f32[289]{0:T(512)S(1)}, u32[]{:S(2)}) copy-start(f32[289]{0:T(512)S(1)} %get-tuple-element.322) | copy-start | bytes 3472
  10.1 92.5 %copy-start.22 = (f32[289]{0:T(512)}, f32[289]{0:T(512)S(1)}, u32[]{:S(2)}) copy-start(f32[289]{0:T(512)S(1)} %get-tuple-element.323) | copy-start | bytes 3472
  12.4 363.3 %all-gather.15.cloned.1.call-start = ((), (), s32[]{:S(2)}) async-start(), calls=%async_computation.2 | async-start | bytes 5455872 | tf_op jit(solution)/shard_map/all_gather | solution.py:180
  15.8 432.8 %all-gather.13.cloned.1.call-start = ((), (), s32[]{:S(2)}) async-start(), calls=%async_computation.1 | async-start | bytes 5455872 | tf_op jit(solution)/shard_map/all_gather | solution.py:167
  16.1 86.6 %copy-start.16 = (bf16[384,1024]{1,0:T(8,128)(2,1)}, bf16[384,1024]{1,0:T(8,128)(2,1)S(1)}, u32[]{:S(2)}) copy-start(bf16[384,1024]{1,0:T(8,128)(2,1)S(1)} %constant_dynamic-update-slice_fusion.4) | copy-start | bytes 2359300
  136.1 217.4 %copy-start.25 = (bf16[1024]{0:T(1024)(128)(2,1)S(1)}, bf16[1024]{0:T(1024)(128)(2,1)}, u32[]{:S(2)}) copy-start(bf16[1024]{0:T(1024)(128)(2,1)} %param.31) | copy-start | bytes 6148
  136.1 217.5 %copy-start.26 = (bf16[1024]{0:T(1024)(128)(2,1)S(1)}, bf16[1024]{0:T(1024)(128)(2,1)}, u32[]{:S(2)}) copy-start(bf16[1024]{0:T(1024)(128)(2,1)} %param.38) | copy-start | bytes 6148
  136.1 217.5 %copy-start.27 = (bf16[1024]{0:T(1024)(128)(2,1)S(1)}, bf16[1024]{0:T(1024)(128)(2,1)}, u32[]{:S(2)}) copy-start(bf16[1024]{0:T(1024)(128)(2,1)} %param.39) | copy-start | bytes 6148
  136.1 217.5 %copy-start.32 = (u32[32]{0:T(128)S(1)}, u32[32]{0:T(128)}, u32[]{:S(2)}) copy-start(u32[32]{0:T(128)} %constant.104) | copy-start | bytes 388
  352.1 10.2 copy-start.2
  352.1 5.7 collective-permute-start
  362.2 13.4 %copy-start.29 = (bf16[512]{0:T(512)(128)(2,1)S(1)}, bf16[512]{0:T(512)(128)(2,1)}, u32[]{:S(2)}) copy-start(bf16[512]{0:T(512)(128)(2,1)} %param.33) | copy-start | bytes 3076
  365.0 400.4 %all-gather.17.cloned.1.call-start = ((), (), s32[]{:S(2)}) async-start(), calls=%async_computation.3 | async-start | bytes 5455872 | tf_op jit(solution)/shard_map/all_gather | solution.py:203
  664.0 6.1 collective-permute-start.2
  681.6 511.2 %all-gather.19.cloned.1.call-start = ((), (), s32[]{:S(2)}) async-start(), calls=%async_computation.4 | async-start | bytes 4014080 | tf_op jit(solution)/shard_map/all_gather | solution.py:255
  681.6 89.8 %copy-start.11 = (bf16[128,1024]{1,0:T(8,128)(2,1)S(1)}, bf16[128,1024]{1,0:T(8,128)(2,1)}, u32[]{:S(2)}) copy-start(bf16[128,1024]{1,0:T(8,128)(2,1)} %param.30) | copy-start | bytes 786436
  845.8 9.2 slice-start.2
  867.4 34.8 %copy-start.28 = (bf16[1024]{0:T(1024)(128)(2,1)S(1)}, bf16[1024]{0:T(1024)(128)(2,1)}, u32[]{:S(2)}) copy-start(bf16[1024]{0:T(1024)(128)(2,1)} %param.35) | copy-start | bytes 6148
  867.5 34.8 %copy-start.31 = (u32[32]{0:T(128)S(1)}, u32[32]{0:T(128)}, u32[]{:S(2)}) copy-start(u32[32]{0:T(128)} %constant.120) | copy-start | bytes 388
  900.9 2.6 collective-permute-start.4
  1122.8 15.8 %copy-start.19 = (f32[1024]{0:T(1024)S(1)}, f32[1024]{0:T(1024)}, u32[]{:S(2)}) copy-start(f32[1024]{0:T(1024)} %copy-done.18) | copy-start | bytes 12292
  1122.8 15.8 %copy-start.21 = (f32[289]{0:T(512)S(1)}, f32[289]{0:T(512)}, u32[]{:S(2)}) copy-start(f32[289]{0:T(512)} %copy-done.20) | copy-start | bytes 3472
  1122.8 15.8 %copy-start.23 = (f32[289]{0:T(512)S(1)}, f32[289]{0:T(512)}, u32[]{:S(2)}) copy-start(f32[289]{0:T(512)} %copy-done.22) | copy-start | bytes 3472
  1123.8 4.9 collective-permute-start.1
  1126.0 7.7 collective-permute-start.3
  (26 other events, 111.4 us)
Sparse Core Ops, SparseCore 0:
  12.5 84.1 all-gather.10
  99.5 147.8 all-gather.14
  365.2 83.3 all-gather.12
  681.7 83.7 all-gather.16
  911.9 29.9 all-gather.18
where the time goes:
time: 1230 us; the launch traced here: 1220 us
  blocking collectives  681 us (55%)
  waiting for transfers between devices  239 us (19%)
  local copies, waits for them, and re-layouts  146 us (12%)
  matrix products  80 us (7%)
  other arithmetic  35.5 us (3%)
  starting transfers between devices  18.7 us (2%)
  between operations  16.8 us (1%)
    unnamed x4, blocking collectives  638 us
    all_gather x1, waiting for transfers between devices, on_device(): lax.all_gather(grad_attn, 'feat', axis=0, tiled=True)[:group_rows]  83.8 us
    all_gather x1, waiting for transfers between devices, on_device(): lax.all_gather(normalized_first, 'feat', axis=0, tiled=True)[:group_rows]  80.6 us
    all_gather x1, waiting for transfers between devices, on_device(): lax.all_gather(normalized_middle, 'feat', axis=0, tiled=True)[:group_rows]  66.8 us
    unnamed x110, local copies, waits for them, and re-layouts  65.4 us
    psum x1, blocking collectives, on_device(): lax.psum((grad_b_attn_out, grad_b_mlp_out, attention_gain_gradient, grad_...  43 us
  transfers between devices with their start and end apart: 10, of which 5 were waited for; matrix products, arithmetic and copies ran while one was open for 42% of the time, Pallas kernels for 0%

commit v1 on v0

--- a/solution.py
+++ b/solution.py
@@ -1,6 +1,10 @@
+import functools
+
 import jax
 import jax.numpy as jnp
 from jax import lax
+from jax.experimental import pallas as pl
+from jax.experimental.pallas import tpu as pltpu
 from jax.sharding import PartitionSpec as P
 
 D = 1024
@@ -99,7 +103,7 @@
     return values.reshape(images, values.shape[0] // images, values.shape[1])
 
 
-def on_device(
+def on_device_general(
     inputs,
     valid,
     cotangent,
@@ -317,6 +321,484 @@
     )
 
 
+BF16 = jnp.bfloat16
+F32 = jnp.float32
+AXES = ("tok", "feat")
+SLOTS = (0, 1, 3, 2)
+PAIRS = ((0, 1), (3, 2))
+VMEM_BYTES = 48 * 1024 * 1024
+
+
+def route(move):
+    found = []
+    for tok in range(4):
+        for feat in range(8):
+            target = move(tok // 2, tok % 2, feat // 2, feat % 2)
+            if target is not None:
+                x, c, z, y = target
+                found.append((tok * 8 + feat, (2 * x + c) * 8 + 2 * z + y))
+    return found
+
+
+SWAP_X = route(lambda x, c, z, y: (1 - x, c, z, y))
+SWAP_C = route(lambda x, c, z, y: (x, 1 - c, z, y))
+SWAP_Y = route(lambda x, c, z, y: (x, c, z, 1 - y))
+SHIFT_Z = [route(lambda x, c, z, y, s=s: (x, c, (z + s) % 4, y)) for s in range(4)]
+FLIP_Z = [route(lambda x, c, z, y, s=s: (x, c, z ^ s, y)) for s in range(4)]
+NEXT = [(t * 8 + f, t * 8 + f + 1) for t in range(4) for f in range(7)]
+PREVIOUS = [(t * 8 + f + 1, t * 8 + f) for t in range(4) for f in range(7)]
+
+
+def send(values, pairs):
+    return lax.ppermute(values, AXES, pairs)
+
+
+def nt(left, right):
+    return lax.dot_general(left, right, (((1,), (1,)), ((), ())), preferred_element_type=F32)
+
+
+def nn(left, right):
+    return lax.dot_general(left, right, (((1,), (0,)), ((), ())), preferred_element_type=F32)
+
+
+def tn(left, right):
+    return lax.dot_general(left, right, (((0,), (0,)), ((), ())), preferred_element_type=F32)
+
+
+def forward_kernel(half, limits_ref, qkv_ref, mixed_ref, probs_ref):
+    rows = 2 * half
+    key_index = lax.broadcasted_iota(jnp.int32, (rows, 1), 0)
+    first, second = limits_ref[0], limits_ref[1]
+    real = (key_index < first) | ((key_index >= half) & (key_index < half + second))
+    penalty = jnp.where(real, 0.0, -1e30)
+    outs = []
+    for h in range(2):
+        q = qkv_ref[:, h * DH : (h + 1) * DH] * jnp.asarray(DH ** (-0.5), BF16)
+        k = qkv_ref[:, 2 * DH + h * DH : 2 * DH + (h + 1) * DH]
+        v = qkv_ref[:, 4 * DH + h * DH : 4 * DH + (h + 1) * DH]
+        scores = nt(k, q) + penalty
+        top = jnp.max(scores, axis=0, keepdims=True)
+        weights = jnp.exp(scores - top)
+        total = jnp.sum(weights, axis=0, keepdims=True)
+        probs = (weights * (1.0 / total)).astype(BF16)
+        probs_ref[0, h] = probs
+        outs.append(tn(v, probs))
+    mixed_ref[...] = jnp.concatenate(outs, axis=0).T.astype(BF16)
+
+
+def backward_kernel(qkv_ref, probs_ref, grad_ref, out_ref, sums_ref):
+    scale = jnp.asarray(DH ** (-0.5), BF16)
+    dq, dk, dv = [], [], []
+    for h in range(2):
+        q = qkv_ref[:, h * DH : (h + 1) * DH] * scale
+        k = qkv_ref[:, 2 * DH + h * DH : 2 * DH + (h + 1) * DH] * scale
+        v = qkv_ref[:, 4 * DH + h * DH : 4 * DH + (h + 1) * DH]
+        g = grad_ref[:, h * DH : (h + 1) * DH]
+        probs = probs_ref[0, h]
+        grad_probs = nt(v, g)
+        wide = probs.astype(F32)
+        inner = jnp.sum(wide * grad_probs, axis=0, keepdims=True)
+        grad_scores = (wide * (grad_probs - inner)).astype(BF16)
+        dv.append(nn(probs, g))
+        dk.append(nn(grad_scores, q))
+        dq.append(tn(k, grad_scores))
+    query = jnp.concatenate(dq, axis=0).T.astype(BF16)
+    value = jnp.concatenate(dv, axis=1).astype(BF16)
+    out_ref[:, : 2 * DH] = query
+    out_ref[:, 2 * DH : 4 * DH] = jnp.concatenate(dk, axis=1).astype(BF16)
+    out_ref[:, 4 * DH :] = value
+    query_sum = jnp.sum(query.astype(F32), axis=0, keepdims=True)
+    value_sum = jnp.sum(value.astype(F32), axis=0, keepdims=True)
+    sums_ref[0] = jnp.concatenate([query_sum, value_sum, jnp.zeros((6, 2 * DH), F32)], axis=0)
+
+
+def attention_forward(limits, qkv, half):
+    rows = 2 * half
+    count = qkv.shape[0] // rows
+    return pl.pallas_call(
+        functools.partial(forward_kernel, half),
+        grid=(count,),
+        in_specs=[
+            pl.BlockSpec(memory_space=pltpu.SMEM),
+            pl.BlockSpec((rows, 6 * DH), lambda i: (i, 0)),
+        ],
+        out_specs=[
+            pl.BlockSpec((rows, 2 * DH), lambda i: (i, 0)),
+            pl.BlockSpec((1, 2, rows, rows), lambda i: (i, 0, 0, 0)),
+        ],
+        out_shape=[
+            jax.ShapeDtypeStruct((count * rows, 2 * DH), BF16),
+            jax.ShapeDtypeStruct((count, 2, rows, rows), BF16),
+        ],
+        compiler_params=pltpu.CompilerParams(vmem_limit_bytes=VMEM_BYTES),
+        cost_estimate=pl.CostEstimate(
+            flops=count * 8 * rows * rows * DH,
+            bytes_accessed=count * rows * (rows * 4 + 16 * DH),
+            transcendentals=count * 2 * rows * rows,
+        ),
+    )(limits, qkv)
+
+
+def attention_backward(qkv, probs, grad, half):
+    rows = 2 * half
+    count = qkv.shape[0] // rows
+    return pl.pallas_call(
+        backward_kernel,
+        grid=(count,),
+        in_specs=[
+            pl.BlockSpec((rows, 6 * DH), lambda i: (i, 0)),
+            pl.BlockSpec((1, 2, rows, rows), lambda i: (i, 0, 0, 0)),
+            pl.BlockSpec((rows, 2 * DH), lambda i: (i, 0)),
+        ],
+        out_specs=[
+            pl.BlockSpec((rows, 6 * DH), lambda i: (i, 0)),
+            pl.BlockSpec((1, 8, 2 * DH), lambda i: (i, 0, 0)),
+        ],
+        out_shape=[
+            jax.ShapeDtypeStruct((count * rows, 6 * DH), BF16),
+            jax.ShapeDtypeStruct((count, 8, 2 * DH), F32),
+        ],
+        compiler_params=pltpu.CompilerParams(vmem_limit_bytes=VMEM_BYTES),
+        cost_estimate=pl.CostEstimate(
+            flops=count * 16 * rows * rows * DH,
+            bytes_accessed=count * rows * (rows * 4 + 28 * DH),
+            transcendentals=0,
+        ),
+    )(qkv, probs, grad)
+
+
+def gather_rows(values):
+    across = send(values, SWAP_Y)
+    return jnp.concatenate([values, across, send(values, SWAP_C), send(across, SWAP_C)], axis=0)
+
+
+def scatter_rows(product, half):
+    other = product(2 * half, 4 * half).astype(BF16)
+    from_core = send(other, SWAP_C)
+    far = (product(half, 2 * half) + from_core[half:].astype(F32)).astype(BF16)
+    from_y = send(far, SWAP_Y)
+    near = product(0, half) + from_core[:half].astype(F32)
+    return near + from_y.astype(F32)
+
+
+def in_order(flag, own, other, axis):
+    first = jnp.where(flag == 0, own, other)
+    second = jnp.where(flag == 0, other, own)
+    return jnp.stack([first, second], axis=axis)
+
+
+def on_device(
+    inputs,
+    valid,
+    cotangent,
+    w_query,
+    w_key,
+    w_value,
+    b_query,
+    b_value,
+    w_attn_out,
+    b_attn_out,
+    w_mlp_in,
+    b_mlp_in,
+    w_mlp_out,
+    b_mlp_out,
+    attention_norm_gain,
+    attention_norm_shift,
+    feedforward_norm_gain,
+    feedforward_norm_shift,
+):
+    rows, width = inputs.shape
+    images = valid.shape[0]
+    heads_local = w_query.shape[0] // DH
+    hidden_local = w_mlp_out.shape[0]
+    shape = (lax.axis_size("tok"), lax.axis_size("feat"), images, heads_local)
+    if shape != (4, 8, 4, 2) or 2 * rows != SEQ + 1 or hidden_local % 512 or width % 128:
+        return on_device_general(
+            inputs,
+            valid,
+            cotangent,
+            w_query,
+            w_key,
+            w_value,
+            b_query,
+            b_value,
+            w_attn_out,
+            b_attn_out,
+            w_mlp_in,
+            b_mlp_in,
+            w_mlp_out,
+            b_mlp_out,
+            attention_norm_gain,
+            attention_norm_shift,
+            feedforward_norm_gain,
+            feedforward_norm_shift,
+        )
+    tok, feat = lax.axis_index("tok"), lax.axis_index("feat")
+    x, c, z, y = tok // 2, tok % 2, feat // 2, feat % 2
+    half = (rows + 15) // 16 * 16
+    quarter = hidden_local // 4
+    part = DH // 2
+
+    def cut(values, start, size):
+        return lax.dynamic_slice_in_dim(values, start, size, 0)
+
+    def attention_piece(side):
+        at = c * DH + side * part
+        bias = jnp.concatenate(
+            [
+                cut(b_query, at, part),
+                cut(b_value, at, part),
+                cut(b_mlp_in, (2 * c + side) * quarter, quarter),
+            ]
+        )
+        bias = jnp.pad(bias[None, :], ((0, 7), (0, width - bias.shape[0])))
+        return jnp.concatenate(
+            [cut(w, at, part) for w in (w_query, w_key, w_value, w_attn_out)] + [bias], axis=0
+        )
+
+    attn_own = {0: attention_piece(x)}
+    attn_other = {0: attention_piece(1 - x)}
+    for s in (1, 3, 2):
+        attn_own[s] = send(attn_own[0], SHIFT_Z[s])
+
+    edge = send(jnp.concatenate([inputs[rows - 4 :], cotangent[rows - 4 :]], axis=0), NEXT)
+    count = rows - y
+    present = lax.broadcasted_iota(jnp.int32, (half, 1), 0) < count
+
+    def aligned(values, before):
+        ext = jnp.concatenate([before, values, jnp.zeros((half - rows, width), BF16)], axis=0)
+        return jnp.where(present, lax.dynamic_slice_in_dim(ext, 4 - z, half, 0), 0)
+
+    stream = aligned(inputs, edge[:4]).astype(F32)
+    first_hat, first_inverse = apply_layer_norm(stream)
+    normed = (
+        first_hat * attention_norm_gain.astype(F32) + attention_norm_shift.astype(F32)
+    ).astype(BF16)
+    normed_all = gather_rows(normed)
+    flag = lax.dynamic_index_in_dim(valid, z, 0, keepdims=False).astype(F32)
+    grad_branch = (aligned(cotangent, edge[4:]).astype(F32) * flag).astype(BF16)
+    output_gradient = grad_branch.astype(F32)
+
+    both = send(jnp.stack([attn_own[1], attn_own[3]]), SWAP_X)
+    attn_other[1], attn_other[3] = both[0], both[1]
+    attn_other[2] = send(attn_own[2], SWAP_X)
+
+    hidden_half = lax.dynamic_slice_in_dim(w_mlp_in, 2 * c * quarter, 2 * quarter, 1).T
+    out_half = cut(w_mlp_out, 2 * c * quarter, 2 * quarter)
+
+    def mlp_piece(side):
+        return jnp.concatenate(
+            [cut(hidden_half, side * quarter, quarter), cut(out_half, side * quarter, quarter)],
+            axis=0,
+        )
+
+    mlp_own = {0: mlp_piece(x)}
+    mlp_other = {0: mlp_piece(1 - x)}
+    for s in (1, 3, 2):
+        mlp_own[s] = send(mlp_own[0], SHIFT_Z[s])
+    both = send(jnp.stack([mlp_own[1], mlp_own[3]]), SWAP_X)
+    mlp_other[1], mlp_other[3] = both[0], both[1]
+    mlp_other[2] = send(mlp_own[2], SWAP_X)
+
+    def attention_rows(matrix, slots):
+        at = slice(matrix * part, (matrix + 1) * part)
+        return [side[s][at] for s in slots for side in (attn_own, attn_other)]
+
+    def bias_of(first, size, slots, sides=(0, 1)):
+        taken = []
+        for s in slots:
+            for side in (attn_own, attn_other):
+                taken.append(side[s][4 * part, first : first + size])
+        return taken
+
+    limits = jnp.stack([rows - y, rows - 1 + y]).astype(jnp.int32)
+    w_pairs, qkv_pairs, mixed_pairs, prob_pairs = [], [], [], []
+    for slots in PAIRS:
+        w_pair = jnp.concatenate([r for m in range(3) for r in attention_rows(m, slots)], axis=0)
+        bias = jnp.concatenate(
+            bias_of(0, part, slots)
+            + [jnp.zeros((2 * DH,), BF16)]
+            + bias_of(part, part, slots)
+        )
+        qkv = (nt(normed_all, w_pair) + bias.astype(F32)).astype(BF16)
+        mixed, probs = attention_forward(limits, qkv, half)
+        w_pairs.append(w_pair)
+        qkv_pairs.append(qkv)
+        mixed_pairs.append(mixed)
+        prob_pairs.append(probs)
+    w_out = jnp.concatenate(attention_rows(3, SLOTS), axis=0)
+    mixed = jnp.concatenate(mixed_pairs, axis=1)
+    attn = scatter_rows(lambda lo, hi: nn(mixed[lo:hi], w_out), half) + b_attn_out.astype(F32)
+
+    middle = stream + attn
+    second_hat, second_inverse = apply_layer_norm(middle)
+    normed_middle = (
+        second_hat * feedforward_norm_gain.astype(F32) + feedforward_norm_shift.astype(F32)
+    ).astype(BF16)
+    middle_all = gather_rows(normed_middle)
+    branch_all = gather_rows(grad_branch)
+
+    w_in = jnp.concatenate([side[s][:quarter] for side in (mlp_own, mlp_other) for s in SLOTS])
+    w_mid = jnp.concatenate([side[s][quarter:] for side in (mlp_own, mlp_other) for s in SLOTS])
+    bias_in = jnp.concatenate(
+        [
+            side[s][4 * part, 2 * part : 2 * part + quarter]
+            for side in (attn_own, attn_other)
+            for s in SLOTS
+        ]
+    )
+    hidden = nt(middle_all, w_in) + bias_in.astype(F32)
+    active = (hidden * jax.nn.sigmoid(SLOPE * hidden)).astype(BF16)
+    grad_active = nt(branch_all, w_mid)
+    grad_hidden = (grad_active * gelu_slope(hidden)).astype(BF16)
+    midpoint_gradient = scatter_rows(lambda lo, hi: nn(grad_hidden[lo:hi], w_in), half)
+    grad_b_mlp_in = column_sums(grad_hidden)
+
+    halves = hidden_local
+
+    def exchange(left, right):
+        other = tn(left[:, halves:], right).astype(BF16)
+        received = send(other, SWAP_X)
+        return (tn(left[:, :halves], right) + received.astype(F32)).astype(BF16)
+
+    grad_out_half = exchange(active, branch_all)
+    grad_in_half = exchange(grad_hidden, middle_all)
+
+    def to_owner(pieces):
+        total = pieces[0].astype(F32)
+        for s in (1, 3, 2):
+            total = total + send(pieces[s], SHIFT_Z[4 - s]).astype(F32)
+        return total.astype(BF16)
+
+    mlp_sum = to_owner(
+        {
+            s: jnp.concatenate(
+                [g[i * quarter : (i + 1) * quarter] for g in (grad_in_half, grad_out_half)], axis=0
+            )
+            for i, s in enumerate(SLOTS)
+        }
+    ).reshape(2, quarter, width)
+    mlp_sum = in_order(x, mlp_sum, send(mlp_sum, SWAP_X), 1)
+    mlp_sum = in_order(c, mlp_sum, send(mlp_sum, SWAP_C), 1)
+    mlp_sum = mlp_sum.reshape(2, hidden_local, width).astype(F32)
+
+    branch = scatter_rows(lambda lo, hi: nn(active[lo:hi], w_mid), half) + b_mlp_out.astype(F32)
+    output = middle + branch
+
+    feedforward_gain_gradient = jnp.sum(midpoint_gradient * second_hat, axis=0)
+    grad_s_mlp = jnp.sum(midpoint_gradient, axis=0)
+    middle_gradient = output_gradient + layer_norm_backward(
+        midpoint_gradient, second_hat, second_inverse, feedforward_norm_gain
+    )
+    grad_attn = middle_gradient.astype(BF16)
+    attn_all = gather_rows(grad_attn)
+    grad_mixed = nt(attn_all, w_out).astype(BF16)
+    grad_w_out = tn(mixed, attn_all).reshape(2, 2, 2, part, width)
+
+    attn_pieces, sum_pairs, grad_pairs = {}, [None, None], [None, None]
+    for p in (1, 0):
+        grad_qkv, sums = attention_backward(
+            qkv_pairs[p], prob_pairs[p], grad_mixed[:, p * 2 * DH : (p + 1) * 2 * DH], half
+        )
+        grad_pairs[p] = grad_qkv
+        sum_pairs[p] = jnp.sum(sums, axis=0)
+        grad_w = tn(grad_qkv, normed_all).reshape(3, 2, 2, part, width)
+        grad_w = jnp.concatenate([grad_w, grad_w_out[p][None]], axis=0)
+        received = send(grad_w[:, :, 1].astype(BF16), SWAP_X)
+        summed = (grad_w[:, :, 0] + received.astype(F32)).astype(BF16)
+        for i, s in enumerate(PAIRS[p]):
+            attn_pieces[s] = summed[:, i]
+    grad_all = jnp.concatenate(grad_pairs, axis=1)
+    w_all = jnp.concatenate(w_pairs, axis=0)
+    normed_gradient = scatter_rows(lambda lo, hi: nn(grad_all[lo:hi], w_all), half)
+    attention_gain_gradient = jnp.sum(normed_gradient * first_hat, axis=0)
+    grad_s_attn = jnp.sum(normed_gradient, axis=0)
+    layer_input_gradient = middle_gradient + layer_norm_backward(
+        normed_gradient, first_hat, first_inverse, attention_norm_gain
+    )
+    attn_sum = to_owner(attn_pieces)
+    attn_sum = in_order(x, attn_sum, send(attn_sum, SWAP_X), 1)
+    attn_sum = in_order(c, attn_sum, send(attn_sum, SWAP_C), 1)
+    attn_sum = attn_sum.reshape(4, 2 * DH, width).astype(F32)
+
+    heads = send(jnp.concatenate([output[:4], layer_input_gradient[:4]], axis=0), PREVIOUS)
+
+    def own_rows(values, after):
+        ext = lax.dynamic_update_slice_in_dim(values, after, count, 0)
+        return lax.dynamic_slice_in_dim(ext, z, rows, 0)
+
+    output_rows = own_rows(output, heads[:4])
+    gradient_rows = own_rows(layer_input_gradient, heads[4:])
+
+    mask = jnp.where(present, flag, 0.0)
+    powers = [jnp.sum(mask * v * v) for v in (stream, attn, branch, output)]
+    powers = jnp.stack(powers + [flag * count.astype(F32)])
+    slot_of = jnp.asarray(SLOTS, jnp.int32)
+    four = jnp.arange(4, dtype=jnp.int32)
+    two = jnp.arange(2, dtype=jnp.int32)
+    by_z = (four[:, None] == (z - slot_of[None, :]) % 4).astype(F32)
+    by_x = (two[:, None] == (two[None, :] + x) % 2).astype(F32)
+    place = ((two[:, None] == y) & (two[None, :] == c)).astype(F32)
+
+    def spread(values):
+        found = jnp.sum(
+            by_z[:, None, :, None, None] * by_x[None, :, None, :, None] * values[None, None],
+            axis=(2, 3),
+        )
+        found = place[None, :, :, None, None] * found[:, None, None]
+        return found.reshape(-1, width)
+
+    def slot_sums(row):
+        return jnp.concatenate([s[row].reshape(2, 2, part) for s in sum_pairs], axis=0)
+
+    hidden_sums = grad_b_mlp_in.reshape(2, 4, quarter).transpose(1, 0, 2)
+    small = jnp.concatenate(
+        [
+            jnp.stack(
+                [
+                    column_sums(grad_attn),
+                    column_sums(grad_branch),
+                    attention_gain_gradient,
+                    grad_s_attn,
+                    feedforward_gain_gradient,
+                    grad_s_mlp,
+                    jnp.pad(powers, (0, width - 5)),
+                ]
+            ),
+            spread(slot_sums(0)),
+            spread(slot_sums(1)),
+            spread(hidden_sums),
+        ],
+        axis=0,
+    )
+    for pairs in (SWAP_C, SWAP_X, SWAP_Y, FLIP_Z[1], FLIP_Z[2]):
+        small = small + send(small, pairs)
+    stream_rms = jnp.sqrt(small[6, :4] / (jnp.maximum(small[6, 4], 1.0) * D))
+    grad_b_query = cut(small[7], feat * heads_local * DH, heads_local * DH)
+    grad_b_value = cut(small[8], feat * heads_local * DH, heads_local * DH)
+    grad_b_mlp_in = cut(small[9:].reshape(-1), feat * hidden_local, hidden_local)
+    return (
+        output_rows,
+        gradient_rows,
+        attn_sum[0],
+        attn_sum[1],
+        attn_sum[2],
+        grad_b_query,
+        grad_b_value,
+        attn_sum[3],
+        small[0],
+        mlp_sum[0].T,
+        grad_b_mlp_in,
+        mlp_sum[1],
+        small[1],
+        small[2],
+        small[3],
+        small[4],
+        small[5],
+        stream_rms,
+    )
+
+
 def solution(mesh):
     in_specs = (
         P(("tok", "feat"), None),

time: 1230 us -> 418 us (0.34)
  blocking collectives: 681 us -> 0 us
  waiting for transfers between devices: 239 us -> 144 us
  local copies, waits for them, and re-layouts: 146 us -> 78.2 us
  starting transfers between devices: 18.7 us -> 70.6 us
  Pallas kernels: 0 us -> 17.5 us
  between operations: 16.8 us -> 3.63 us
    unnamed x4 -> x0, blocking collectives: 638 us -> none
    all_gather x5 -> x0, waiting for transfers between devices: 231 us -> none  [the longest x1 83.8 us: on_device(): lax.all_gather(grad_attn, 'feat', axis=0, tiled=True)[:group_rows]]
    ppermute x0 -> x51, waiting for transfers between devices: none -> 144 us  [send(): return lax.ppermute(values, AXES, pairs)]
    ppermute x0 -> x51, starting transfers between devices: none -> 70.6 us  [send(): return lax.ppermute(values, AXES, pairs)]
    psum x1 -> x0, blocking collectives: 43 us -> none  [on_device(): lax.psum((grad_b_attn_out, grad_b_mlp_out, attention_gain_gradient, grad_...]
    unnamed x110 -> x162, local copies, waits for them, and re-layouts: 65.4 us -> 41.8 us
    pallas_call x0 -> x4, Pallas kernels: none -> 17.5 us  [the longest x2 8.83 us: attention_forward(): pl.pallas_call(functools.partial(forward_kernel, half), grid=(count,), in...]
    pad x5 -> x1, local copies, waits for them, and re-layouts: 16.6 us -> 0.01 us  [on_device(): jnp.pad(powers, (0, width - 5))]
  transfers between devices with their start and end apart: 10 -> 51, of which waited for: 5 -> 17; matrix products, arithmetic and copies ran while one was open for 42% -> 36% of each run, Pallas kernels for 0% -> 4%
where the time goes in v1:
time: 418 us; the launch traced here: 410 us
  waiting for transfers between devices  144 us (34%)
  local copies, waits for them, and re-layouts  78.2 us (19%)
  starting transfers between devices  70.6 us (17%)
  matrix products  69 us (17%)
  other arithmetic  27.1 us (6%)
  Pallas kernels  17.5 us (4%)
    ppermute x51, waiting for transfers between devices, send(): return lax.ppermute(values, AXES, pairs)  144 us
    ppermute x51, starting transfers between devices, send(): return lax.ppermute(values, AXES, pairs)  70.6 us
    unnamed x162, local copies, waits for them, and re-layouts  41.8 us
    dot_general x12, matrix products, nn(): lax.dot_general(left, right, (((1,), (0,)), ((), ())), preferred_element_...  25.6 us
    dot_general x5, matrix products, nt(): lax.dot_general(left, right, (((1,), (1,)), ((), ())), preferred_element_...  22.1 us
    dot_general x7, matrix products, tn(): lax.dot_general(left, right, (((0,), (0,)), ((), ())), preferred_element_...  21.3 us
    pallas_call x2, Pallas kernels, attention_forward(): pl.pallas_call(functools.partial(forward_kernel, half), grid=(count,), in...  8.83 us
    pallas_call x2, Pallas kernels, attention_backward(): pl.pallas_call(backward_kernel, grid=(count,), in_specs=[pl.BlockSpec((ro...  8.63 us
  transfers between devices with their start and end apart: 51, of which 17 were waited for; matrix products, arithmetic and copies ran while one was open for 36% of the time, Pallas kernels for 4%

profile of v1, /device:TPU:0, one launch (start us, length us, event | category | flops | bytes accessed | tf_op | source)
XLA Modules:
  0.0 410.4 jit_solution(645139450210108969)
XLA Ops:
  10.5 5.0 %collective-permute-start.5 = (bf16[136,1024]{1,0:T(8,128)(2,1)}, bf16[136,1024]{1,0:T(8,128)(2,1)S(1)}, u32[]{:S(2)}, u32[]{:S(2)}) collective-permute-start(bf16[136,1024]{1,0:T(8,128)(2,1)} %constant_dynamic-update-slice_fusion), channel_id=1, source_target_pairs={{0,6},{1,7},{2,0},{3,1},{4,2},{5,3},{6,4},{7,5},{8,14},{9,15},{10,... | collective-permute-start | bytes 835592 | tf_op jit(solution)/shard_map/ppermute | solution.py:353
  18.2 3.4 collective-permute-start
  28.5 3.4 collective-permute-start.14
  41.3 3.3 collective-permute-start.1
  46.3 5.7 %collective-permute-done.7 = bf16[136,1024]{1,0:T(8,128)(2,1)} collective-permute-done((bf16[136,1024]{1,0:T(8,128)(2,1)}, bf16[136,1024]{1,0:T(8,128)(2,1)}, u32[]{:S(2)}, u32[]{:S(2)}) %collective-permute-start.7) | collective-permute-done | bytes 278560 | tf_op jit(solution)/shard_map/ppermute | solution.py:353
  55.0 8.0 %collective-permute-done.8 = bf16[136,1024]{1,0:T(8,128)(2,1)S(1)} collective-permute-done((bf16[136,1024]{1,0:T(8,128)(2,1)}, bf16[136,1024]{1,0:T(8,128)(2,1)S(1)}, u32[]{:S(2)}, u32[]{:S(2)}) %collective-permute-start.8) | collective-permute-done | bytes 278560 | tf_op jit(solution)/shard_map/ppermute | solution.py:353
  82.5 4.1 %fusion.qkv_ref = bf16[1216,384]{1,0:T(8,128)(2,1)S(1)} fusion(bf16[384,1024]{1,0:T(8,128)(2,1)} %get-tuple-element.101, f32[384]{0:T(512)S(1)} %convert_element_type.265, bf16[304,1024]{1,0:T(8,128)(2,1)} %collective-permute-done.3, bf16[304,1024]{1,0:T(8,128)(2,1)} %collective-permute-done.2, bf16[304,1024]{1,0:T(8,128)(2,1)} %collective-permute-done.1, ...), kind=kOutput, calls=%fused_computation.12 | convolution fusion | flops 967196672 | bytes 4212224 | tf_op jit(solution)/shard_map/dot_general | solution.py:357
  86.7 4.5 %shard_map.322 = (bf16[1216,128]{1,0:T(8,128)(2,1)S(1)}, bf16[2,2,608,608]{3,2,1,0:T(8,128)(2,1)S(1)}) custom-call(s32[2]{0:T(128)S(1)} %pad_add_fusion.limits_ref, bf16[1216,384]{1,0:T(8,128)(2,1)S(1)} %fusion.qkv_ref), custom_call_target="tpu_custom_call" | custom-call | flops 378535936 | bytes 4202496 | tf_op jit(solution)/shard_map/pallas_call | solution.py:418
  91.3 4.2 %fusion.1.qkv_ref = bf16[1216,384]{1,0:T(8,128)(2,1)S(1)} fusion(bf16[384,1024]{1,0:T(8,128)(2,1)S(1)} %copy-done.44, f32[384]{0:T(512)S(1)} %convert_element_type.267, bf16[304,1024]{1,0:T(8,128)(2,1)} %collective-permute-done.3, bf16[304,1024]{1,0:T(8,128)(2,1)} %collective-permute-done.2, bf16[304,1024]{1,0:T(8,128)(2,1)} %collective-permute-done.1, ...), kind=kOutput, calls=%fused_computation.13 | convolution fusion | flops 967196672 | bytes 4212224 | tf_op jit(solution)/shard_map/dot_general | solution.py:357
  95.5 4.3 %shard_map.323 = (bf16[1216,128]{1,0:T(8,128)(2,1)S(1)}, bf16[2,2,608,608]{3,2,1,0:T(8,128)(2,1)S(1)}) custom-call(s32[2]{0:T(128)S(1)} %pad_add_fusion.limits_ref, bf16[1216,384]{1,0:T(8,128)(2,1)S(1)} %fusion.1.qkv_ref), custom_call_target="tpu_custom_call" | custom-call | flops 378535936 | bytes 4202496 | tf_op jit(solution)/shard_map/pallas_call | solution.py:418
  119.5 12.0 %collective-permute-done.10 = bf16[304,1024]{1,0:T(8,128)(2,1)S(1)} collective-permute-done((bf16[304,1024]{1,0:T(8,128)(2,1)S(1)}, bf16[304,1024]{1,0:T(8,128)(2,1)S(1)}, u32[]{:S(2)}, u32[]{:S(2)}) %collective-permute-start.10) | collective-permute-done | bytes 622624 | tf_op jit(solution)/shard_map/ppermute | solution.py:353
  141.9 10.6 %collective-permute-done.11 = bf16[304,1024]{1,0:T(8,128)(2,1)} collective-permute-done((bf16[304,1024]{1,0:T(8,128)(2,1)}, bf16[304,1024]{1,0:T(8,128)(2,1)}, u32[]{:S(2)}, u32[]{:S(2)}) %collective-permute-start.11) | collective-permute-done | bytes 622624 | tf_op jit(solution)/shard_map/ppermute | solution.py:353
  158.1 5.5 %multiply_convert_fusion.1 = (bf16[1216,1024]{1,0:T(8,128)(2,1)S(1)}, f32[1216,1024]{1,0:T(8,128)S(1)}) fusion(f32[1024]{0:T(1024)S(1)} %convert_element_type.278, bf16[1024,1024]{1,0:T(8,128)(2,1)} %get-tuple-element.114, bf16[304,1024]{1,0:T(8,128)(2,1)S(1)} %collective-permute-done.13, bf16[304,1024]{1,0:T(8,128)(2,1)S(1)} %collective-permute-done.12, ...), kind=kOutput, calls=%fused_computation.2 | convolution fusion | flops 2568814592 | bytes 12062720 | tf_op jit(solution)/shard_map/dot_general | solution.py:357
  163.6 4.1 %convolution_convert_fusion.5 = bf16[512,1024]{1,0:T(8,128)(2,1)S(1)} fusion(bf16[1216,1024]{1,0:T(8,128)(2,1)S(1)} %get-tuple-element.195, bf16[304,1024]{1,0:T(8,128)(2,1)} %collective-permute-done.23, bf16[304,1024]{1,0:T(8,128)(2,1)} %collective-permute-done.22, bf16[304,1024]{1,0:T(8,128)(2,1)} %collective-permute-done.21, ...), kind=kOutput, calls=%fused_computation.34 | convolution fusion | flops 1285554176 | bytes 4784128 | tf_op jit(solution)/shard_map/dot_general | solution.py:365
  169.2 6.1 %convert_reduce_fusion = (f32[1024]{0:T(1024)S(1)}, bf16[1216,1024]{1,0:T(8,128)(2,1)S(1)}) fusion(f32[1216,1024]{1,0:T(8,128)S(1)} %get-tuple-element.196, f32[1024]{0:T(1024)S(1)} %convert_element_type.278, bf16[1024,1024]{1,0:T(8,128)(2,1)S(1)} %copy-done.40, bf16[304,1024]{1,0:T(8,128)(2,1)} %collective-permute-done.23, ...), kind=kOutput, calls=%fused_computation | convolution fusion | flops 2576284672 | bytes 12066816 | tf_op jit(solution)/shard_map/dot_general | solution.py:357
  183.1 10.7 %collective-permute-done.45 = bf16[512,1024]{1,0:T(8,128)(2,1)S(1)} collective-permute-done((bf16[512,1024]{1,0:T(8,128)(2,1)S(1)}, bf16[512,1024]{1,0:T(8,128)(2,1)S(1)}, u32[]{:S(2)}, u32[]{:S(2)}) %collective-permute-start.45) | collective-permute-done | bytes 1048608 | tf_op jit(solution)/shard_map/ppermute | solution.py:353
  193.7 3.7 add_convert_fusion
  197.5 18.3 %collective-permute-done.44 = bf16[512,1024]{1,0:T(8,128)(2,1)S(1)} collective-permute-done((bf16[512,1024]{1,0:T(8,128)(2,1)S(1)}, bf16[512,1024]{1,0:T(8,128)(2,1)S(1)}, u32[]{:S(2)}, u32[]{:S(2)}) %collective-permute-start.44) | collective-permute-done | bytes 1048608 | tf_op jit(solution)/shard_map/ppermute | solution.py:353
  228.7 6.6 %collective-permute-done.25 = bf16[304,1024]{1,0:T(8,128)(2,1)S(1)} collective-permute-done((bf16[304,1024]{1,0:T(8,128)(2,1)S(1)}, bf16[304,1024]{1,0:T(8,128)(2,1)S(1)}, u32[]{:S(2)}, u32[]{:S(2)}) %collective-permute-start.25) | collective-permute-done | bytes 622624 | tf_op jit(solution)/shard_map/ppermute | solution.py:353
  241.4 19.8 %collective-permute-done.48 = bf16[256,1024]{1,0:T(8,128)(2,1)} collective-permute-done((bf16[256,1024]{1,0:T(8,128)(2,1)}, bf16[256,1024]{1,0:T(8,128)(2,1)}, u32[]{:S(2)}, u32[]{:S(2)}) %collective-permute-start.48) | collective-permute-done | bytes 524320 | tf_op jit(solution)/shard_map/ppermute | solution.py:353
  268.1 6.3 %collective-permute-done.49 = bf16[2,128,1024]{2,1,0:T(8,128)(2,1)S(1)} collective-permute-done((bf16[2,128,1024]{2,1,0:T(8,128)(2,1)S(1)}, bf16[2,128,1024]{2,1,0:T(8,128)(2,1)S(1)}, u32[]{:S(2)}, u32[]{:S(2)}) %collective-permute-start.49) | collective-permute-done | bytes 524320 | tf_op jit(solution)/shard_map/ppermute | solution.py:353
  278.2 4.4 %shard_map.324 = (bf16[1216,384]{1,0:T(8,128)(2,1)S(1)}, f32[2,8,128]{2,1,0:T(8,128)S(1)}) custom-call(bf16[1216,384]{1,0:T(8,128)(2,1)S(1)} %copy-done.5, bf16[2,2,608,608]{3,2,1,0:T(8,128)(2,1)S(1)} %copy-done.1, bf16[1216,128]{1,0:T(8,128)(2,1)S(1)} %get-tuple-element.95.grad_ref), custom_call_target="tpu_custom_call" | custom-call | flops 757071872 | bytes 5136384 | tf_op jit(solution)/shard_map/pallas_call | solution.py:445
  282.8 4.2 %shard_map.325 = (bf16[1216,384]{1,0:T(8,128)(2,1)S(1)}, f32[2,8,128]{2,1,0:T(8,128)S(1)}) custom-call(bf16[1216,384]{1,0:T(8,128)(2,1)S(1)} %copy-done.3, bf16[2,2,608,608]{3,2,1,0:T(8,128)(2,1)S(1)} %get-tuple-element.30.probs_ref, bf16[1216,128]{1,0:T(8,128)(2,1)S(1)} %get-tuple-element.94.grad_ref), custom_call_target="tpu_custom_call" | custom-call | flops 757071872 | bytes 5136384 | tf_op jit(solution)/shard_map/pallas_call | solution.py:445
  303.4 7.8 %collective-permute-done.34 = bf16[4,2,32,1024]{3,2,0,1:T(8,128)(2,1)} collective-permute-done((bf16[4,2,32,1024]{3,2,0,1:T(8,128)(2,1)}, bf16[4,2,32,1024]{3,2,0,1:T(8,128)(2,1)}, u32[]{:S(2)}, u32[]{:S(2)}) %collective-permute-start.34) | collective-permute-done | bytes 524320 | tf_op jit(solution)/shard_map/ppermute | solution.py:353
  312.3 12.8 %collective-permute-start.36 = (bf16[4,32,1024]{2,1,0:T(8,128)(2,1)S(1)}, bf16[4,32,1024]{2,1,0:T(8,128)(2,1)S(1)}, u32[]{:S(2)}, u32[]{:S(2)}) collective-permute-start(bf16[4,32,1024]{2,1,0:T(8,128)(2,1)S(1)} %get-tuple-element.112), channel_id=1, source_target_pairs={{0,4},{1,5},{2,6},{3,7},{4,0},{5,1},{6,2},{7,3},{8,12},{9,13},{10,... | collective-permute-start | bytes 786440 | tf_op jit(solution)/shard_map/ppermute | solution.py:353
  326.5 3.8 collective-permute-start.33
  330.7 12.0 %collective-permute-done.36 = bf16[4,32,1024]{2,1,0:T(8,128)(2,1)S(1)} collective-permute-done((bf16[4,32,1024]{2,1,0:T(8,128)(2,1)S(1)}, bf16[4,32,1024]{2,1,0:T(8,128)(2,1)S(1)}, u32[]{:S(2)}, u32[]{:S(2)}) %collective-permute-start.36) | collective-permute-done | bytes 262176 | tf_op jit(solution)/shard_map/ppermute | solution.py:353
  343.0 4.0 collective-permute-done.33
  350.4 5.2 %collective-permute-done.37 = bf16[4,32,1024]{2,1,0:T(8,128)(2,1)S(1)} collective-permute-done((bf16[4,32,1024]{2,1,0:T(8,128)(2,1)S(1)}, bf16[4,32,1024]{2,1,0:T(8,128)(2,1)S(1)}, u32[]{:S(2)}, u32[]{:S(2)}) %collective-permute-start.37) | collective-permute-done | bytes 262176 | tf_op jit(solution)/shard_map/ppermute | solution.py:353
  364.5 11.3 %collective-permute-done.30 = bf16[304,1024]{1,0:T(8,128)(2,1)S(1)} collective-permute-done((bf16[304,1024]{1,0:T(8,128)(2,1)}, bf16[304,1024]{1,0:T(8,128)(2,1)S(1)}, u32[]{:S(2)}, u32[]{:S(2)}) %collective-permute-start.30) | collective-permute-done | bytes 622624 | tf_op jit(solution)/shard_map/ppermute | solution.py:353
  377.7 3.9 fusion.26
  402.4 3.6 collective-permute-done.43
  (404 shorter events, 184.1 us)
Async XLA Ops:
  10.5 30.7 %collective-permute-start.5 = (bf16[136,1024]{1,0:T(8,128)(2,1)}, bf16[136,1024]{1,0:T(8,128)(2,1)S(1)}, u32[]{:S(2)}, u32[]{:S(2)}) collective-permute-start(bf16[136,1024]{1,0:T(8,128)(2,1)} %constant_dynamic-update-slice_fusion), channel_id=1, source_target_pairs={{0,6},{1,7},{2,0},{3,1},{4,2},{5,3},{6,4},{7,5},{8,14},{9,15},{10,... | collective-permute-start | bytes 835592 | tf_op jit(solution)/shard_map/ppermute | solution.py:353
  15.6 29.0 %collective-permute-start.4 = (bf16[136,1024]{1,0:T(8,128)(2,1)}, bf16[136,1024]{1,0:T(8,128)(2,1)S(1)}, u32[]{:S(2)}, u32[]{:S(2)}) collective-permute-start(bf16[136,1024]{1,0:T(8,128)(2,1)} %constant_dynamic-update-slice_fusion), channel_id=1, source_target_pairs={{0,2},{1,3},{2,4},{3,5},{4,6},{5,7},{6,0},{7,1},{8,10},{9,11},{10,... | collective-permute-start | bytes 835592 | tf_op jit(solution)/shard_map/ppermute | solution.py:353
  15.6 36.5 %collective-permute-start.7 = (bf16[136,1024]{1,0:T(8,128)(2,1)}, bf16[136,1024]{1,0:T(8,128)(2,1)}, u32[]{:S(2)}, u32[]{:S(2)}) collective-permute-start(bf16[136,1024]{1,0:T(8,128)(2,1)} %constant_dynamic-update-slice_fusion), channel_id=1, source_target_pairs={{0,4},{1,5},{2,6},{3,7},{4,0},{5,1},{6,2},{7,3},{8,12},{9,13},{10,... | collective-permute-start | bytes 835592 | tf_op jit(solution)/shard_map/ppermute | solution.py:353
  18.2 18.5 %collective-permute-start = (bf16[8,1024]{1,0:T(8,128)(2,1)S(1)}, bf16[8,1024]{1,0:T(8,128)(2,1)S(1)}, u32[]{:S(2)}, u32[]{:S(2)}) collective-permute-start(bf16[8,1024]{1,0:T(8,128)(2,1)S(1)} %pad_maximum_fusion.17), channel_id=1, source_target_pairs={{0,1},{1,2},{2,3},{3,4},{4,5},{5,6},{6,7},{8,9},{9,10},{10,11},{11... | collective-permute-start | bytes 49160 | tf_op jit(solution)/shard_map/ppermute | solution.py:353
  28.5 77.1 %collective-permute-start.14 = (bf16[256,1024]{1,0:T(8,128)(2,1)}, bf16[256,1024]{1,0:T(8,128)(2,1)}, u32[]{:S(2)}, u32[]{:S(2)}) collective-permute-start(bf16[256,1024]{1,0:T(8,128)(2,1)} %pad_maximum_fusion.9), channel_id=1, source_target_pairs={{0,2},{1,3},{2,4},{3,5},{4,6},{5,7},{6,0},{7,1},{8,10},{9,11},{10,... | collective-permute-start | bytes 1572872 | tf_op jit(solution)/shard_map/ppermute | solution.py:353
  36.7 69.2 %collective-permute-start.15 = (bf16[256,1024]{1,0:T(8,128)(2,1)}, bf16[256,1024]{1,0:T(8,128)(2,1)}, u32[]{:S(2)}, u32[]{:S(2)}) collective-permute-start(bf16[256,1024]{1,0:T(8,128)(2,1)} %pad_maximum_fusion.9), channel_id=1, source_target_pairs={{0,6},{1,7},{2,0},{3,1},{4,2},{5,3},{6,4},{7,5},{8,14},{9,15},{10,... | collective-permute-start | bytes 1572872 | tf_op jit(solution)/shard_map/ppermute | solution.py:353
  41.3 24.5 %collective-permute-start.1 = (bf16[304,1024]{1,0:T(8,128)(2,1)}, bf16[304,1024]{1,0:T(8,128)(2,1)}, u32[]{:S(2)}, u32[]{:S(2)}) collective-permute-start(bf16[304,1024]{1,0:T(8,128)(2,1)} %fusion.21), channel_id=1, source_target_pairs={{0,1},{1,0},{2,3},{3,2},{4,5},{5,4},{6,7},{7,6},{8,9},{9,8},{10,11... | collective-permute-start | bytes 1867784 | tf_op jit(solution)/shard_map/ppermute | solution.py:353
  44.6 21.2 %collective-permute-start.6 = (bf16[2,136,1024]{2,1,0:T(8,128)(2,1)S(1)}, bf16[2,136,1024]{2,1,0:T(8,128)(2,1)S(1)}, u32[]{:S(2)}, u32[]{:S(2)}) collective-permute-start(bf16[2,136,1024]{2,1,0:T(8,128)(2,1)S(1)} %pad_maximum_fusion.8), channel_id=1, source_target_pairs={{0,16},{1,17},{2,18},{3,19},{4,20},{5,21},{6,22},{7,23},{8,24},{9,... | collective-permute-start | bytes 1671176 | tf_op jit(solution)/shard_map/ppermute | solution.py:353
  63.0 46.7 %collective-permute-start.16 = (bf16[256,1024]{1,0:T(8,128)(2,1)}, bf16[256,1024]{1,0:T(8,128)(2,1)}, u32[]{:S(2)}, u32[]{:S(2)}) collective-permute-start(bf16[256,1024]{1,0:T(8,128)(2,1)} %pad_maximum_fusion.9), channel_id=1, source_target_pairs={{0,4},{1,5},{2,6},{3,7},{4,0},{5,1},{6,2},{7,3},{8,12},{9,13},{10,... | collective-permute-start | bytes 1572872 | tf_op jit(solution)/shard_map/ppermute | solution.py:353
  65.8 16.7 %collective-permute-start.2 = (bf16[304,1024]{1,0:T(8,128)(2,1)}, bf16[304,1024]{1,0:T(8,128)(2,1)}, u32[]{:S(2)}, u32[]{:S(2)}) collective-permute-start(bf16[304,1024]{1,0:T(8,128)(2,1)} %fusion.21), channel_id=1, source_target_pairs={{0,8},{1,9},{2,10},{3,11},{4,12},{5,13},{6,14},{7,15},{8,0},{9,1},... | collective-permute-start | bytes 1867784 | tf_op jit(solution)/shard_map/ppermute | solution.py:353
  101.6 37.4 %collective-permute-start.21 = (bf16[304,1024]{1,0:T(8,128)(2,1)}, bf16[304,1024]{1,0:T(8,128)(2,1)}, u32[]{:S(2)}, u32[]{:S(2)}) collective-permute-start(bf16[304,1024]{1,0:T(8,128)(2,1)} %get-tuple-element.57), channel_id=1, source_target_pairs={{0,1},{1,0},{2,3},{3,2},{4,5},{5,4},{6,7},{7,6},{8,9},{9,8},{10,11... | collective-permute-start | bytes 1867784 | tf_op jit(solution)/shard_map/ppermute | solution.py:353
  105.6 57.9 %collective-permute-start.22 = (bf16[304,1024]{1,0:T(8,128)(2,1)}, bf16[304,1024]{1,0:T(8,128)(2,1)}, u32[]{:S(2)}, u32[]{:S(2)}) collective-permute-start(bf16[304,1024]{1,0:T(8,128)(2,1)} %get-tuple-element.57), channel_id=1, source_target_pairs={{0,8},{1,9},{2,10},{3,11},{4,12},{5,13},{6,14},{7,15},{8,0},{9,1},... | collective-permute-start | bytes 1867784 | tf_op jit(solution)/shard_map/ppermute | solution.py:353
  108.2 33.1 %collective-permute-start.17 = (bf16[2,256,1024]{2,1,0:T(8,128)(2,1)}, bf16[2,256,1024]{2,1,0:T(8,128)(2,1)}, u32[]{:S(2)}, u32[]{:S(2)}) collective-permute-start(bf16[2,256,1024]{2,1,0:T(8,128)(2,1)} %pad_maximum_fusion.6), channel_id=1, source_target_pairs={{0,16},{1,17},{2,18},{3,19},{4,20},{5,21},{6,22},{7,23},{8,24},{9,... | collective-permute-start | bytes 3145736 | tf_op jit(solution)/shard_map/ppermute | solution.py:353
  109.7 46.5 %collective-permute-start.18 = (bf16[256,1024]{1,0:T(8,128)(2,1)}, bf16[256,1024]{1,0:T(8,128)(2,1)}, u32[]{:S(2)}, u32[]{:S(2)}) collective-permute-start(bf16[256,1024]{1,0:T(8,128)(2,1)} %collective-permute-done.16), channel_id=1, source_target_pairs={{0,16},{1,17},{2,18},{3,19},{4,20},{5,21},{6,22},{7,23},{8,24},{9,... | collective-permute-start | bytes 1572872 | tf_op jit(solution)/shard_map/ppermute | solution.py:353
  113.6 17.9 %collective-permute-start.10 = (bf16[304,1024]{1,0:T(8,128)(2,1)S(1)}, bf16[304,1024]{1,0:T(8,128)(2,1)S(1)}, u32[]{:S(2)}, u32[]{:S(2)}) collective-permute-start(bf16[304,1024]{1,0:T(8,128)(2,1)S(1)} %fusion.8), channel_id=1, source_target_pairs={{0,1},{1,0},{2,3},{3,2},{4,5},{5,4},{6,7},{7,6},{8,9},{9,8},{10,11... | collective-permute-start | bytes 1867784 | tf_op jit(solution)/shard_map/ppermute | solution.py:353
  139.0 24.6 %collective-permute-start.23 = (bf16[304,1024]{1,0:T(8,128)(2,1)}, bf16[304,1024]{1,0:T(8,128)(2,1)}, u32[]{:S(2)}, u32[]{:S(2)}) collective-permute-start(bf16[304,1024]{1,0:T(8,128)(2,1)} %collective-permute-done.21), channel_id=1, source_target_pairs={{0,8},{1,9},{2,10},{3,11},{4,12},{5,13},{6,14},{7,15},{8,0},{9,1},... | collective-permute-start | bytes 1867784 | tf_op jit(solution)/shard_map/ppermute | solution.py:353
  141.3 16.8 %collective-permute-start.12 = (bf16[304,1024]{1,0:T(8,128)(2,1)}, bf16[304,1024]{1,0:T(8,128)(2,1)S(1)}, u32[]{:S(2)}, u32[]{:S(2)}) collective-permute-start(bf16[304,1024]{1,0:T(8,128)(2,1)} %add_convert_fusion.2), channel_id=1, source_target_pairs={{0,8},{1,9},{2,10},{3,11},{4,12},{5,13},{6,14},{7,15},{8,0},{9,1},... | collective-permute-start | bytes 1867784 | tf_op jit(solution)/shard_map/ppermute | solution.py:353
  167.7 26.0 %collective-permute-start.45 = (bf16[512,1024]{1,0:T(8,128)(2,1)S(1)}, bf16[512,1024]{1,0:T(8,128)(2,1)S(1)}, u32[]{:S(2)}, u32[]{:S(2)}) collective-permute-start(bf16[512,1024]{1,0:T(8,128)(2,1)S(1)} %convolution_convert_fusion.5), channel_id=1, source_target_pairs={{0,16},{1,17},{2,18},{3,19},{4,20},{5,21},{6,22},{7,23},{8,24},{9,... | collective-permute-start | bytes 3145736 | tf_op jit(solution)/shard_map/ppermute | solution.py:353
  176.8 41.9 %collective-permute-start.24 = (bf16[608,1024]{1,0:T(8,128)(2,1)S(1)}, bf16[608,1024]{1,0:T(8,128)(2,1)S(1)}, u32[]{:S(2)}, u32[]{:S(2)}) collective-permute-start(bf16[608,1024]{1,0:T(8,128)(2,1)S(1)} %convolution_convert_fusion.2), channel_id=1, source_target_pairs={{0,8},{1,9},{2,10},{3,11},{4,12},{5,13},{6,14},{7,15},{8,0},{9,1},... | collective-permute-start | bytes 3735560 | tf_op jit(solution)/shard_map/ppermute | solution.py:353
  179.9 35.9 %collective-permute-start.44 = (bf16[512,1024]{1,0:T(8,128)(2,1)S(1)}, bf16[512,1024]{1,0:T(8,128)(2,1)S(1)}, u32[]{:S(2)}, u32[]{:S(2)}) collective-permute-start(bf16[512,1024]{1,0:T(8,128)(2,1)S(1)} %convolution_convert_fusion.6), channel_id=1, source_target_pairs={{0,16},{1,17},{2,18},{3,19},{4,20},{5,21},{6,22},{7,23},{8,24},{9,... | collective-permute-start | bytes 3145736 | tf_op jit(solution)/shard_map/ppermute | solution.py:353
  183.1 82.1 %collective-permute-start.19 = (bf16[608,1024]{1,0:T(8,128)(2,1)}, bf16[608,1024]{1,0:T(8,128)(2,1)}, u32[]{:S(2)}, u32[]{:S(2)}) collective-permute-start(bf16[608,1024]{1,0:T(8,128)(2,1)} %convolution_convert_fusion.3), channel_id=1, source_target_pairs={{0,8},{1,9},{2,10},{3,11},{4,12},{5,13},{6,14},{7,15},{8,0},{9,1},... | collective-permute-start | bytes 3735560 | tf_op jit(solution)/shard_map/ppermute | solution.py:353
  222.9 38.3 %collective-permute-start.48 = (bf16[256,1024]{1,0:T(8,128)(2,1)}, bf16[256,1024]{1,0:T(8,128)(2,1)}, u32[]{:S(2)}, u32[]{:S(2)}) collective-permute-start(bf16[256,1024]{1,0:T(8,128)(2,1)} %pad_maximum_fusion.13), channel_id=1, source_target_pairs={{0,4},{1,5},{2,6},{3,7},{4,0},{5,1},{6,2},{7,3},{8,12},{9,13},{10,... | collective-permute-start | bytes 1572872 | tf_op jit(solution)/shard_map/ppermute | solution.py:353
  223.7 37.5 %collective-permute-start.47 = (bf16[256,1024]{1,0:T(8,128)(2,1)}, bf16[256,1024]{1,0:T(8,128)(2,1)}, u32[]{:S(2)}, u32[]{:S(2)}) collective-permute-start(bf16[256,1024]{1,0:T(8,128)(2,1)} %pad_maximum_fusion.12), channel_id=1, source_target_pairs={{0,2},{1,3},{2,4},{3,5},{4,6},{5,7},{6,0},{7,1},{8,10},{9,11},{10,... | collective-permute-start | bytes 1572872 | tf_op jit(solution)/shard_map/ppermute | solution.py:353
  226.3 34.9 %collective-permute-start.46 = (bf16[256,1024]{1,0:T(8,128)(2,1)}, bf16[256,1024]{1,0:T(8,128)(2,1)}, u32[]{:S(2)}, u32[]{:S(2)}) collective-permute-start(bf16[256,1024]{1,0:T(8,128)(2,1)} %pad_maximum_fusion.11), channel_id=1, source_target_pairs={{0,6},{1,7},{2,0},{3,1},{4,2},{5,3},{6,4},{7,5},{8,14},{9,15},{10,... | collective-permute-start | bytes 1572872 | tf_op jit(solution)/shard_map/ppermute | solution.py:353
  239.5 25.2 %collective-permute-start.26 = (bf16[304,1024]{1,0:T(8,128)(2,1)}, bf16[304,1024]{1,0:T(8,128)(2,1)}, u32[]{:S(2)}, u32[]{:S(2)}) collective-permute-start(bf16[304,1024]{1,0:T(8,128)(2,1)} %get-tuple-element.59), channel_id=1, source_target_pairs={{0,1},{1,0},{2,3},{3,2},{4,5},{5,4},{6,7},{7,6},{8,9},{9,8},{10,11... | collective-permute-start | bytes 1867784 | tf_op jit(solution)/shard_map/ppermute | solution.py:353
  275.7 73.0 %collective-permute-start.50 = (bf16[2,2,128,1024]{3,2,0,1:T(8,128)(2,1)}, bf16[2,2,128,1024]{3,2,0,1:T(8,128)(2,1)}, u32[]{:S(2)}, u32[]{:S(2)}) collective-permute-start(bf16[2,2,128,1024]{3,2,0,1:T(8,128)(2,1)} %pad_maximum_fusion.7), channel_id=1, source_target_pairs={{0,8},{1,9},{2,10},{3,11},{4,12},{5,13},{6,14},{7,15},{8,0},{9,1},... | collective-permute-start | bytes 3145736 | tf_op jit(solution)/shard_map/ppermute | solution.py:353
  289.4 67.0 %collective-permute-start.29 = (bf16[608,1024]{1,0:T(8,128)(2,1)}, bf16[608,1024]{1,0:T(8,128)(2,1)}, u32[]{:S(2)}, u32[]{:S(2)}) collective-permute-start(bf16[608,1024]{1,0:T(8,128)(2,1)} %convolution_convert_fusion.1), channel_id=1, source_target_pairs={{0,8},{1,9},{2,10},{3,11},{4,12},{5,13},{6,14},{7,15},{8,0},{9,1},... | collective-permute-start | bytes 3735560 | tf_op jit(solution)/shard_map/ppermute | solution.py:353
  302.3 22.8 %collective-permute-start.32 = (bf16[4,2,32,1024]{3,2,1,0:T(8,128)(2,1)}, bf16[4,2,32,1024]{3,2,1,0:T(8,128)(2,1)}, u32[]{:S(2)}, u32[]{:S(2)}) collective-permute-start(bf16[4,2,32,1024]{3,2,1,0:T(8,128)(2,1)} %fusion.53), channel_id=1, source_target_pairs={{0,16},{1,17},{2,18},{3,19},{4,20},{5,21},{6,22},{7,23},{8,24},{9,... | collective-permute-start | bytes 1572872 | tf_op jit(solution)/shard_map/ppermute | solution.py:353
  312.3 30.3 %collective-permute-start.36 = (bf16[4,32,1024]{2,1,0:T(8,128)(2,1)S(1)}, bf16[4,32,1024]{2,1,0:T(8,128)(2,1)S(1)}, u32[]{:S(2)}, u32[]{:S(2)}) collective-permute-start(bf16[4,32,1024]{2,1,0:T(8,128)(2,1)S(1)} %get-tuple-element.112), channel_id=1, source_target_pairs={{0,4},{1,5},{2,6},{3,7},{4,0},{5,1},{6,2},{7,3},{8,12},{9,13},{10,... | collective-permute-start | bytes 786440 | tf_op jit(solution)/shard_map/ppermute | solution.py:353
  325.2 17.8 %collective-permute-start.35 = (bf16[4,32,1024]{2,1,0:T(8,128)(2,1)S(1)}, bf16[4,32,1024]{2,1,0:T(8,128)(2,1)S(1)}, u32[]{:S(2)}, u32[]{:S(2)}) collective-permute-start(bf16[4,32,1024]{2,1,0:T(8,128)(2,1)S(1)} %get-tuple-element.111), channel_id=1, source_target_pairs={{0,2},{1,3},{2,4},{3,5},{4,6},{5,7},{6,0},{7,1},{8,10},{9,11},{10,... | collective-permute-start | bytes 786440 | tf_op jit(solution)/shard_map/ppermute | solution.py:353
  326.5 20.5 %collective-permute-start.33 = (bf16[4,32,1024]{2,1,0:T(8,128)(2,1)S(1)}, bf16[4,32,1024]{2,1,0:T(8,128)(2,1)S(1)}, u32[]{:S(2)}, u32[]{:S(2)}) collective-permute-start(bf16[4,32,1024]{2,1,0:T(8,128)(2,1)S(1)} %slice_bitcast_fusion.4), channel_id=1, source_target_pairs={{0,6},{1,7},{2,0},{3,1},{4,2},{5,3},{6,4},{7,5},{8,14},{9,15},{10,... | collective-permute-start | bytes 786440 | tf_op jit(solution)/shard_map/ppermute | solution.py:353
  342.7 35.0 %collective-permute-start.20 = (bf16[304,1024]{1,0:T(8,128)(2,1)}, bf16[304,1024]{1,0:T(8,128)(2,1)}, u32[]{:S(2)}, u32[]{:S(2)}) collective-permute-start(bf16[304,1024]{1,0:T(8,128)(2,1)} %fusion.9), channel_id=1, source_target_pairs={{0,1},{1,0},{2,3},{3,2},{4,5},{5,4},{6,7},{7,6},{8,9},{9,8},{10,11... | collective-permute-start | bytes 1867784 | tf_op jit(solution)/shard_map/ppermute | solution.py:353
  (73 other events, 764.7 us)

commit v2 on v0

--- a/solution.py
+++ b/solution.py
@@ -1,6 +1,10 @@
+import functools
+
 import jax
 import jax.numpy as jnp
 from jax import lax
+from jax.experimental import pallas as pl
+from jax.experimental.pallas import tpu as pltpu
 from jax.sharding import PartitionSpec as P
 
 D = 1024
@@ -99,7 +103,7 @@
     return values.reshape(images, values.shape[0] // images, values.shape[1])
 
 
-def on_device(
+def on_device_general(
     inputs,
     valid,
     cotangent,
@@ -317,6 +321,989 @@
     )
 
 
+BF16 = jnp.bfloat16
+F32 = jnp.float32
+AXES = ("tok", "feat")
+SLOTS = (0, 1, 3, 2)
+PAIRS = ((0, 1), (3, 2))
+CHUNK = 16
+PART = DH // 2
+
+
+def route(move):
+    found = []
+    for tok in range(4):
+        for feat in range(8):
+            target = move(tok // 2, tok % 2, feat // 2, feat % 2)
+            if target is not None:
+                x, c, z, y = target
+                found.append((tok * 8 + feat, (2 * x + c) * 8 + 2 * z + y))
+    return found
+
+
+SWAP_X = route(lambda x, c, z, y: (1 - x, c, z, y))
+SWAP_C = route(lambda x, c, z, y: (x, 1 - c, z, y))
+SWAP_Y = route(lambda x, c, z, y: (x, c, z, 1 - y))
+UP_Z = route(lambda x, c, z, y: (x, c, (z + 1) % 4, y))
+DOWN_Z = route(lambda x, c, z, y: (x, c, (z + 3) % 4, y))
+FLIP_Z = [route(lambda x, c, z, y, s=s: (x, c, z ^ s, y)) for s in range(4)]
+NEXT = [(t * 8 + f, t * 8 + f + 1) for t in range(4) for f in range(7)]
+PREVIOUS = [(t * 8 + f + 1, t * 8 + f) for t in range(4) for f in range(7)]
+
+
+def send(values, pairs):
+    return lax.ppermute(values, AXES, pairs)
+
+
+def nt(left, right):
+    return lax.dot_general(left, right, (((1,), (1,)), ((), ())), preferred_element_type=F32)
+
+
+def nn(left, right):
+    return lax.dot_general(left, right, (((1,), (0,)), ((), ())), preferred_element_type=F32)
+
+
+def tn(left, right):
+    return lax.dot_general(left, right, (((0,), (0,)), ((), ())), preferred_element_type=F32)
+
+
+SMEM = pl.BlockSpec(memory_space=pltpu.SMEM)
+HBM = pl.BlockSpec(memory_space=pltpu.HBM)
+VMEM = pl.BlockSpec(memory_space=pltpu.VMEM)
+
+
+def kernel_call(body, operands, specs, outs, scratch=(), after=(), vmem=12):
+    count, extra = len(operands), len(after)
+
+    def kernel(*refs):
+        body(*refs[:count], *refs[count + extra :])
+
+    return pl.pallas_call(
+        kernel,
+        in_specs=list(specs) + [VMEM] * extra,
+        out_specs=[VMEM] * len(outs),
+        out_shape=[jax.ShapeDtypeStruct(shape, dtype) for shape, dtype in outs],
+        scratch_shapes=list(scratch),
+        compiler_params=pltpu.CompilerParams(
+            vmem_limit_bytes=vmem * 2**20, fuse_transposed_lhs_in_matmul=True
+        ),
+        cost_estimate=pl.CostEstimate(flops=10**10, bytes_accessed=2**16, transcendentals=0),
+    )(*operands, *after)
+
+
+def coordinates():
+    tok, feat = lax.axis_index("tok"), lax.axis_index("feat")
+    return tok // 2, tok % 2, feat // 2, feat % 2
+
+
+def chunks(half):
+    return [slice(at, at + CHUNK) for at in range(0, half, CHUNK)]
+
+
+def row_of(vector):
+    return vector[...].astype(F32).reshape(1, vector.shape[0])
+
+
+def folded(values):
+    return values[:8] + values[8:]
+
+
+def moment_norm(values):
+    center = jnp.mean(values, axis=1, keepdims=True)
+    spread = jnp.mean(values * values, axis=1, keepdims=True) - center * center
+    inverse = lax.rsqrt(spread + EPSILON)
+    return (values - center) * inverse, inverse
+
+
+def attention_weights_kernel(wq, wk, wv, wo, b_query, b_value, b_hidden, *refs):
+    own, other, both, query, value, hidden, sems = refs
+    piece = own.shape[0]
+    x, c, _, _ = coordinates()
+    width = own.shape[1]
+    copies = []
+    for source, target in ((b_query, query), (b_value, value), (b_hidden, hidden)):
+        copies.append(pltpu.make_async_copy(source, target, sems.at[len(copies)]))
+    targets = ((own, 0, x), (other, 0, 1 - x), (both, 0, x), (both, piece, 1 - x))
+    for out, first, side in targets:
+        at = pl.multiple_of(c * DH + side * PART, PART)
+        for m, w in enumerate((wq, wk, wv, wo)):
+            copies.append(
+                pltpu.make_async_copy(
+                    w.at[pl.ds(at, PART)], out.at[pl.ds(first + m * PART, PART)], sems.at[len(copies)]
+                )
+            )
+    for copy in copies:
+        copy.start()
+    for copy in copies[:3]:
+        copy.wait()
+    parts = [row_of(vector) for vector in (query, value, hidden)]
+    taken = sum(part.shape[1] for part in parts)
+    bias = jnp.concatenate(parts + [jnp.zeros((1, width - taken), F32)], axis=1)
+    bias = jnp.broadcast_to(bias, (16, width)).astype(BF16)
+    for out, first, _ in targets:
+        out[first + 4 * PART : first + piece, :] = bias
+    for copy in copies[3:]:
+        copy.wait()
+
+
+def edge_kernel(inputs, cotangent, edge):
+    rows = inputs.shape[0]
+    at = (rows - 8) // 16 * 16
+    for i, values in enumerate((inputs, cotangent)):
+        edge[8 * i : 8 * i + 8, :] = values[at:, :].astype(F32)[rows - 8 - at :].astype(BF16)
+
+
+def mlp_weights_kernel(w_in, w_out, own, other, both):
+    x, c, _, _ = coordinates()
+    quarter = own.shape[0] // 2
+    for out, first, side in ((own, 0, x), (other, 2 * quarter, 1 - x)):
+        at = pl.multiple_of((2 * c + side) * quarter, quarter)
+        found = w_in[:, pl.ds(at, quarter)].T
+        rest = w_out[pl.ds(at, quarter), :]
+        out[:quarter, :] = found
+        out[quarter:, :] = rest
+        both[first : first + quarter, :] = found
+        both[first + quarter : first + 2 * quarter, :] = rest
+
+
+def halves_of(refs, count):
+    own_zero, other_zero, own_one, other_one, both, own_two, other_two = refs
+    own = [own_zero, own_one, both.at[pl.ds(0, count)], own_two]
+    return own, [other_zero, other_one, both.at[pl.ds(count, count)], other_two]
+
+
+def entry_kernel(
+    valid, inputs, cotangent, edge, gain_vector, shift_vector, stream, normed, branch, again, ext
+):
+    _, _, z, y = coordinates()
+    rows = inputs.shape[0]
+    half = stream.shape[0]
+    gain, shift = row_of(gain_vector), row_of(shift_vector)
+    flag = valid[z].astype(F32)
+
+    def aligned(at):
+        found = pltpu.roll(ext[at.start : at.stop + 8, :], CHUNK + z, 0)[:CHUNK]
+        index = at.start + lax.broadcasted_iota(jnp.int32, (CHUNK, 1), 0)
+        return jnp.where(index < rows - y, found, 0.0)
+
+    def fill(values, first):
+        ext[0:8, :] = edge[...].astype(F32)[first : first + 8]
+        ext[8 : 8 + rows, :] = values[...].astype(F32)
+
+    fill(inputs, 0)
+    for at in chunks(half):
+        found = aligned(at)
+        stream[at, :] = found.astype(BF16)
+        hat, _ = moment_norm(found)
+        normed[at, :] = (hat * gain + shift).astype(BF16)
+    fill(cotangent, 8)
+    for at in chunks(half):
+        branch[at, :] = (aligned(at) * flag).astype(BF16)
+        again[at, :] = branch[at, :]
+
+
+def softmax_columns(scores):
+    top = jnp.max(scores, axis=0, keepdims=True)
+    weights = jnp.exp(scores - top)
+    return weights * (1.0 / jnp.sum(weights, axis=0, keepdims=True))
+
+
+def forward_body(rows, halves, w_in, w_out, bias, qkv, probs, mixed, partials):
+    half = halves[0].shape[0]
+    _, _, _, y = coordinates()
+    entry = jnp.concatenate([halves[0][...], halves[1][...]], axis=0)
+    qkv[...] = (nt(entry, w_in) + bias).astype(BF16)
+    key_index = lax.broadcasted_iota(jnp.int32, (2 * half, 1), 0)
+    first = rows - y
+    second = half + rows - 1 + y
+    real = (key_index < first) | ((key_index >= half) & (key_index < second))
+    penalty = jnp.where(real, 0.0, -1e30)
+    for p in range(2):
+        outs = []
+        for h in (2 * p, 2 * p + 1):
+            at = slice(h * DH, (h + 1) * DH)
+            q = qkv[:, at] * jnp.asarray(DH ** (-0.5), BF16)
+            k = qkv[:, 4 * DH + h * DH : 4 * DH + (h + 1) * DH]
+            v = qkv[:, 8 * DH + h * DH : 8 * DH + (h + 1) * DH]
+            found = softmax_columns(nt(k, q) + penalty).astype(BF16)
+            probs[h] = found
+            outs.append(tn(v, found))
+        mixed[:, 2 * DH * p : 2 * DH * (p + 1)] = jnp.concatenate(outs, axis=0).T.astype(BF16)
+    found = nn(mixed[...], w_out).astype(BF16)
+    at = 0
+    for out in partials:
+        out[...] = found[at : at + out.shape[0]]
+        at += out.shape[0]
+
+
+def ordered_bias(row, first):
+    x, c, _, _ = coordinates()
+    block = jnp.where(c == 0, row[:, first : first + DH], row[:, first + DH : first + 2 * DH])
+    swapped = jnp.concatenate([block[:, PART:], block[:, :PART]], axis=1)
+    return jnp.where(x == 0, block, swapped)
+
+
+def first_forward_kernel(rows, *refs):
+    halves, refs = refs[:2], refs[2:]
+    own, other = halves_of(refs[:7], refs[0].shape[0])
+    refs = refs[7:]
+    qkv, probs, mixed, partial, w_in, w_out, bias = refs
+    for m in range(4):
+        target = w_out if m == 3 else w_in
+        for k in range(4):
+            at = (0 if m == 3 else m * 4 * DH) + k * DH
+            target[at : at + PART, :] = own[k][m * PART : (m + 1) * PART, :]
+            target[at + PART : at + DH, :] = other[k][m * PART : (m + 1) * PART, :]
+    rows_of = [own[k][4 * PART :, :].astype(F32)[0:1] for k in range(4)]
+    query = jnp.concatenate([ordered_bias(r, 0) for r in rows_of], axis=1)
+    value = jnp.concatenate([ordered_bias(r, 2 * DH) for r in rows_of], axis=1)
+    bias[...] = jnp.broadcast_to(
+        jnp.concatenate([query, jnp.zeros_like(query), value], axis=1), bias.shape
+    )
+    forward_body(
+        rows,
+        halves,
+        w_in[...],
+        w_out[...],
+        bias[0:1, :],
+        qkv,
+        probs,
+        mixed,
+        (partial,),
+    )
+
+
+def second_forward_kernel(rows, near, far, w_in, w_out, bias, *refs):
+    qkv, probs, mixed, *partials = refs
+    forward_body(
+        rows,
+        (near, far),
+        w_in[...],
+        w_out[...],
+        bias[0:1, :],
+        qkv,
+        probs,
+        mixed,
+        partials,
+    )
+
+
+def real_rows(at, rows, y):
+    return at.start + lax.broadcasted_iota(jnp.int32, (CHUNK, 1), 0) < rows - y
+
+
+def middle_kernel(
+    rows,
+    valid,
+    partial,
+    from_core,
+    from_y,
+    stream,
+    bias_vector,
+    gain_vector,
+    shift_vector,
+    middle,
+    normed,
+    powers,
+):
+    _, _, z, y = coordinates()
+    bias, gain, shift = row_of(bias_vector), row_of(gain_vector), row_of(shift_vector)
+    total = jnp.zeros((8, middle.shape[1]), F32)
+    for at in chunks(middle.shape[0]):
+        attn = partial[at, :].astype(F32) + from_core[at, :].astype(F32)
+        attn = attn + from_y[at, :].astype(F32) + bias
+        found = stream[at, :].astype(F32) + attn
+        middle[at, :] = found
+        hat, _ = moment_norm(found)
+        normed[at, :] = (hat * gain + shift).astype(BF16)
+        total = total + folded(jnp.where(real_rows(at, rows, y), attn * attn, 0.0))
+    powers[...] = total * valid[z].astype(F32)
+
+
+def mlp_kernel(near, far, grad_near, grad_far, *refs):
+    own, other = halves_of(refs[:7], refs[0].shape[0])
+    bias_of, refs = refs[7:11], refs[11:]
+    active, grad_hidden, mid_near, mid_far, out_near, out_far, sums = refs
+    x, c, _, _ = coordinates()
+    half = near.shape[0]
+    quarter = own[0].shape[0] // 2
+    w_in = [ref[:quarter, :] for side in (own, other) for ref in side]
+    w_out = [ref[quarter:, :] for side in (own, other) for ref in side]
+    bias = []
+    for side in (x, 1 - x):
+        at = pl.multiple_of(4 * DH + (2 * c + side) * quarter, quarter)
+        for k in range(4):
+            bias.append(bias_of[k][4 * PART :, pl.ds(at, quarter)].astype(F32)[0:1])
+    bias = jnp.concatenate(bias, axis=1)
+    rows = jnp.concatenate([near[...], far[...]], axis=0)
+    grads = jnp.concatenate([grad_near[...], grad_far[...]], axis=0)
+    size = 2 * quarter
+    for n in range(4):
+        at = slice(n * size, (n + 1) * size)
+        pair = slice(2 * n, 2 * n + 2)
+        u = nt(rows, jnp.concatenate(w_in[pair], axis=0)) + bias[:, at]
+        gate = jax.nn.sigmoid(SLOPE * u)
+        act = u * gate
+        active[:, at] = act.astype(BF16)
+        slope = gate + SLOPE * act * (1.0 - gate)
+        found = (nt(grads, jnp.concatenate(w_out[pair], axis=0)) * slope).astype(BF16)
+        grad_hidden[:, at] = found
+        sums[:, at] = jnp.broadcast_to(
+            jnp.sum(found.astype(F32), axis=0, keepdims=True), (8, size)
+        )
+    found = nn(grad_hidden[...], jnp.concatenate(w_in, axis=0)).astype(BF16)
+    mid_near[...] = found[:half]
+    mid_far[...] = found[half:]
+    found = nn(active[...], jnp.concatenate(w_out, axis=0)).astype(BF16)
+    out_near[...] = found[:half]
+    out_far[...] = found[half:]
+
+
+def products_kernel(split, left_first, left_second, *refs):
+    pieces, outs = refs[:4], refs[4:]
+    right = jnp.concatenate([piece[...] for piece in pieces], axis=0)
+    hidden = left_first.shape[1] // 2
+    quarter = hidden // 4
+    for side in (1, 0):
+        at = slice(side * hidden, (side + 1) * hidden)
+        left = jnp.concatenate([left_first[:, at], left_second[:, at]], axis=0)
+        found = tn(left, right).astype(BF16)
+        if split:
+            for k in range(4):
+                outs[k][side * quarter : (side + 1) * quarter, :] = found[
+                    k * quarter : (k + 1) * quarter
+                ]
+        else:
+            outs[side][...] = found
+
+
+def far_sum_kernel(values, received, out):
+    first = received.shape[0] - out.shape[0]
+    for at in chunks(out.shape[0]):
+        moved = slice(first + at.start, first + at.stop)
+        out[at, :] = (values[at, :].astype(F32) + received[moved, :].astype(F32)).astype(BF16)
+
+
+def add_split_kernel(keep, received, *outs):
+    at = 0
+    for out in outs:
+        size = out.shape[0]
+        out[...] = (
+            keep[at : at + size, :].astype(F32) + received[at : at + size, :].astype(F32)
+        ).astype(BF16)
+        at += size
+
+
+def output_kernel(
+    rows,
+    valid,
+    partial,
+    from_core,
+    from_y,
+    middle,
+    stream,
+    bias_vector,
+    attn_power,
+    sums,
+    output,
+    heads,
+    small,
+):
+    _, _, z, y = coordinates()
+    bias = row_of(bias_vector)
+    width = middle.shape[1]
+    totals = [jnp.zeros((8, width), F32) for _ in range(3)]
+    for at in chunks(middle.shape[0]):
+        branch = partial[at, :].astype(F32) + from_core[at, :].astype(F32)
+        branch = branch + from_y[at, :].astype(F32) + bias
+        found = middle[at, :] + branch
+        output[at, :] = found
+        entry = stream[at, :].astype(F32)
+        real = real_rows(at, rows, y)
+        for i, v in enumerate((entry, branch, found)):
+            totals[i] = totals[i] + folded(jnp.where(real, v * v, 0.0))
+    heads[...] = output[0:8, :]
+    flag = valid[z]
+    lane = lax.broadcasted_iota(jnp.int32, (1, width), 1)
+    entry = jnp.where(lane == 4, (flag * (rows - y)).astype(F32), 0.0)
+    powers = [totals[0] * flag.astype(F32), attn_power[...]]
+    powers += [total * flag.astype(F32) for total in totals[1:]]
+    for i, power in enumerate(powers):
+        whole = jnp.sum(jnp.sum(power, axis=0, keepdims=True), axis=1, keepdims=True)
+        entry = entry + jnp.where(lane == i, whole, 0.0)
+    row = lax.broadcasted_iota(jnp.int32, (8, 1), 0)
+    small[...] = jnp.where(row == 6, entry, sums[...])
+
+
+def norm_back(grad, hat, inverse, gain):
+    scaled = grad * gain
+    plain = jnp.mean(scaled, axis=1, keepdims=True)
+    cross = jnp.mean(scaled * hat, axis=1, keepdims=True)
+    return inverse * (scaled - plain - hat * cross)
+
+
+def middle_back_kernel(
+    partial, from_core, from_y, middle, branch, gain_vector, grad, low, sums
+):
+    width = middle.shape[1]
+    gain = row_of(gain_vector)
+    totals = [jnp.zeros((8, width), F32) for _ in range(4)]
+    for at in chunks(middle.shape[0]):
+        found = partial[at, :].astype(F32) + from_core[at, :].astype(F32)
+        found = found + from_y[at, :].astype(F32)
+        hat, inverse = moment_norm(middle[at, :])
+        gy = branch[at, :].astype(F32)
+        total = gy + norm_back(found, hat, inverse, gain)
+        grad[at, :] = total
+        rounded = total.astype(BF16)
+        low[at, :] = rounded
+        for i, v in enumerate((rounded.astype(F32), gy, found * hat, found)):
+            totals[i] = totals[i] + folded(v)
+    sums[...] = jnp.concatenate(
+        [jnp.sum(v, axis=0, keepdims=True) for v in totals] + [jnp.zeros((4, width), F32)], axis=0
+    )
+
+
+def backward_kernel(pair, *refs):
+    grads, normed, refs = refs[:4], refs[4:8], refs[8:]
+    w_out, qkv_own, qkv_other, probs_own, probs_other = refs[:5]
+    mixed_own, mixed_other, sums_chip, sums_distant = refs[5:9]
+    out_own, out_other, give, keep = refs[9:]
+    half = grads[0].shape[0]
+    rows = 2 * half
+    lanes = 2 * DH
+    first = pair * lanes
+    scale = jnp.asarray(DH ** (-0.5), BF16)
+    grad_rows = jnp.concatenate([ref[...] for ref in grads], axis=0)
+    wide = nt(grad_rows, w_out[first : first + lanes, :]).astype(BF16)
+    hidden_sums = sums_chip[0:1, :] + sums_distant[0:1, :]
+    totals = []
+    images = ((qkv_own, probs_own, out_own), (qkv_other, probs_other, out_other))
+    for image, (qkv, probs, out) in enumerate(images):
+        dq, dk, dv = [], [], []
+        for h in range(2):
+            at = first + h * DH
+            q = qkv[:, at : at + DH] * scale
+            k = qkv[:, 4 * DH + at : 4 * DH + at + DH] * scale
+            v = qkv[:, 8 * DH + at : 8 * DH + at + DH]
+            g = wide[image * rows : (image + 1) * rows, h * DH : (h + 1) * DH]
+            found = probs[2 * pair + h]
+            grad_probs = nt(v, g)
+            scores = found.astype(F32)
+            product = scores * grad_probs
+            inner = jnp.sum(product, axis=0, keepdims=True)
+            grad_scores = (product - scores * inner).astype(BF16)
+            dv.append(nn(found, g))
+            dk.append(nn(grad_scores, q))
+            dq.append(tn(k, grad_scores))
+        query = jnp.concatenate(dq, axis=0).T.astype(BF16)
+        value = jnp.concatenate(dv, axis=1).astype(BF16)
+        out[:, :lanes] = query
+        out[:, lanes : 2 * lanes] = jnp.concatenate(dk, axis=1).astype(BF16)
+        out[:, 2 * lanes :] = value
+        totals.append(
+            [jnp.sum(v.astype(F32), axis=0, keepdims=True) for v in (query, value)]
+        )
+    query_sum, value_sum = (totals[0][i] + totals[1][i] for i in range(2))
+    stacked = jnp.concatenate([out_own[...], out_other[...]], axis=0)
+    grad_w = tn(stacked, jnp.concatenate([ref[...] for ref in normed], axis=0)).astype(BF16)
+    mixed = jnp.concatenate(
+        [ref[:, first : first + lanes] for ref in (mixed_own, mixed_other)], axis=0
+    )
+    grad_o = tn(mixed, grad_rows).astype(BF16)
+    size = 4 * PART + 16
+    quarter = hidden_sums.shape[1] // 8
+    width = give.shape[1]
+    for side, out in enumerate((keep, give)):
+        for i in range(2):
+            for m in range(4):
+                source = grad_o if m == 3 else grad_w
+                at = (0 if m == 3 else m * lanes) + i * DH + side * PART
+                out[i * size + m * PART : i * size + (m + 1) * PART, :] = source[at : at + PART]
+            at = i * DH + side * PART
+            block = (side * 4 + 2 * pair + i) * quarter
+            row = jnp.concatenate(
+                [
+                    query_sum[:, at : at + PART],
+                    value_sum[:, at : at + PART],
+                    jnp.zeros((1, DH), F32),
+                    hidden_sums[:, block : block + quarter],
+                    jnp.zeros((1, width - lanes - quarter), F32),
+                ],
+                axis=1,
+            )
+            out[i * size + 4 * PART : (i + 1) * size, :] = jnp.broadcast_to(row, (16, width)).astype(
+                BF16
+            )
+
+
+def entry_product_kernel(first_pair, second_pair, w_in, *outs):
+    lanes = 2 * DH
+    joined = jnp.concatenate(
+        [
+            ref[:, m * lanes : (m + 1) * lanes]
+            for m in range(3)
+            for ref in (first_pair, second_pair)
+        ],
+        axis=1,
+    )
+    found = nn(joined, w_in[...]).astype(BF16)
+    at = 0
+    for out in outs:
+        out[...] = found[at : at + out.shape[0]]
+        at += out.shape[0]
+
+
+def entry_back_kernel(
+    rows,
+    valid,
+    partial,
+    from_core,
+    from_y,
+    stream,
+    grad_middle,
+    gain_vector,
+    middle_sums,
+    grad,
+    heads,
+    small,
+):
+    width = stream.shape[1]
+    gain = row_of(gain_vector)
+    totals = [jnp.zeros((8, width), F32) for _ in range(2)]
+    for at in chunks(stream.shape[0]):
+        found = partial[at, :].astype(F32) + from_core[at, :].astype(F32)
+        found = found + from_y[at, :].astype(F32)
+        hat, inverse = moment_norm(stream[at, :].astype(F32))
+        grad[at, :] = grad_middle[at, :] + norm_back(found, hat, inverse, gain)
+        for i, v in enumerate((found * hat, found)):
+            totals[i] = totals[i] + folded(v)
+    heads[...] = grad[0:8, :]
+    small[...] = jnp.concatenate(
+        [middle_sums[0:2, :]]
+        + [jnp.sum(v, axis=0, keepdims=True) for v in totals]
+        + [middle_sums[2:4, :], middle_sums[6:8, :]],
+        axis=0,
+    )
+
+
+def exit_kernel(output, grad, after, output_rows, grad_rows, ext):
+    _, _, z, y = coordinates()
+    half = output.shape[0]
+    rows = output_rows.shape[0]
+    count = rows - y
+    index = lax.broadcasted_iota(jnp.int32, (half, 1), 0)
+    ext[8:, :] = jnp.zeros((half - 8, ext.shape[1]), F32)
+    for values, at, out in ((output, 0, output_rows), (grad, 8, grad_rows)):
+        ext[0:8, :] = after[at : at + 8, :]
+        moved = pltpu.roll(values[...], half - z, 0)
+        beyond = pltpu.roll(ext[...], count - z, 0)
+        out[...] = jnp.where(index < count - z, moved, beyond)[:rows]
+
+
+def attention_gradients_kernel(own, across, core, core_across, *outs):
+    x, c, _, _ = coordinates()
+    query, value, hidden = outs[4:]
+    pieces = ((own, c, x), (across, c, 1 - x), (core, 1 - c, x), (core_across, 1 - c, 1 - x))
+    for ref, c_of, x_of in pieces:
+        at = pl.multiple_of(c_of * DH + x_of * PART, PART)
+        for m in range(4):
+            outs[m][pl.ds(at, PART), :] = ref[m * PART : (m + 1) * PART, :].astype(F32)
+    rows = [ref[4 * PART :, :].astype(F32)[0:1] for ref, _, _ in pieces]
+    natural = []
+    for c_of in range(2):
+        for x_of in range(2):
+            same = jnp.where(x == x_of, rows[0], rows[1])
+            changed = jnp.where(x == x_of, rows[2], rows[3])
+            natural.append(jnp.where(c == c_of, same, changed))
+    quarter = hidden.shape[0] // 4
+    for out, at, size in ((query, 0, PART), (value, PART, PART), (hidden, 2 * DH, quarter)):
+        found = jnp.concatenate([row[:, at : at + size] for row in natural], axis=1)
+        out[...] = found.reshape(out.shape)
+
+
+def mlp_in_gradient_kernel(own, across, core, core_across, out):
+    x, c, _, _ = coordinates()
+    pieces = ((own, c, x), (across, c, 1 - x), (core, 1 - c, x), (core_across, 1 - c, 1 - x))
+    for ref, c_of, x_of in pieces:
+        quarter = ref.shape[0]
+        at = pl.multiple_of((2 * c_of + x_of) * quarter, quarter)
+        out[:, pl.ds(at, quarter)] = ref[...].astype(F32).T
+
+
+def swapped_sum_kernel(own, received, out):
+    size = own.shape[0] // 2
+    out[:size, :] = (own[:size, :].astype(F32) + received[size:, :].astype(F32)).astype(BF16)
+    out[size:, :] = (own[size:, :].astype(F32) + received[:size, :].astype(F32)).astype(BF16)
+
+
+def mlp_out_gradient_kernel(own, core, out):
+    x, c, _, _ = coordinates()
+    for ref, c_of in ((own, c), (core, 1 - c)):
+        quarter = ref.shape[0] // 2
+        for i, side in enumerate((x, 1 - x)):
+            at = pl.multiple_of((2 * c_of + side) * quarter, quarter)
+            out[pl.ds(at, quarter), :] = ref[i * quarter : (i + 1) * quarter, :].astype(F32)
+
+
+def sums_kernel(small, received, *outs):
+    found = small[...] + received[...]
+    for i, out in enumerate(outs[:-1]):
+        out[...] = found[i : i + 1].reshape(out.shape)
+    outs[-1][...] = found[6:7, : outs[-1].shape[0]].reshape(outs[-1].shape)
+
+
+def copy_kernel(source, target):
+    target[...] = source[...]
+
+
+def add_wide_kernel(first, second, out):
+    out[...] = first[...] + second[...]
+
+
+def add_split_last_kernel(keep, received, last, zero, one):
+    size = zero.shape[0]
+    zero[...] = (keep[:size, :].astype(F32) + received[:size, :].astype(F32)).astype(BF16)
+    found = keep[size:, :].astype(F32) + received[size:, :].astype(F32)
+    one[...] = (found + last[...].astype(F32)).astype(BF16)
+
+
+def add_three_kernel(first, second, third, out):
+    out[...] = (
+        first[...].astype(F32) + second[...].astype(F32) + third[...].astype(F32)
+    ).astype(BF16)
+
+
+def on_device(
+    inputs,
+    valid,
+    cotangent,
+    w_query,
+    w_key,
+    w_value,
+    b_query,
+    b_value,
+    w_attn_out,
+    b_attn_out,
+    w_mlp_in,
+    b_mlp_in,
+    w_mlp_out,
+    b_mlp_out,
+    attention_norm_gain,
+    attention_norm_shift,
+    feedforward_norm_gain,
+    feedforward_norm_shift,
+):
+    rows, width = inputs.shape
+    images = valid.shape[0]
+    heads_local = w_query.shape[0] // DH
+    hidden_local = w_mlp_out.shape[0]
+    shape = (lax.axis_size("tok"), lax.axis_size("feat"), images, heads_local, hidden_local, width)
+    if shape != (4, 8, 4, 2, 512, 1024) or 2 * rows != SEQ + 1:
+        return on_device_general(
+            inputs,
+            valid,
+            cotangent,
+            w_query,
+            w_key,
+            w_value,
+            b_query,
+            b_value,
+            w_attn_out,
+            b_attn_out,
+            w_mlp_in,
+            b_mlp_in,
+            w_mlp_out,
+            b_mlp_out,
+            attention_norm_gain,
+            attention_norm_shift,
+            feedforward_norm_gain,
+            feedforward_norm_shift,
+        )
+    half = (rows + 15) // 16 * 16
+    image = 2 * half
+    quarter = hidden_local // 4
+    piece = 4 * PART + 16
+    row_block = (half, width)
+    low_rows, wide_rows = (row_block, BF16), (row_block, F32)
+    last = ()
+
+    def call(body, operands, outs, scratch=(), gate=(), specs=None):
+        nonlocal last
+        specs = [VMEM] * len(operands) if specs is None else specs
+        found = kernel_call(body, operands, specs, outs, scratch, last + tuple(gate))
+        last = (min(found, key=lambda v: v.size * v.dtype.itemsize),)
+        return found
+
+    def pin(values, gate=()):
+        return call(copy_kernel, (values,), [(values.shape, values.dtype)], gate=gate)[0]
+
+    def far_sum(values, received, gate=()):
+        return call(far_sum_kernel, (values, received), [low_rows], gate=gate)[0]
+
+    def split(values, received, sizes, gate=()):
+        outs = [((size, width), BF16) for size in sizes]
+        return call(add_split_kernel, (values, received), outs, gate=gate)
+
+    def add_last(values, one, three, gate=()):
+        return call(add_three_kernel, (values, one, three), [(values.shape, BF16)], gate=gate)[0]
+
+    in_hbm = [
+        pltpu.with_memory_space_constraint(w, pltpu.HBM)
+        for w in (w_query, w_key, w_value, w_attn_out, b_query, b_value, b_mlp_in)
+    ]
+    attn_own, attn_other, attn_both = call(
+        attention_weights_kernel,
+        in_hbm,
+        [((piece, width), BF16)] * 2 + [((2 * piece, width), BF16)],
+        scratch=[
+            pltpu.VMEM((2 * DH,), BF16),
+            pltpu.VMEM((2 * DH,), BF16),
+            pltpu.VMEM((hidden_local,), BF16),
+            pltpu.SemaphoreType.DMA((19,)),
+        ],
+        specs=[HBM] * 7,
+    )
+    own_one = send(attn_own, UP_Z)
+    attn_three = send(attn_both, DOWN_Z)
+    (edge,) = call(edge_kernel, (inputs, cotangent), [((16, width), BF16)])
+    edge = send(edge, NEXT)
+    mlp_own, mlp_other, mlp_both = call(
+        mlp_weights_kernel,
+        (w_mlp_in, w_mlp_out),
+        [((2 * quarter, width), BF16)] * 2 + [((4 * quarter, width), BF16)],
+    )
+    stream, normed, branch_grad, branch_again = call(
+        entry_kernel,
+        (valid, inputs, cotangent, edge, attention_norm_gain, attention_norm_shift),
+        [low_rows] * 4,
+        scratch=[pltpu.VMEM((half + 8, width), F32)],
+        gate=(own_one,),
+        specs=[SMEM] + [VMEM] * 5,
+    )
+    own_two = send(own_one, UP_Z)
+    other_one = send(own_one, SWAP_X)
+    normed_y, normed_c = send(normed, SWAP_Y), send(normed, SWAP_C)
+    mlp_first = pin(mlp_own, (attn_three, normed_c))
+    mlp_one = send(mlp_first, UP_Z)
+    pin(edge, (own_two, other_one))
+    other_two = send(own_two, SWAP_X)
+    branch_again = pin(branch_again, (normed_y,))
+    normed_yc = send(normed_y, SWAP_C)
+    branch_y, branch_c = send(branch_again, SWAP_Y), send(branch_again, SWAP_C)
+    attn_pieces = (attn_own, attn_other, own_one, other_one, attn_three, own_two, other_two)
+
+    head_out = [
+        ((image, 12 * DH), BF16),
+        ((4, image, image), BF16),
+        ((image, 4 * DH), BF16),
+    ]
+    qkv_other, probs_other, mixed_other, partial_other, w_heads, w_out, head_bias = call(
+        functools.partial(first_forward_kernel, rows),
+        (normed_c, normed_yc) + attn_pieces,
+        head_out
+        + [((image, width), BF16)]
+        + [((12 * DH, width), BF16), ((4 * DH, width), BF16), ((8, 12 * DH), F32)],
+        gate=(branch_c,),
+    )
+    from_core = send(partial_other, SWAP_C)
+    mlp_both = pin(mlp_both, (mlp_one,))
+    mlp_three = send(mlp_both, DOWN_Z)
+    mlp_two = send(mlp_one, UP_Z)
+    mlp_other_one = send(mlp_one, SWAP_X)
+    qkv_own, probs_own, mixed_own, partial_near, partial_far = call(
+        functools.partial(second_forward_kernel, rows),
+        (normed, normed_y, w_heads, w_out, head_bias),
+        head_out + [low_rows] * 2,
+    )
+    attn_far = far_sum(partial_far, from_core, (branch_y,))
+    from_y = send(attn_far, SWAP_Y)
+    branch_yc = send(branch_y, SWAP_C)
+    middle, normed_middle, attn_power = call(
+        functools.partial(middle_kernel, rows),
+        (valid, partial_near, from_core, from_y, stream)
+        + (b_attn_out, feedforward_norm_gain, feedforward_norm_shift),
+        [wide_rows, low_rows, ((8, width), F32)],
+        gate=(mlp_other_one, branch_yc),
+        specs=[SMEM] + [VMEM] * 7,
+    )
+    middle_y, middle_c = send(normed_middle, SWAP_Y), send(normed_middle, SWAP_C)
+    pin(attn_power, (mlp_two, middle_c))
+    mlp_other_two = send(mlp_two, SWAP_X)
+
+    middle_yc = send(middle_y, SWAP_C)
+    pieces = (mlp_own, mlp_other, mlp_one, mlp_other_one, mlp_three, mlp_two, mlp_other_two)
+    pieces += (attn_own, own_one, attn_three, own_two)
+    mlp_out = (
+        [((image, 8 * quarter), BF16)] * 2 + [low_rows] * 4 + [((8, 8 * quarter), F32)]
+    )
+    chip = call(
+        mlp_kernel,
+        (normed_middle, middle_c, branch_grad, branch_c) + pieces,
+        mlp_out,
+        gate=(middle_y,),
+    )
+    mid_core, out_core = send(chip[3], SWAP_C), send(chip[5], SWAP_C)
+    distant = call(mlp_kernel, (middle_y, middle_yc, branch_y, branch_yc) + pieces, mlp_out)
+    out_distant = send(distant[5], SWAP_C)
+    mid_far = far_sum(distant[2], send(distant[3], SWAP_C), (mid_core, out_core))
+    mid_y = send(mid_far, SWAP_Y)
+
+    grad_out = call(
+        functools.partial(products_kernel, True),
+        (chip[0], distant[0], branch_grad, branch_c, branch_y, branch_yc),
+        [((2 * quarter, width), BF16)] * 4,
+        gate=(out_distant,),
+    )
+    grad_out = dict(zip(SLOTS, grad_out))
+    out_two = send(grad_out[2], DOWN_Z)
+    out_three = send(grad_out[3], UP_Z)
+    grad_in_keep, grad_in_give = call(
+        functools.partial(products_kernel, False),
+        (chip[1], distant[1], normed_middle, middle_c, middle_y, middle_yc),
+        [((4 * quarter, width), BF16)] * 2,
+    )
+    in_received = send(grad_in_give, SWAP_X)
+    grad_middle, grad_attn, middle_sums = call(
+        middle_back_kernel,
+        (chip[2], mid_core, mid_y, middle, branch_grad, feedforward_norm_gain),
+        [wide_rows, low_rows, ((8, width), F32)],
+    )
+    grad_y, grad_c = send(grad_attn, SWAP_Y), send(grad_attn, SWAP_C)
+    out_far = far_sum(distant[4], out_distant)
+    (one,) = split(grad_out[1], out_two, (2 * quarter,), (grad_c,))
+    out_one = send(one, DOWN_Z)
+    grad_yc = send(grad_y, SWAP_C)
+
+    def backward(p, gate=()):
+        return call(
+            functools.partial(backward_kernel, p),
+            (grad_attn, grad_y, grad_c, grad_yc, normed, normed_y, normed_c, normed_yc)
+            + (w_out, qkv_own, qkv_other, probs_own, probs_other)
+            + (mixed_own, mixed_other, chip[6], distant[6]),
+            [((image, 6 * DH), BF16)] * 2 + [((2 * piece, width), BF16)] * 2,
+            gate=gate,
+        )
+
+    second_own, second_other, give, keep = backward(1, (out_three,))
+    received = send(give, SWAP_X)
+    out_y = send(pin(out_far, (out_one,)), SWAP_Y)
+    in_pieces = split(grad_in_keep, in_received, (quarter,) * 4)
+    in_pieces = dict(zip(SLOTS, in_pieces))
+    in_two = send(in_pieces[2], DOWN_Z)
+    in_three = send(in_pieces[3], UP_Z)
+    first_own, first_other, give_first, keep_first = backward(0)
+    received_first = send(give_first, SWAP_X)
+    (one,) = split(in_pieces[1], in_two, (quarter,), (out_y,))
+    in_one = send(one, DOWN_Z)
+    (entry_other,) = call(
+        entry_product_kernel, (first_other, second_other, w_heads), [((image, width), BF16)]
+    )
+    entry_core = send(entry_other, SWAP_C)
+    three, two = split(keep, received, (piece,) * 2, (in_three,))
+    attn_two = send(two, DOWN_Z)
+    attn_three = send(three, UP_Z)
+    entry_near, entry_far = call(
+        entry_product_kernel, (first_own, second_own, w_heads), [low_rows] * 2
+    )
+    entry_far = far_sum(entry_far, entry_core, (in_one,))
+    entry_y = send(entry_far, SWAP_Y)
+    output, output_heads, power_sums = call(
+        functools.partial(output_kernel, rows),
+        (valid, chip[4], out_core, out_y, middle, stream, b_mlp_out, attn_power, middle_sums),
+        [wide_rows, ((8, width), F32), ((8, width), F32)],
+        specs=[SMEM] + [VMEM] * 8,
+    )
+    out_total = call(
+        add_three_kernel,
+        (grad_out[0], out_one, out_three),
+        [((2 * quarter, width), BF16)],
+        gate=(received_first,),
+    )[0]
+    out_across = send(out_total, SWAP_X)
+    zero, one = call(
+        add_split_last_kernel,
+        (keep_first, received_first, attn_two),
+        [((piece, width), BF16)] * 2,
+    )
+    attn_one = send(one, DOWN_Z)
+    in_total = add_last(in_pieces[0], in_one, in_three)
+    gradient, heads, small = call(
+        functools.partial(entry_back_kernel, rows),
+        (valid, entry_near, entry_core, entry_y, stream, grad_middle)
+        + (attention_norm_gain, power_sums),
+        [wide_rows, ((8, width), F32), ((8, width), F32)],
+        gate=(attn_three,),
+        specs=[SMEM] + [VMEM] * 7,
+    )
+
+    def add_small(received, gate=()):
+        return call(add_wide_kernel, (small, received), [(small.shape, F32)], gate=gate)[0]
+
+    in_across, in_core = send(in_total, SWAP_X), send(in_total, SWAP_C)
+    heads_after = send(jnp.concatenate([output_heads, heads]), PREVIOUS)
+    small = add_small(send(small, SWAP_C), (in_core,))
+    small_y = send(small, SWAP_Y)
+    (out_whole,) = call(
+        swapped_sum_kernel, (out_total, out_across), [((2 * quarter, width), BF16)]
+    )
+    out_core = send(out_whole, SWAP_C)
+    attn_total = add_last(zero, attn_one, attn_three, (heads_after,))
+    attn_across, attn_core = send(attn_total, SWAP_X), send(attn_total, SWAP_C)
+    small = add_small(small_y, (out_core, attn_core))
+    small_z = send(small, FLIP_Z[1])
+    output_rows, gradient_rows = call(
+        exit_kernel,
+        (output, gradient, heads_after),
+        [((rows, width), F32)] * 2,
+        scratch=[pltpu.VMEM((half, width), F32)],
+    )
+    small = add_small(small_z, (in_across,))
+    small_z = send(small, FLIP_Z[2])
+    in_last = send(in_across, SWAP_C)
+    (grad_w_mlp_out,) = call(
+        mlp_out_gradient_kernel, (out_whole, out_core), [((hidden_local, width), F32)]
+    )
+    small = add_small(small_z, (attn_across,))
+    small_x = send(small, SWAP_X)
+    attn_last = send(attn_across, SWAP_C)
+    (grad_w_mlp_in,) = call(
+        mlp_in_gradient_kernel,
+        (in_total, in_across, in_core, in_last),
+        [((width, hidden_local), F32)],
+    )
+    attn_grads = call(
+        attention_gradients_kernel,
+        (attn_total, attn_across, attn_core, attn_last),
+        [((2 * DH, width), F32)] * 4
+        + [((2 * DH,), F32), ((2 * DH,), F32), ((hidden_local,), F32)],
+    )
+    *vectors, powers = call(
+        sums_kernel, (small, small_x), [((width,), F32)] * 6 + [((2 * DH,), F32)]
+    )
+    stream_rms = jnp.sqrt(powers[:4] / (jnp.maximum(powers[4], 1.0) * D))
+    return (
+        output_rows,
+        gradient_rows,
+        attn_grads[0],
+        attn_grads[1],
+        attn_grads[2],
+        attn_grads[4],
+        attn_grads[5],
+        attn_grads[3],
+        vectors[0],
+        grad_w_mlp_in,
+        attn_grads[6],
+        grad_w_mlp_out,
+        vectors[1],
+        vectors[2],
+        vectors[3],
+        vectors[4],
+        vectors[5],
+        stream_rms,
+    )
+
+
 def solution(mesh):
     in_specs = (
         P(("tok", "feat"), None),

time: 1230 us -> 279 us (0.23)
  blocking collectives: 681 us -> 0 us
  local copies, waits for them, and re-layouts: 146 us -> 5.98 us
  waiting for transfers between devices: 239 us -> 131 us
  matrix products: 80 us -> 0 us
  Pallas kernels: 0 us -> 70 us
  starting transfers between devices: 18.7 us -> 66 us
  other arithmetic: 35.5 us -> 0.53 us
  between operations: 16.8 us -> 2.19 us
    unnamed x4 -> x0, blocking collectives: 638 us -> none
    all_gather x5 -> x0, waiting for transfers between devices: 231 us -> none  [the longest x1 83.8 us: on_device(): lax.all_gather(grad_attn, 'feat', axis=0, tiled=True)[:group_rows]]
    ppermute x0 -> x59, waiting for transfers between devices: none -> 131 us  [send(): return lax.ppermute(values, AXES, pairs)]
    dot_general x40 -> x0, matrix products: 80 us -> none  [the longest x4 11.2 us: image_backward(): jnp.einsum('qhd,khd->hqk', grad_heads, value_heads, preferred_element_typ...]
    pallas_call x0 -> x46, Pallas kernels: none -> 70 us  [kernel_call(): pl.pallas_call(kernel, in_specs=list(specs) + [VMEM] * extra, out_specs=[...]
    ppermute x0 -> x59, starting transfers between devices: none -> 66 us  [send(): return lax.ppermute(values, AXES, pairs)]
    unnamed x110 -> x46, local copies, waits for them, and re-layouts: 65.4 us -> 5.4 us
    psum x1 -> x0, blocking collectives: 43 us -> none  [on_device(): lax.psum((grad_b_attn_out, grad_b_mlp_out, attention_gain_gradient, grad_...]
  transfers between devices with their start and end apart: 10 -> 59, of which waited for: 5 -> 24; matrix products, arithmetic and copies ran while one was open for 42% -> 0% of each run, Pallas kernels for 0% -> 23%
where the time goes in v2:
time: 279 us; the launch traced here: 276 us
  waiting for transfers between devices  131 us (47%)
  Pallas kernels  70 us (25%)
  starting transfers between devices  66 us (24%)
  local copies, waits for them, and re-layouts  5.98 us (2%)
    ppermute x59, waiting for transfers between devices, send(): return lax.ppermute(values, AXES, pairs)  131 us
    pallas_call x46, Pallas kernels, kernel_call(): pl.pallas_call(kernel, in_specs=list(specs) + [VMEM] * extra, out_specs=[...  70 us
    ppermute x59, starting transfers between devices, send(): return lax.ppermute(values, AXES, pairs)  66 us
  transfers between devices with their start and end apart: 59, of which 24 were waited for; matrix products, arithmetic and copies ran while one was open for 0% of the time, Pallas kernels for 23%

profile of v2, /device:TPU:0, one launch (start us, length us, event | category | flops | bytes accessed | tf_op | source)
XLA Modules:
  0.0 275.8 jit_solution(10128298489527208832)
XLA Ops:
  2.2 3.1 %collective-permute-start.1 = (bf16[144,1024]{1,0:T(8,128)(2,1)S(1)}, bf16[144,1024]{1,0:T(8,128)(2,1)S(1)}, u32[]{:S(2)}, u32[]{:S(2)}) collective-permute-start(bf16[144,1024]{1,0:T(8,128)(2,1)S(1)} %get-tuple-element.106.refs_2_.refs_11_), channel_id=1, source_target_pairs={{0,2},{1,3},{2,4},{3,5},{4,6},{5,7},{6,0},{7,1},{8,10},{9,11},{10,... | collective-permute-start | bytes 884744 | tf_op jit(solution)/shard_map/ppermute | solution.py:355
  5.4 3.6 %collective-permute-start = (bf16[16,1024]{1,0:T(8,128)(2,1)S(1)}, bf16[16,1024]{1,0:T(8,128)(2,1)S(1)}, u32[]{:S(2)}, u32[]{:S(2)}) collective-permute-start(bf16[16,1024]{1,0:T(8,128)(2,1)S(1)} %shard_map.314.refs_2_), channel_id=1, source_target_pairs={{0,1},{1,2},{2,3},{3,4},{4,5},{5,6},{6,7},{8,9},{9,10},{10,11},{11... | collective-permute-start | bytes 98312 | tf_op jit(solution)/shard_map/ppermute | solution.py:355
  10.5 3.8 %collective-permute-done.1.refs_7_.refs_4_.refs_12_ = bf16[144,1024]{1,0:T(8,128)(2,1)S(1)} collective-permute-done((bf16[144,1024]{1,0:T(8,128)(2,1)S(1)}, bf16[144,1024]{1,0:T(8,128)(2,1)S(1)}, u32[]{:S(2)}, u32[]{:S(2)}) %collective-permute-start.1) | collective-permute-done | bytes 294944 | tf_op jit(solution)/shard_map/ppermute | solution.py:355
  16.2 3.5 %collective-permute-start.6 = (bf16[288,1024]{1,0:T(8,128)(2,1)S(1)}, bf16[288,1024]{1,0:T(8,128)(2,1)S(1)}, u32[]{:S(2)}, u32[]{:S(2)}) collective-permute-start(bf16[288,1024]{1,0:T(8,128)(2,1)S(1)} %get-tuple-element.110), channel_id=1, source_target_pairs={{0,6},{1,7},{2,0},{3,1},{4,2},{5,3},{6,4},{7,5},{8,14},{9,15},{10,... | collective-permute-start | bytes 1769480 | tf_op jit(solution)/shard_map/ppermute | solution.py:355
  21.3 12.0 %collective-permute-done.6.refs_2_.refs_6_.refs_13_ = bf16[288,1024]{1,0:T(8,128)(2,1)S(1)} collective-permute-done((bf16[288,1024]{1,0:T(8,128)(2,1)S(1)}, bf16[288,1024]{1,0:T(8,128)(2,1)S(1)}, u32[]{:S(2)}, u32[]{:S(2)}) %collective-permute-start.6) | collective-permute-done | bytes 589856 | tf_op jit(solution)/shard_map/ppermute | solution.py:355
  33.4 6.7 %collective-permute-done.7.refs_2_.refs_7_.refs_14_ = bf16[144,1024]{1,0:T(8,128)(2,1)S(1)} collective-permute-done((bf16[144,1024]{1,0:T(8,128)(2,1)S(1)}, bf16[144,1024]{1,0:T(8,128)(2,1)S(1)}, u32[]{:S(2)}, u32[]{:S(2)}) %collective-permute-start.7) | collective-permute-done | bytes 294944 | tf_op jit(solution)/shard_map/ppermute | solution.py:355
  44.1 5.5 %collective-permute-done.8.refs_8_ = bf16[144,1024]{1,0:T(8,128)(2,1)S(1)} collective-permute-done((bf16[144,1024]{1,0:T(8,128)(2,1)S(1)}, bf16[144,1024]{1,0:T(8,128)(2,1)S(1)}, u32[]{:S(2)}, u32[]{:S(2)}) %collective-permute-start.8) | collective-permute-done | bytes 294944 | tf_op jit(solution)/shard_map/ppermute | solution.py:355
  49.7 5.0 %shard_map.320 = (bf16[608,768]{1,0:T(8,128)(2,1)S(1)}, bf16[4,608,608]{2,1,0:T(8,128)(2,1)S(1)}, bf16[608,256]{1,0:T(8,128)(2,1)S(1)}, bf16[608,1024]{1,0:T(8,1...) custom-call(bf16[304,1024]{1,0:T(8,128)(2,1)S(1)} %collective-permute-done.3.refs_3, ...), custom_call_target="tpu_custom_call" | custom-call | flops 10000000000 | bytes 65536 | tf_op jit(solution)/shard_map/pallas_call | solution.py:381
  54.8 4.6 %collective-permute-done.12.refs_3_.refs_2_.refs_4_ = bf16[304,1024]{1,0:T(8,128)(2,1)S(1)} collective-permute-done((bf16[304,1024]{1,0:T(8,128)(2,1)S(1)}, bf16[304,1024]{1,0:T(8,128)(2,1)S(1)}, u32[]{:S(2)}, u32[]{:S(2)}) %collective-permute-start.12) | collective-permute-done | bytes 622624 | tf_op jit(solution)/shard_map/ppermute | solution.py:355
  59.5 5.1 %shard_map.322 = (bf16[608,768]{1,0:T(8,128)(2,1)S(1)}, bf16[4,608,608]{2,1,0:T(8,128)(2,1)S(1)}, bf16[608,256]{1,0:T(8,128)(2,1)S(1)}, bf16[304,1024]{1,0:T(8,128)(2,1)S(1)}, bf16[304,1024]{1,0:T(8,128)(2,1)S(1)}) custom-call(bf16[304,1024]{1,0:T(8,128)(2,1)S(1)} %get-tuple-element.108.refs_0_.refs_4_, ...), custom_call_target="tpu_custom_call" | custom-call | flops 10000000000 | bytes 65536 | tf_op jit(solution)/shard_map/pallas_call | solution.py:381
  65.6 13.6 %collective-permute-done.14.refs_9_.refs_7_ = bf16[256,1024]{1,0:T(8,128)(2,1)S(1)} collective-permute-done((bf16[256,1024]{1,0:T(8,128)(2,1)S(1)}, bf16[256,1024]{1,0:T(8,128)(2,1)S(1)}, u32[]{:S(2)}, u32[]{:S(2)}) %collective-permute-start.14) | collective-permute-done | bytes 524320 | tf_op jit(solution)/shard_map/ppermute | solution.py:355
  84.2 3.1 %collective-permute-start.17 = (bf16[512,1024]{1,0:T(8,128)(2,1)S(1)}, bf16[512,1024]{1,0:T(8,128)(2,1)S(1)}, u32[]{:S(2)}, u32[]{:S(2)}) collective-permute-start(bf16[512,1024]{1,0:T(8,128)(2,1)S(1)} %shard_map.321.refs_5_), channel_id=1, source_target_pairs={{0,6},{1,7},{2,0},{3,1},{4,2},{5,3},{6,4},{7,5},{8,14},{9,15},{10,... | collective-permute-start | bytes 3145736 | tf_op jit(solution)/shard_map/ppermute | solution.py:355
  87.3 12.4 %collective-permute-done.18.refs_2_.refs_9_ = bf16[256,1024]{1,0:T(8,128)(2,1)S(1)} collective-permute-done((bf16[256,1024]{1,0:T(8,128)(2,1)S(1)}, bf16[256,1024]{1,0:T(8,128)(2,1)S(1)}, u32[]{:S(2)}, u32[]{:S(2)}) %collective-permute-start.18) | collective-permute-done | bytes 524320 | tf_op jit(solution)/shard_map/ppermute | solution.py:355
  100.2 12.6 %collective-permute-done.19.refs_10_ = bf16[256,1024]{1,0:T(8,128)(2,1)S(1)} collective-permute-done((bf16[256,1024]{1,0:T(8,128)(2,1)S(1)}, bf16[256,1024]{1,0:T(8,128)(2,1)S(1)}, u32[]{:S(2)}, u32[]{:S(2)}) %collective-permute-start.19) | collective-permute-done | bytes 524320 | tf_op jit(solution)/shard_map/ppermute | solution.py:355
  112.8 8.3 %collective-permute-done.17.refs_8_ = bf16[512,1024]{1,0:T(8,128)(2,1)S(1)} collective-permute-done((bf16[512,1024]{1,0:T(8,128)(2,1)S(1)}, bf16[512,1024]{1,0:T(8,128)(2,1)S(1)}, u32[]{:S(2)}, u32[]{:S(2)}) %collective-permute-start.17) | collective-permute-done | bytes 1048608 | tf_op jit(solution)/shard_map/ppermute | solution.py:355
  121.1 5.7 %shard_map.326 = (bf16[608,1024]{1,0:T(8,128)(2,1)S(1)}, bf16[608,1024]{1,0:T(8,128)(2,1)S(1)}, bf16[304,1024]{1,0:T(8,128)(2,1)S(1)}, bf16[304,1024]{1,0:T(8,12...) custom-call(bf16[304,1024]{1,0:T(8,128)(2,1)S(1)} %get-tuple-element.121.refs_0_.re, ...), custom_call_target="tpu_custom_call" | custom-call | flops 10000000000 | bytes 65536 | tf_op jit(solution)/shard_map/pallas_call | solution.py:381
  127.4 5.7 %shard_map.327 = (bf16[608,1024]{1,0:T(8,128)(2,1)S(1)}, bf16[608,1024]{1,0:T(8,128)(2,1)S(1)}, bf16[304,1024]{1,0:T(8,128)(2,1)S(1)}, bf16[304,1024]{1,0:T(8,12...) custom-call(bf16[304,1024]{1,0:T(8,128)(2,1)S(1)} %collective-permute-done.20.refs_, ...), custom_call_target="tpu_custom_call" | custom-call | flops 10000000000 | bytes 65536 | tf_op jit(solution)/shard_map/pallas_call | solution.py:381
  136.4 5.3 %shard_map.329 = (bf16[256,1024]{1,0:T(8,128)(2,1)S(1)}, bf16[256,1024]{1,0:T(8,128)(2,1)S(1)}, bf16[256,1024]{1,0:T(8,128)(2,1)S(1)}, bf16[256,1024]{1,0:T(8,128)(2,1)S(1)}) custom-call(bf16[608,1024]{1,0:T(8,128)(2,1)S(1)} %get-tuple-element.138.refs_0_, bf16[608,1024]{1,0:T(8,128)(2,1)S(1)} %get-tuple-element.139.refs_1_, ...), custom_call_target="tpu_custom_call" | custom-call | flops 10000000000 | bytes 65536 | tf_op jit(solution)/shard_map/pallas_call | solution.py:381
  143.8 5.1 %shard_map.330 = (bf16[512,1024]{1,0:T(8,128)(2,1)S(1)}, bf16[512,1024]{1,0:T(8,128)(2,1)S(1)}) custom-call(bf16[608,1024]{1,0:T(8,128)(2,1)S(1)} %get-tuple-element.136.refs_0_, bf16[608,1024]{1,0:T(8,128)(2,1)S(1)} %get-tuple-element.137.refs_1_, bf16[304,1024]{1,0:T(8,128)(2,1)S(1)} %get-tuple-element.121.refs_0_.refs_2_, ...), custom_call_target="tpu_custom_call" | custom-call | flops 10000000000 | bytes 65536 | tf_op jit(solution)/shard_map/pallas_call | solution.py:381
  154.1 15.3 %collective-permute-done.27.refs_1_ = bf16[304,1024]{1,0:T(8,128)(2,1)S(1)} collective-permute-done((bf16[304,1024]{1,0:T(8,128)(2,1)S(1)}, bf16[304,1024]{1,0:T(8,128)(2,1)S(1)}, u32[]{:S(2)}, u32[]{:S(2)}) %collective-permute-start.27) | collective-permute-done | bytes 622624 | tf_op jit(solution)/shard_map/ppermute | solution.py:355
  169.5 7.3 %collective-permute-start.32 = (bf16[256,1024]{1,0:T(8,128)(2,1)S(1)}, bf16[256,1024]{1,0:T(8,128)(2,1)S(1)}, u32[]{:S(2)}, u32[]{:S(2)}) collective-permute-start(bf16[256,1024]{1,0:T(8,128)(2,1)S(1)} %shard_map.333.refs_17_), channel_id=1, source_target_pairs={{0,6},{1,7},{2,0},{3,1},{4,2},{5,3},{6,4},{7,5},{8,14},{9,15},{10,... | collective-permute-start | bytes 1572872 | tf_op jit(solution)/shard_map/ppermute | solution.py:355
  176.8 8.1 %shard_map.334 = (bf16[608,384]{1,0:T(8,128)(2,1)S(1)}, bf16[608,384]{1,0:T(8,128)(2,1)S(1)}, bf16[288,1024]{1,0:T(8,128)(2,1)S(1)}, bf16[288,1024]{1,0:T(8,128)(2,1)S(1)}) custom-call(bf16[304,1024]{1,0:T(8,128)(2,1)S(1)} %get-tuple-element.143.refs_0_, bf16[304,1024]{1,0:T(8,128)(2,1)S(1)} %collective-permute-done.27.refs_1_, ...), custom_call_target="tpu_custom_call" | custom-call | flops 10000000000 | bytes 65536 | tf_op jit(solution)/shard_map/pallas_call | solution.py:381
  184.9 3.7 %collective-permute-done.32.refs_2_.refs_1_ = bf16[256,1024]{1,0:T(8,128)(2,1)S(1)} collective-permute-done((bf16[256,1024]{1,0:T(8,128)(2,1)S(1)}, bf16[256,1024]{1,0:T(8,128)(2,1)S(1)}, u32[]{:S(2)}, u32[]{:S(2)}) %collective-permute-start.32) | collective-permute-done | bytes 524320 | tf_op jit(solution)/shard_map/ppermute | solution.py:355
  190.4 4.3 %collective-permute-start.36 = (bf16[128,1024]{1,0:T(8,128)(2,1)S(1)}, bf16[128,1024]{1,0:T(8,128)(2,1)S(1)}, u32[]{:S(2)}, u32[]{:S(2)}) collective-permute-start(bf16[128,1024]{1,0:T(8,128)(2,1)S(1)} %get-tuple-element.161), channel_id=1, source_target_pairs={{0,6},{1,7},{2,0},{3,1},{4,2},{5,3},{6,4},{7,5},{8,14},{9,15},{10,... | collective-permute-start | bytes 786440 | tf_op jit(solution)/shard_map/ppermute | solution.py:355
  196.5 8.1 %shard_map.337 = (bf16[608,384]{1,0:T(8,128)(2,1)S(1)}, bf16[608,384]{1,0:T(8,128)(2,1)S(1)}, bf16[288,1024]{1,0:T(8,128)(2,1)S(1)}, bf16[288,1024]{1,0:T(8,128)(2,1)S(1)}) custom-call(bf16[304,1024]{1,0:T(8,128)(2,1)S(1)} %get-tuple-element.143.refs_0_, bf16[304,1024]{1,0:T(8,128)(2,1)S(1)} %collective-permute-done.27.refs_1_, ...), custom_call_target="tpu_custom_call" | custom-call | flops 10000000000 | bytes 65536 | tf_op jit(solution)/shard_map/pallas_call | solution.py:381
  205.2 3.8 %collective-permute-start.39 = (bf16[128,1024]{1,0:T(8,128)(2,1)S(1)}, bf16[128,1024]{1,0:T(8,128)(2,1)S(1)}, u32[]{:S(2)}, u32[]{:S(2)}) collective-permute-start(bf16[128,1024]{1,0:T(8,128)(2,1)S(1)} %shard_map.338.refs_3_), channel_id=1, source_target_pairs={{0,6},{1,7},{2,0},{3,1},{4,2},{5,3},{6,4},{7,5},{8,14},{9,15},{10,... | collective-permute-start | bytes 786440 | tf_op jit(solution)/shard_map/ppermute | solution.py:355
  213.3 3.1 %collective-permute-start.42 = (bf16[144,1024]{1,0:T(8,128)(2,1)S(1)}, bf16[144,1024]{1,0:T(8,128)(2,1)S(1)}, u32[]{:S(2)}, u32[]{:S(2)}) collective-permute-start(bf16[144,1024]{1,0:T(8,128)(2,1)S(1)} %get-tuple-element.171), channel_id=1, source_target_pairs={{0,6},{1,7},{2,0},{3,1},{4,2},{5,3},{6,4},{7,5},{8,14},{9,15},{10,... | collective-permute-start | bytes 884744 | tf_op jit(solution)/shard_map/ppermute | solution.py:355
  218.9 3.1 %collective-permute-done.41.refs_4_.refs_1_ = bf16[288,1024]{1,0:T(8,128)(2,1)S(1)} collective-permute-done((bf16[288,1024]{1,0:T(8,128)(2,1)S(1)}, bf16[288,1024]{1,0:T(8,128)(2,1)S(1)}, u32[]{:S(2)}, u32[]{:S(2)}) %collective-permute-start.41) | collective-permute-done | bytes 589856 | tf_op jit(solution)/shard_map/ppermute | solution.py:355
  223.8 4.4 %collective-permute-done.42.refs_2_ = bf16[144,1024]{1,0:T(8,128)(2,1)S(1)} collective-permute-done((bf16[144,1024]{1,0:T(8,128)(2,1)S(1)}, bf16[144,1024]{1,0:T(8,128)(2,1)S(1)}, u32[]{:S(2)}, u32[]{:S(2)}) %collective-permute-start.42) | collective-permute-done | bytes 294944 | tf_op jit(solution)/shard_map/ppermute | solution.py:355
  235.6 2.4 collective-permute-done.48.refs_1_
  243.9 10.1 %collective-permute-done.54.refs_3_.refs_1_ = bf16[128,1024]{1,0:T(8,128)(2,1)S(1)} collective-permute-done((bf16[128,1024]{1,0:T(8,128)(2,1)S(1)}, bf16[128,1024]{1,0:T(8,128)(2,1)S(1)}, u32[]{:S(2)}, u32[]{:S(2)}) %collective-permute-start.54) | collective-permute-done | bytes 262176 | tf_op jit(solution)/shard_map/ppermute | solution.py:355
  254.7 3.1 %shard_map.352 = (f32[289,1024]{1,0:T(8,128)}, f32[289,1024]{1,0:T(8,128)}) custom-call(f32[304,1024]{1,0:T(8,128)S(1)} %get-tuple-element.166.refs_0_, f32[304,1024]{1,0:T(8,128)S(1)} %get-tuple-element.174.refs_1_, f32[16,1024]{1,0:T(8,128)S(1)} %collective-permute-done.44.refs_4_.refs_2_, f32[8,1024]{1,0:T(8,128)S(1)} %shard_map.351.refs_3_.refs_0_), custom_call_target="tpu_custom_call" | custom-call | flops 10000000000 | bytes 65536 | tf_op jit(solution)/shard_map/pallas_call | solution.py:381
  (181 shorter events, 72.1 us)
Async XLA Ops:
  16.1 17.2 %collective-permute-start.3 = (bf16[304,1024]{1,0:T(8,128)(2,1)S(1)}, bf16[304,1024]{1,0:T(8,128)(2,1)S(1)}, u32[]{:S(2)}, u32[]{:S(2)}) collective-permute-start(bf16[304,1024]{1,0:T(8,128)(2,1)S(1)} %get-tuple-element.108.refs_0_.refs_4_), channel_id=1, source_target_pairs={{0,8},{1,9},{2,10},{3,11},{4,12},{5,13},{6,14},{7,15},{8,0},{9,1},... | collective-permute-start | bytes 1867784 | tf_op jit(solution)/shard_map/ppermute | solution.py:355
  16.2 17.2 %collective-permute-start.6 = (bf16[288,1024]{1,0:T(8,128)(2,1)S(1)}, bf16[288,1024]{1,0:T(8,128)(2,1)S(1)}, u32[]{:S(2)}, u32[]{:S(2)}) collective-permute-start(bf16[288,1024]{1,0:T(8,128)(2,1)S(1)} %get-tuple-element.110), channel_id=1, source_target_pairs={{0,6},{1,7},{2,0},{3,1},{4,2},{5,3},{6,4},{7,5},{8,14},{9,15},{10,... | collective-permute-start | bytes 1769480 | tf_op jit(solution)/shard_map/ppermute | solution.py:355
  19.6 20.4 %collective-permute-start.2 = (bf16[304,1024]{1,0:T(8,128)(2,1)S(1)}, bf16[304,1024]{1,0:T(8,128)(2,1)S(1)}, u32[]{:S(2)}, u32[]{:S(2)}) collective-permute-start(bf16[304,1024]{1,0:T(8,128)(2,1)S(1)} %get-tuple-element.108.refs_0_.refs_4_), channel_id=1, source_target_pairs={{0,1},{1,0},{2,3},{3,2},{4,5},{5,4},{6,7},{7,6},{8,9},{9,8},{10,11... | collective-permute-start | bytes 1867784 | tf_op jit(solution)/shard_map/ppermute | solution.py:355
  19.8 20.2 %collective-permute-start.7 = (bf16[144,1024]{1,0:T(8,128)(2,1)S(1)}, bf16[144,1024]{1,0:T(8,128)(2,1)S(1)}, u32[]{:S(2)}, u32[]{:S(2)}) collective-permute-start(bf16[144,1024]{1,0:T(8,128)(2,1)S(1)} %collective-permute-done.1.refs_7_.refs_4_.refs_12_), channel_id=1, source_target_pairs={{0,2},{1,3},{2,4},{3,5},{4,6},{5,7},{6,0},{7,1},{8,10},{9,11},{10,... | collective-permute-start | bytes 884744 | tf_op jit(solution)/shard_map/ppermute | solution.py:355
  19.8 20.2 %collective-permute-start.5 = (bf16[144,1024]{1,0:T(8,128)(2,1)S(1)}, bf16[144,1024]{1,0:T(8,128)(2,1)S(1)}, u32[]{:S(2)}, u32[]{:S(2)}) collective-permute-start(bf16[144,1024]{1,0:T(8,128)(2,1)S(1)} %collective-permute-done.1.refs_7_.refs_4_.refs_12_), channel_id=1, source_target_pairs={{0,16},{1,17},{2,18},{3,19},{4,20},{5,21},{6,22},{7,23},{8,24},{9,... | collective-permute-start | bytes 884744 | tf_op jit(solution)/shard_map/ppermute | solution.py:355
  42.2 17.2 %collective-permute-start.10 = (bf16[256,1024]{1,0:T(8,128)(2,1)S(1)}, bf16[256,1024]{1,0:T(8,128)(2,1)S(1)}, u32[]{:S(2)}, u32[]{:S(2)}) collective-permute-start(bf16[256,1024]{1,0:T(8,128)(2,1)S(1)} %shard_map.317.refs_1_), channel_id=1, source_target_pairs={{0,2},{1,3},{2,4},{3,5},{4,6},{5,7},{6,0},{7,1},{8,10},{9,11},{10,... | collective-permute-start | bytes 1572872 | tf_op jit(solution)/shard_map/ppermute | solution.py:355
  44.0 15.5 %collective-permute-start.12 = (bf16[304,1024]{1,0:T(8,128)(2,1)S(1)}, bf16[304,1024]{1,0:T(8,128)(2,1)S(1)}, u32[]{:S(2)}, u32[]{:S(2)}) collective-permute-start(bf16[304,1024]{1,0:T(8,128)(2,1)S(1)} %shard_map.319.refs_9_), channel_id=1, source_target_pairs={{0,1},{1,0},{2,3},{3,2},{4,5},{5,4},{6,7},{7,6},{8,9},{9,8},{10,11... | collective-permute-start | bytes 1867784 | tf_op jit(solution)/shard_map/ppermute | solution.py:355
  59.4 19.8 %collective-permute-start.15 = (bf16[304,1024]{1,0:T(8,128)(2,1)S(1)}, bf16[304,1024]{1,0:T(8,128)(2,1)S(1)}, u32[]{:S(2)}, u32[]{:S(2)}) collective-permute-start(bf16[304,1024]{1,0:T(8,128)(2,1)S(1)} %collective-permute-done.12.refs_3_.refs_2_.refs_4_), channel_id=1, source_target_pairs={{0,8},{1,9},{2,10},{3,11},{4,12},{5,13},{6,14},{7,15},{8,0},{9,1},... | collective-permute-start | bytes 1867784 | tf_op jit(solution)/shard_map/ppermute | solution.py:355
  64.8 16.5 %collective-permute-start.13 = (bf16[304,1024]{1,0:T(8,128)(2,1)S(1)}, bf16[304,1024]{1,0:T(8,128)(2,1)S(1)}, u32[]{:S(2)}, u32[]{:S(2)}) collective-permute-start(bf16[304,1024]{1,0:T(8,128)(2,1)S(1)} %shard_map.323.refs_8_), channel_id=1, source_target_pairs={{0,1},{1,0},{2,3},{3,2},{4,5},{5,4},{6,7},{7,6},{8,9},{9,8},{10,11... | collective-permute-start | bytes 1867784 | tf_op jit(solution)/shard_map/ppermute | solution.py:355
  82.7 17.5 %collective-permute-start.20 = (bf16[304,1024]{1,0:T(8,128)(2,1)S(1)}, bf16[304,1024]{1,0:T(8,128)(2,1)S(1)}, u32[]{:S(2)}, u32[]{:S(2)}) collective-permute-start(bf16[304,1024]{1,0:T(8,128)(2,1)S(1)} %get-tuple-element.121.refs_0_.refs_2_), channel_id=1, source_target_pairs={{0,1},{1,0},{2,3},{3,2},{4,5},{5,4},{6,7},{7,6},{8,9},{9,8},{10,11... | collective-permute-start | bytes 1867784 | tf_op jit(solution)/shard_map/ppermute | solution.py:355
  83.1 17.1 %collective-permute-start.16 = (bf16[304,1024]{1,0:T(8,128)(2,1)S(1)}, bf16[304,1024]{1,0:T(8,128)(2,1)S(1)}, u32[]{:S(2)}, u32[]{:S(2)}) collective-permute-start(bf16[304,1024]{1,0:T(8,128)(2,1)S(1)} %get-tuple-element.121.refs_0_.refs_2_), channel_id=1, source_target_pairs={{0,8},{1,9},{2,10},{3,11},{4,12},{5,13},{6,14},{7,15},{8,0},{9,1},... | collective-permute-start | bytes 1867784 | tf_op jit(solution)/shard_map/ppermute | solution.py:355
  83.1 16.6 %collective-permute-start.18 = (bf16[256,1024]{1,0:T(8,128)(2,1)S(1)}, bf16[256,1024]{1,0:T(8,128)(2,1)S(1)}, u32[]{:S(2)}, u32[]{:S(2)}) collective-permute-start(bf16[256,1024]{1,0:T(8,128)(2,1)S(1)} %collective-permute-done.10.refs_2_.refs_6_), channel_id=1, source_target_pairs={{0,2},{1,3},{2,4},{3,5},{4,6},{5,7},{6,0},{7,1},{8,10},{9,11},{10,... | collective-permute-start | bytes 1572872 | tf_op jit(solution)/shard_map/ppermute | solution.py:355
  84.2 36.9 %collective-permute-start.17 = (bf16[512,1024]{1,0:T(8,128)(2,1)S(1)}, bf16[512,1024]{1,0:T(8,128)(2,1)S(1)}, u32[]{:S(2)}, u32[]{:S(2)}) collective-permute-start(bf16[512,1024]{1,0:T(8,128)(2,1)S(1)} %shard_map.321.refs_5_), channel_id=1, source_target_pairs={{0,6},{1,7},{2,0},{3,1},{4,2},{5,3},{6,4},{7,5},{8,14},{9,15},{10,... | collective-permute-start | bytes 3145736 | tf_op jit(solution)/shard_map/ppermute | solution.py:355
  100.2 27.2 %collective-permute-start.22 = (bf16[304,1024]{1,0:T(8,128)(2,1)S(1)}, bf16[304,1024]{1,0:T(8,128)(2,1)S(1)}, u32[]{:S(2)}, u32[]{:S(2)}) collective-permute-start(bf16[304,1024]{1,0:T(8,128)(2,1)S(1)} %collective-permute-done.20.refs_16_.refs_0_.refs_4_), channel_id=1, source_target_pairs={{0,8},{1,9},{2,10},{3,11},{4,12},{5,13},{6,14},{7,15},{8,0},{9,1},... | collective-permute-start | bytes 1867784 | tf_op jit(solution)/shard_map/ppermute | solution.py:355
  135.4 16.1 %collective-permute-start.26 = (bf16[304,1024]{1,0:T(8,128)(2,1)S(1)}, bf16[304,1024]{1,0:T(8,128)(2,1)S(1)}, u32[]{:S(2)}, u32[]{:S(2)}) collective-permute-start(bf16[304,1024]{1,0:T(8,128)(2,1)S(1)} %shard_map.328.refs_6_), channel_id=1, source_target_pairs={{0,1},{1,0},{2,3},{3,2},{4,5},{5,4},{6,7},{7,6},{8,9},{9,8},{10,11... | collective-permute-start | bytes 1867784 | tf_op jit(solution)/shard_map/ppermute | solution.py:355
  141.7 27.7 %collective-permute-start.30 = (bf16[256,1024]{1,0:T(8,128)(2,1)S(1)}, bf16[256,1024]{1,0:T(8,128)(2,1)S(1)}, u32[]{:S(2)}, u32[]{:S(2)}) collective-permute-start(bf16[256,1024]{1,0:T(8,128)(2,1)S(1)} %get-tuple-element.150), channel_id=1, source_target_pairs={{0,6},{1,7},{2,0},{3,1},{4,2},{5,3},{6,4},{7,5},{8,14},{9,15},{10,... | collective-permute-start | bytes 1572872 | tf_op jit(solution)/shard_map/ppermute | solution.py:355
  143.5 33.4 %collective-permute-start.31 = (bf16[256,1024]{1,0:T(8,128)(2,1)S(1)}, bf16[256,1024]{1,0:T(8,128)(2,1)S(1)}, u32[]{:S(2)}, u32[]{:S(2)}) collective-permute-start(bf16[256,1024]{1,0:T(8,128)(2,1)S(1)} %get-tuple-element.151), channel_id=1, source_target_pairs={{0,2},{1,3},{2,4},{3,5},{4,6},{5,7},{6,0},{7,1},{8,10},{9,11},{10,... | collective-permute-start | bytes 1572872 | tf_op jit(solution)/shard_map/ppermute | solution.py:355
  148.9 41.2 %collective-permute-start.34 = (bf16[512,1024]{1,0:T(8,128)(2,1)S(1)}, bf16[512,1024]{1,0:T(8,128)(2,1)S(1)}, u32[]{:S(2)}, u32[]{:S(2)}) collective-permute-start(bf16[512,1024]{1,0:T(8,128)(2,1)S(1)} %get-tuple-element.153), channel_id=1, source_target_pairs={{0,16},{1,17},{2,18},{3,19},{4,20},{5,21},{6,22},{7,23},{8,24},{9,... | collective-permute-start | bytes 3145736 | tf_op jit(solution)/shard_map/ppermute | solution.py:355
  152.8 16.5 %collective-permute-start.28 = (bf16[304,1024]{1,0:T(8,128)(2,1)S(1)}, bf16[304,1024]{1,0:T(8,128)(2,1)S(1)}, u32[]{:S(2)}, u32[]{:S(2)}) collective-permute-start(bf16[304,1024]{1,0:T(8,128)(2,1)S(1)} %get-tuple-element.143.refs_0_), channel_id=1, source_target_pairs={{0,8},{1,9},{2,10},{3,11},{4,12},{5,13},{6,14},{7,15},{8,0},{9,1},... | collective-permute-start | bytes 1867784 | tf_op jit(solution)/shard_map/ppermute | solution.py:355
  152.9 16.4 %collective-permute-start.27 = (bf16[304,1024]{1,0:T(8,128)(2,1)S(1)}, bf16[304,1024]{1,0:T(8,128)(2,1)S(1)}, u32[]{:S(2)}, u32[]{:S(2)}) collective-permute-start(bf16[304,1024]{1,0:T(8,128)(2,1)S(1)} %get-tuple-element.143.refs_0_), channel_id=1, source_target_pairs={{0,1},{1,0},{2,3},{3,2},{4,5},{5,4},{6,7},{7,6},{8,9},{9,8},{10,11... | collective-permute-start | bytes 1867784 | tf_op jit(solution)/shard_map/ppermute | solution.py:355
  169.5 19.2 %collective-permute-start.32 = (bf16[256,1024]{1,0:T(8,128)(2,1)S(1)}, bf16[256,1024]{1,0:T(8,128)(2,1)S(1)}, u32[]{:S(2)}, u32[]{:S(2)}) collective-permute-start(bf16[256,1024]{1,0:T(8,128)(2,1)S(1)} %shard_map.333.refs_17_), channel_id=1, source_target_pairs={{0,6},{1,7},{2,0},{3,1},{4,2},{5,3},{6,4},{7,5},{8,14},{9,15},{10,... | collective-permute-start | bytes 1572872 | tf_op jit(solution)/shard_map/ppermute | solution.py:355
  188.7 16.4 %collective-permute-start.33 = (bf16[304,1024]{1,0:T(8,128)(2,1)S(1)}, bf16[304,1024]{1,0:T(8,128)(2,1)S(1)}, u32[]{:S(2)}, u32[]{:S(2)}) collective-permute-start(bf16[304,1024]{1,0:T(8,128)(2,1)S(1)} %shard_map.335.refs_2_), channel_id=1, source_target_pairs={{0,1},{1,0},{2,3},{3,2},{4,5},{5,4},{6,7},{7,6},{8,9},{9,8},{10,11... | collective-permute-start | bytes 1867784 | tf_op jit(solution)/shard_map/ppermute | solution.py:355
  190.4 14.8 %collective-permute-start.36 = (bf16[128,1024]{1,0:T(8,128)(2,1)S(1)}, bf16[128,1024]{1,0:T(8,128)(2,1)S(1)}, u32[]{:S(2)}, u32[]{:S(2)}) collective-permute-start(bf16[128,1024]{1,0:T(8,128)(2,1)S(1)} %get-tuple-element.161), channel_id=1, source_target_pairs={{0,6},{1,7},{2,0},{3,1},{4,2},{5,3},{6,4},{7,5},{8,14},{9,15},{10,... | collective-permute-start | bytes 786440 | tf_op jit(solution)/shard_map/ppermute | solution.py:355
  194.7 15.5 %collective-permute-start.37 = (bf16[128,1024]{1,0:T(8,128)(2,1)S(1)}, bf16[128,1024]{1,0:T(8,128)(2,1)S(1)}, u32[]{:S(2)}, u32[]{:S(2)}) collective-permute-start(bf16[128,1024]{1,0:T(8,128)(2,1)S(1)} %get-tuple-element.162), channel_id=1, source_target_pairs={{0,2},{1,3},{2,4},{3,5},{4,6},{5,7},{6,0},{7,1},{8,10},{9,11},{10,... | collective-permute-start | bytes 786440 | tf_op jit(solution)/shard_map/ppermute | solution.py:355
  194.9 16.3 %collective-permute-start.35 = (bf16[288,1024]{1,0:T(8,128)(2,1)S(1)}, bf16[288,1024]{1,0:T(8,128)(2,1)S(1)}, u32[]{:S(2)}, u32[]{:S(2)}) collective-permute-start(bf16[288,1024]{1,0:T(8,128)(2,1)S(1)} %get-tuple-element.157), channel_id=1, source_target_pairs={{0,16},{1,17},{2,18},{3,19},{4,20},{5,21},{6,22},{7,23},{8,24},{9,... | collective-permute-start | bytes 1769480 | tf_op jit(solution)/shard_map/ppermute | solution.py:355
  204.6 17.5 %collective-permute-start.41 = (bf16[288,1024]{1,0:T(8,128)(2,1)S(1)}, bf16[288,1024]{1,0:T(8,128)(2,1)S(1)}, u32[]{:S(2)}, u32[]{:S(2)}) collective-permute-start(bf16[288,1024]{1,0:T(8,128)(2,1)S(1)} %get-tuple-element.170), channel_id=1, source_target_pairs={{0,16},{1,17},{2,18},{3,19},{4,20},{5,21},{6,22},{7,23},{8,24},{9,... | collective-permute-start | bytes 1769480 | tf_op jit(solution)/shard_map/ppermute | solution.py:355
  212.5 18.2 %collective-permute-start.43 = (bf16[144,1024]{1,0:T(8,128)(2,1)S(1)}, bf16[144,1024]{1,0:T(8,128)(2,1)S(1)}, u32[]{:S(2)}, u32[]{:S(2)}) collective-permute-start(bf16[144,1024]{1,0:T(8,128)(2,1)S(1)} %get-tuple-element.163.refs_3_), channel_id=1, source_target_pairs={{0,2},{1,3},{2,4},{3,5},{4,6},{5,7},{6,0},{7,1},{8,10},{9,11},{10,... | collective-permute-start | bytes 884744 | tf_op jit(solution)/shard_map/ppermute | solution.py:355
  213.3 14.9 %collective-permute-start.42 = (bf16[144,1024]{1,0:T(8,128)(2,1)S(1)}, bf16[144,1024]{1,0:T(8,128)(2,1)S(1)}, u32[]{:S(2)}, u32[]{:S(2)}) collective-permute-start(bf16[144,1024]{1,0:T(8,128)(2,1)S(1)} %get-tuple-element.171), channel_id=1, source_target_pairs={{0,6},{1,7},{2,0},{3,1},{4,2},{5,3},{6,4},{7,5},{8,14},{9,15},{10,... | collective-permute-start | bytes 884744 | tf_op jit(solution)/shard_map/ppermute | solution.py:355
  216.6 15.0 %collective-permute-start.40 = (bf16[304,1024]{1,0:T(8,128)(2,1)S(1)}, bf16[304,1024]{1,0:T(8,128)(2,1)S(1)}, u32[]{:S(2)}, u32[]{:S(2)}) collective-permute-start(bf16[304,1024]{1,0:T(8,128)(2,1)S(1)} %shard_map.342.refs_9_), channel_id=1, source_target_pairs={{0,1},{1,0},{2,3},{3,2},{4,5},{5,4},{6,7},{7,6},{8,9},{9,8},{10,11... | collective-permute-start | bytes 1867784 | tf_op jit(solution)/shard_map/ppermute | solution.py:355
  235.0 19.6 %collective-permute-start.50 = (bf16[256,1024]{1,0:T(8,128)(2,1)S(1)}, bf16[256,1024]{1,0:T(8,128)(2,1)S(1)}, u32[]{:S(2)}, u32[]{:S(2)}) collective-permute-start(bf16[256,1024]{1,0:T(8,128)(2,1)S(1)} %shard_map.349.refs_3_.refs_0_), channel_id=1, source_target_pairs={{0,8},{1,9},{2,10},{3,11},{4,12},{5,13},{6,14},{7,15},{8,0},{9,1},... | collective-permute-start | bytes 1572872 | tf_op jit(solution)/shard_map/ppermute | solution.py:355
  239.8 14.3 %collective-permute-start.52 = (bf16[144,1024]{1,0:T(8,128)(2,1)S(1)}, bf16[144,1024]{1,0:T(8,128)(2,1)S(1)}, u32[]{:S(2)}, u32[]{:S(2)}) collective-permute-start(bf16[144,1024]{1,0:T(8,128)(2,1)S(1)} %shard_map.350.refs_2_.refs_0_), channel_id=1, source_target_pairs={{0,16},{1,17},{2,18},{3,19},{4,20},{5,21},{6,22},{7,23},{8,24},{9,... | collective-permute-start | bytes 884744 | tf_op jit(solution)/shard_map/ppermute | solution.py:355
  254.1 15.4 %collective-permute-start.53 = (bf16[144,1024]{1,0:T(8,128)(2,1)S(1)}, bf16[144,1024]{1,0:T(8,128)(2,1)S(1)}, u32[]{:S(2)}, u32[]{:S(2)}) collective-permute-start(bf16[144,1024]{1,0:T(8,128)(2,1)S(1)} %collective-permute-done.52.refs_3_.refs_1_), channel_id=1, source_target_pairs={{0,8},{1,9},{2,10},{3,11},{4,12},{5,13},{6,14},{7,15},{8,0},{9,1},... | collective-permute-start | bytes 884744 | tf_op jit(solution)/shard_map/ppermute | solution.py:355
  (50 other events, 433.7 us)

commit v3 on v2

--- a/solution.py
+++ b/solution.py
@@ -330,6 +330,68 @@
 PART = DH // 2
 
 
+SPANS = {
+    0: 6,
+    1: 1,
+    2: 0.01,
+    3: 30,
+    4: 1,
+    6: 60,
+    7: 6,
+    8: 0.01,
+    11: 6,
+    15: 0.01,
+    18: 10,
+    19: 0.01,
+    23: 0.01,
+    24: 6,
+    25: 0.01,
+    27: 60,
+    28: 3,
+    29: 3,
+    30: 3,
+    33: 1,
+    34: 3,
+    35: 0.01,
+    36: 0.01,
+    37: 10,
+    39: 0.01,
+    40: 10,
+    44: 1,
+    45: 0.01,
+    46: 0.01,
+}
+EARLY = {
+    4: (6,),
+    7: (2,),
+    8: (6,),
+    10: (11,),
+    13: (15,),
+    14: (21,),
+    18: (25,),
+    20: (26,),
+    25: (33,),
+    27: (36,),
+    31: (39,),
+    36: (45,),
+    37: (46,),
+    38: (52,),
+    39: (51,),
+    42: (52,),
+    43: (58,),
+    44: (55,),
+    46: (52,),
+}
+LATE = {
+    4: (1, 0),
+    13: (1,),
+    14: (0,),
+    29: (0,),
+    32: (0,),
+    37: (1, 0),
+}
+
+
 def route(move):
     found = []
     for tok in range(4):
@@ -351,10 +413,6 @@
 PREVIOUS = [(t * 8 + f + 1, t * 8 + f) for t in range(4) for f in range(7)]
 
 
-def send(values, pairs):
-    return lax.ppermute(values, AXES, pairs)
-
-
 def nt(left, right):
     return lax.dot_general(left, right, (((1,), (1,)), ((), ())), preferred_element_type=F32)
 
@@ -372,7 +430,7 @@
 VMEM = pl.BlockSpec(memory_space=pltpu.VMEM)
 
 
-def kernel_call(body, operands, specs, outs, scratch=(), after=(), vmem=12):
+def kernel_call(body, operands, specs, outs, scratch=(), after=(), span=0.01, vmem=12):
     count, extra = len(operands), len(after)
 
     def kernel(*refs):
@@ -387,7 +445,9 @@
         compiler_params=pltpu.CompilerParams(
             vmem_limit_bytes=vmem * 2**20, fuse_transposed_lhs_in_matmul=True
         ),
-        cost_estimate=pl.CostEstimate(flops=10**10, bytes_accessed=2**16, transcendentals=0),
+        cost_estimate=pl.CostEstimate(
+            flops=int(span * 1e9), bytes_accessed=2**16, transcendentals=0
+        ),
     )(*operands, *after)
 
 
@@ -508,9 +568,10 @@
     return weights * (1.0 / jnp.sum(weights, axis=0, keepdims=True))
 
 
-def forward_body(rows, halves, w_in, w_out, bias, qkv, probs, mixed, partials):
+def pair_forward(rows, halves, w_in, bias, qkv, probs, mixed):
     half = halves[0].shape[0]
     _, _, _, y = coordinates()
+    lanes = 2 * DH
     entry = jnp.concatenate([halves[0][...], halves[1][...]], axis=0)
     qkv[...] = (nt(entry, w_in) + bias).astype(BF16)
     key_index = lax.broadcasted_iota(jnp.int32, (2 * half, 1), 0)
@@ -518,20 +579,36 @@
     second = half + rows - 1 + y
     real = (key_index < first) | ((key_index >= half) & (key_index < second))
     penalty = jnp.where(real, 0.0, -1e30)
-    for p in range(2):
-        outs = []
-        for h in (2 * p, 2 * p + 1):
-            at = slice(h * DH, (h + 1) * DH)
-            q = qkv[:, at] * jnp.asarray(DH ** (-0.5), BF16)
-            k = qkv[:, 4 * DH + h * DH : 4 * DH + (h + 1) * DH]
-            v = qkv[:, 8 * DH + h * DH : 8 * DH + (h + 1) * DH]
-            found = softmax_columns(nt(k, q) + penalty).astype(BF16)
-            probs[h] = found
-            outs.append(tn(v, found))
-        mixed[:, 2 * DH * p : 2 * DH * (p + 1)] = jnp.concatenate(outs, axis=0).T.astype(BF16)
-    found = nn(mixed[...], w_out).astype(BF16)
+    outs = []
+    for h in range(2):
+        q = qkv[:, h * DH : (h + 1) * DH] * jnp.asarray(DH ** (-0.5), BF16)
+        k = qkv[:, lanes + h * DH : lanes + (h + 1) * DH]
+        v = qkv[:, 2 * lanes + h * DH : 2 * lanes + (h + 1) * DH]
+        found = softmax_columns(nt(k, q) + penalty).astype(BF16)
+        probs[h] = found
+        outs.append(tn(v, found))
+    mixed[...] = jnp.concatenate(outs, axis=0).T.astype(BF16)
+
+
+def pair_weights(own, other, w_in, w_out):
+    for m in range(4):
+        target = w_out if m == 3 else w_in
+        for i in range(2):
+            at = (0 if m == 3 else m * 2 * DH) + i * DH
+            target[at : at + PART, :] = own[i][m * PART : (m + 1) * PART, :]
+            target[at + PART : at + DH, :] = other[i][m * PART : (m + 1) * PART, :]
+    rows_of = [own[i][4 * PART : 4 * PART + 16, :].astype(F32)[0:1] for i in range(2)]
+    query = jnp.concatenate([ordered_bias(r, 0) for r in rows_of], axis=1)
+    value = jnp.concatenate([ordered_bias(r, 2 * DH) for r in rows_of], axis=1)
+    return jnp.concatenate([query, jnp.zeros_like(query), value], axis=1)
+
+
+def projected(first_mixed, second_mixed, first_out, second_out, outs):
+    mixed = jnp.concatenate([first_mixed[...], second_mixed[...]], axis=1)
+    weights = jnp.concatenate([first_out[...], second_out[...]], axis=0)
+    found = nn(mixed, weights).astype(BF16)
     at = 0
-    for out in partials:
+    for out in outs:
         out[...] = found[at : at + out.shape[0]]
         at += out.shape[0]
 
@@ -543,49 +620,37 @@
     return jnp.where(x == 0, block, swapped)
 
 
-def first_forward_kernel(rows, *refs):
-    halves, refs = refs[:2], refs[2:]
-    own, other = halves_of(refs[:7], refs[0].shape[0])
-    refs = refs[7:]
-    qkv, probs, mixed, partial, w_in, w_out, bias = refs
-    for m in range(4):
-        target = w_out if m == 3 else w_in
-        for k in range(4):
-            at = (0 if m == 3 else m * 4 * DH) + k * DH
-            target[at : at + PART, :] = own[k][m * PART : (m + 1) * PART, :]
-            target[at + PART : at + DH, :] = other[k][m * PART : (m + 1) * PART, :]
-    rows_of = [own[k][4 * PART :, :].astype(F32)[0:1] for k in range(4)]
-    query = jnp.concatenate([ordered_bias(r, 0) for r in rows_of], axis=1)
-    value = jnp.concatenate([ordered_bias(r, 2 * DH) for r in rows_of], axis=1)
-    bias[...] = jnp.broadcast_to(
-        jnp.concatenate([query, jnp.zeros_like(query), value], axis=1), bias.shape
-    )
-    forward_body(
-        rows,
-        halves,
-        w_in[...],
-        w_out[...],
-        bias[0:1, :],
-        qkv,
-        probs,
-        mixed,
-        (partial,),
-    )
-
-
-def second_forward_kernel(rows, near, far, w_in, w_out, bias, *refs):
+def first_pair_kernel(rows, near, far, near_other, far_other, *refs):
+    own_zero, other_zero, own_one, other_one, *refs = refs
+    qkv_own, qkv_other, probs_own, probs_other, mixed_own, mixed_other, w_in, w_out = refs
+    bias = pair_weights((own_zero, own_one), (other_zero, other_one), w_in, w_out)
+    weights = w_in[...]
+    pair_forward(rows, (near_other, far_other), weights, bias, qkv_other, probs_other, mixed_other)
+    pair_forward(rows, (near, far), weights, bias, qkv_own, probs_own, mixed_own)
+
+
+def second_pair_other_kernel(rows, near, far, both, own_two, other_two, *refs):
+    first_mixed, first_out, qkv, probs, mixed, partial, w_in, w_out, bias = refs
+    piece = own_two.shape[0]
+    own = (both.at[pl.ds(0, piece)], own_two)
+    other = (both.at[pl.ds(piece, piece)], other_two)
+    found = pair_weights(own, other, w_in, w_out)
+    bias[...] = jnp.broadcast_to(found, bias.shape)
+    pair_forward(rows, (near, far), w_in[...], found, qkv, probs, mixed)
+    projected(first_mixed, mixed, first_out, w_out, (partial,))
+
+
+def second_pair_own_kernel(rows, near, far, w_in, w_out, bias, first_mixed, first_out, *refs):
     qkv, probs, mixed, *partials = refs
-    forward_body(
-        rows,
-        (near, far),
-        w_in[...],
-        w_out[...],
-        bias[0:1, :],
-        qkv,
-        probs,
-        mixed,
-        partials,
-    )
+    pair_forward(rows, (near, far), w_in[...], bias[0:1, :], qkv, probs, mixed)
+    projected(first_mixed, mixed, first_out, w_out, partials)
+
+
+def joined_rows(refs, at):
+    size = refs[0].shape[0]
+    if at.start < size:
+        return refs[0][at, :]
+    return refs[1][at.start - size : at.stop - size, :]
 
 
 def real_rows(at, rows, y):
@@ -597,7 +662,8 @@
     valid,
     partial,
     from_core,
-    from_y,
+    from_y_first,
+    from_y_second,
     stream,
     bias_vector,
     gain_vector,
@@ -610,8 +676,9 @@
     bias, gain, shift = row_of(bias_vector), row_of(gain_vector), row_of(shift_vector)
     total = jnp.zeros((8, middle.shape[1]), F32)
     for at in chunks(middle.shape[0]):
+        from_y = joined_rows((from_y_first, from_y_second), at)
         attn = partial[at, :].astype(F32) + from_core[at, :].astype(F32)
-        attn = attn + from_y[at, :].astype(F32) + bias
+        attn = attn + from_y.astype(F32) + bias
         found = stream[at, :].astype(F32) + attn
         middle[at, :] = found
         hat, _ = moment_norm(found)
@@ -677,11 +744,16 @@
             outs[side][...] = found
 
 
-def far_sum_kernel(values, received, out):
-    first = received.shape[0] - out.shape[0]
-    for at in chunks(out.shape[0]):
-        moved = slice(first + at.start, first + at.stop)
-        out[at, :] = (values[at, :].astype(F32) + received[moved, :].astype(F32)).astype(BF16)
+def far_sum_kernel(values, received, *outs):
+    first = received.shape[0] - values.shape[0]
+    done = 0
+    for out in outs:
+        for at in chunks(out.shape[0]):
+            source = slice(done + at.start, done + at.stop)
+            moved = slice(first + source.start, first + source.stop)
+            found = values[source, :].astype(F32) + received[moved, :].astype(F32)
+            out[at, :] = found.astype(BF16)
+        done += out.shape[0]
 
 
 def add_split_kernel(keep, received, *outs):
@@ -772,22 +844,21 @@
     half = grads[0].shape[0]
     rows = 2 * half
     lanes = 2 * DH
-    first = pair * lanes
     scale = jnp.asarray(DH ** (-0.5), BF16)
     grad_rows = jnp.concatenate([ref[...] for ref in grads], axis=0)
-    wide = nt(grad_rows, w_out[first : first + lanes, :]).astype(BF16)
+    wide = nt(grad_rows, w_out[...]).astype(BF16)
     hidden_sums = sums_chip[0:1, :] + sums_distant[0:1, :]
     totals = []
     images = ((qkv_own, probs_own, out_own), (qkv_other, probs_other, out_other))
     for image, (qkv, probs, out) in enumerate(images):
         dq, dk, dv = [], [], []
         for h in range(2):
-            at = first + h * DH
+            at = h * DH
             q = qkv[:, at : at + DH] * scale
-            k = qkv[:, 4 * DH + at : 4 * DH + at + DH] * scale
-            v = qkv[:, 8 * DH + at : 8 * DH + at + DH]
+            k = qkv[:, lanes + at : lanes + at + DH] * scale
+            v = qkv[:, 2 * lanes + at : 2 * lanes + at + DH]
             g = wide[image * rows : (image + 1) * rows, h * DH : (h + 1) * DH]
-            found = probs[2 * pair + h]
+            found = probs[h]
             grad_probs = nt(v, g)
             scores = found.astype(F32)
             product = scores * grad_probs
@@ -807,9 +878,7 @@
     query_sum, value_sum = (totals[0][i] + totals[1][i] for i in range(2))
     stacked = jnp.concatenate([out_own[...], out_other[...]], axis=0)
     grad_w = tn(stacked, jnp.concatenate([ref[...] for ref in normed], axis=0)).astype(BF16)
-    mixed = jnp.concatenate(
-        [ref[:, first : first + lanes] for ref in (mixed_own, mixed_other)], axis=0
-    )
+    mixed = jnp.concatenate([mixed_own[...], mixed_other[...]], axis=0)
     grad_o = tn(mixed, grad_rows).astype(BF16)
     size = 4 * PART + 16
     quarter = hidden_sums.shape[1] // 8
@@ -837,17 +906,10 @@
             )
 
 
-def entry_product_kernel(first_pair, second_pair, w_in, *outs):
-    lanes = 2 * DH
-    joined = jnp.concatenate(
-        [
-            ref[:, m * lanes : (m + 1) * lanes]
-            for m in range(3)
-            for ref in (first_pair, second_pair)
-        ],
-        axis=1,
-    )
-    found = nn(joined, w_in[...]).astype(BF16)
+def entry_product_kernel(first_pair, second_pair, first_weights, second_weights, *outs):
+    joined = jnp.concatenate([first_pair[...], second_pair[...]], axis=1)
+    weights = jnp.concatenate([first_weights[...], second_weights[...]], axis=0)
+    found = nn(joined, weights).astype(BF16)
     at = 0
     for out in outs:
         out[...] = found[at : at + out.shape[0]]
@@ -1026,20 +1088,35 @@
     piece = 4 * PART + 16
     row_block = (half, width)
     low_rows, wide_rows = (row_block, BF16), (row_block, F32)
-    last = ()
-
-    def call(body, operands, outs, scratch=(), gate=(), specs=None):
+    last, usual = (), 0.01
+    calls, sent = [], []
+
+    def send(values, pairs):
+        found = lax.ppermute(values, AXES, pairs)
+        sent.append(found)
+        return found
+
+
+    def call(body, operands, outs, scratch=(), gate=(), specs=None, span=None, final=False):
         nonlocal last
         specs = [VMEM] * len(operands) if specs is None else specs
-        found = kernel_call(body, operands, specs, outs, scratch, last + tuple(gate))
-        last = (min(found, key=lambda v: v.size * v.dtype.itemsize),)
+        number = len(calls)
+        calls.append(number)
+        span = SPANS.get(number, usual if span is None else span)
+        gate = [g for i, g in enumerate(gate) if i not in LATE.get(number, ())]
+        gate += [sent[i] for i in EARLY.get(number, ()) if i < len(sent)]
+        found = kernel_call(body, operands, specs, outs, scratch, last + tuple(gate), span)
+        if not final:
+            last = (min(found, key=lambda v: v.size * v.dtype.itemsize),)
         return found
 
     def pin(values, gate=()):
         return call(copy_kernel, (values,), [(values.shape, values.dtype)], gate=gate)[0]
 
-    def far_sum(values, received, gate=()):
-        return call(far_sum_kernel, (values, received), [low_rows], gate=gate)[0]
+    def far_sum(values, received, gate=(), sizes=(half,)):
+        outs = [((size, width), BF16) for size in sizes]
+        found = call(far_sum_kernel, (values, received), outs, gate=gate)
+        return found if len(sizes) > 1 else found[0]
 
     def split(values, received, sizes, gate=()):
         outs = [((size, width), BF16) for size in sizes]
@@ -1079,8 +1156,7 @@
         [low_rows] * 4,
         scratch=[pltpu.VMEM((half + 8, width), F32)],
         gate=(own_one,),
-        specs=[SMEM] + [VMEM] * 5,
-    )
+        specs=[SMEM] + [VMEM] * 5, span=30)
     own_two = send(own_one, UP_Z)
     other_one = send(own_one, SWAP_X)
     normed_y, normed_c = send(normed, SWAP_Y), send(normed, SWAP_C)
@@ -1091,46 +1167,60 @@
     branch_again = pin(branch_again, (normed_y,))
     normed_yc = send(normed_y, SWAP_C)
     branch_y, branch_c = send(branch_again, SWAP_Y), send(branch_again, SWAP_C)
-    attn_pieces = (attn_own, attn_other, own_one, other_one, attn_three, own_two, other_two)
-
-    head_out = [
-        ((image, 12 * DH), BF16),
-        ((4, image, image), BF16),
-        ((image, 4 * DH), BF16),
-    ]
-    qkv_other, probs_other, mixed_other, partial_other, w_heads, w_out, head_bias = call(
-        functools.partial(first_forward_kernel, rows),
-        (normed_c, normed_yc) + attn_pieces,
-        head_out
+
+    lanes = 2 * DH
+    pair_out = [((image, 3 * lanes), BF16)], [((2, image, image), BF16)], [((image, lanes), BF16)]
+    weight_out = [((3 * lanes, width), BF16), ((lanes, width), BF16)]
+    first_pair = call(
+        functools.partial(first_pair_kernel, rows),
+        (normed, normed_y, normed_c, normed_yc, attn_own, attn_other, own_one, other_one),
+        pair_out[0] * 2 + pair_out[1] * 2 + pair_out[2] * 2 + weight_out,
+        span=30,
+    )
+    w_first, out_first = first_pair[6:]
+    qkv_other, probs_other, mixed_other, partial_other, w_second, out_second, second_bias = call(
+        functools.partial(second_pair_other_kernel, rows),
+        (normed_c, normed_yc, attn_three, own_two, other_two, first_pair[5], out_first),
+        pair_out[0]
+        + pair_out[1]
+        + pair_out[2]
         + [((image, width), BF16)]
-        + [((12 * DH, width), BF16), ((4 * DH, width), BF16), ((8, 12 * DH), F32)],
+        + weight_out
+        + [((8, 3 * lanes), F32)],
         gate=(branch_c,),
+        span=30,
     )
     from_core = send(partial_other, SWAP_C)
-    mlp_both = pin(mlp_both, (mlp_one,))
-    mlp_three = send(mlp_both, DOWN_Z)
     mlp_two = send(mlp_one, UP_Z)
     mlp_other_one = send(mlp_one, SWAP_X)
     qkv_own, probs_own, mixed_own, partial_near, partial_far = call(
-        functools.partial(second_forward_kernel, rows),
-        (normed, normed_y, w_heads, w_out, head_bias),
-        head_out + [low_rows] * 2,
-    )
-    attn_far = far_sum(partial_far, from_core, (branch_y,))
-    from_y = send(attn_far, SWAP_Y)
+        functools.partial(second_pair_own_kernel, rows),
+        (normed, normed_y, w_second, out_second, second_bias, first_pair[4], out_first),
+        pair_out[0] + pair_out[1] + pair_out[2] + [low_rows] * 2,
+        gate=(mlp_one,),
+        span=30,
+    )
+    saved = (
+        (out_first,) + tuple(first_pair[:6]),
+        (out_second, qkv_own, qkv_other, probs_own, probs_other, mixed_own, mixed_other),
+    )
+    parts_of_half = (half // 2 + 8, half - half // 2 - 8)
+    attn_far = far_sum(partial_far, from_core, (branch_y,), parts_of_half)
+    from_y = tuple(send(part, SWAP_Y) for part in attn_far)
+    mlp_three = send(pin(mlp_both), DOWN_Z)
     branch_yc = send(branch_y, SWAP_C)
     middle, normed_middle, attn_power = call(
         functools.partial(middle_kernel, rows),
-        (valid, partial_near, from_core, from_y, stream)
+        (valid, partial_near, from_core) + from_y + (stream,)
         + (b_attn_out, feedforward_norm_gain, feedforward_norm_shift),
         [wide_rows, low_rows, ((8, width), F32)],
         gate=(mlp_other_one, branch_yc),
-        specs=[SMEM] + [VMEM] * 7,
-    )
+        specs=[SMEM] + [VMEM] * 8, span=30)
     middle_y, middle_c = send(normed_middle, SWAP_Y), send(normed_middle, SWAP_C)
     pin(attn_power, (mlp_two, middle_c))
     mlp_other_two = send(mlp_two, SWAP_X)
 
+    usual = 10
     middle_yc = send(middle_y, SWAP_C)
     pieces = (mlp_own, mlp_other, mlp_one, mlp_other_one, mlp_three, mlp_two, mlp_other_two)
     pieces += (attn_own, own_one, attn_three, own_two)
@@ -1179,35 +1269,35 @@
         return call(
             functools.partial(backward_kernel, p),
             (grad_attn, grad_y, grad_c, grad_yc, normed, normed_y, normed_c, normed_yc)
-            + (w_out, qkv_own, qkv_other, probs_own, probs_other)
-            + (mixed_own, mixed_other, chip[6], distant[6]),
+            + saved[p]
+            + (chip[6], distant[6]),
             [((image, 6 * DH), BF16)] * 2 + [((2 * piece, width), BF16)] * 2,
             gate=gate,
         )
 
-    second_own, second_other, give, keep = backward(1, (out_three,))
+    second_own, second_other, give, keep = backward(1)
     received = send(give, SWAP_X)
-    out_y = send(pin(out_far, (out_one,)), SWAP_Y)
+    out_y = send(pin(out_far), SWAP_Y)
+    first_own, first_other, give_first, keep_first = backward(0, (out_one, out_three))
+    received_first = send(give_first, SWAP_X)
     in_pieces = split(grad_in_keep, in_received, (quarter,) * 4)
     in_pieces = dict(zip(SLOTS, in_pieces))
     in_two = send(in_pieces[2], DOWN_Z)
     in_three = send(in_pieces[3], UP_Z)
-    first_own, first_other, give_first, keep_first = backward(0)
-    received_first = send(give_first, SWAP_X)
-    (one,) = split(in_pieces[1], in_two, (quarter,), (out_y,))
-    in_one = send(one, DOWN_Z)
     (entry_other,) = call(
-        entry_product_kernel, (first_other, second_other, w_heads), [((image, width), BF16)]
+        entry_product_kernel, (first_other, second_other, w_first, w_second), [((image, width), BF16)]
     )
     entry_core = send(entry_other, SWAP_C)
+    entry_near, entry_far = call(
+        entry_product_kernel, (first_own, second_own, w_first, w_second), [low_rows] * 2
+    )
+    entry_far = far_sum(entry_far, entry_core)
+    entry_y = send(entry_far, SWAP_Y)
     three, two = split(keep, received, (piece,) * 2, (in_three,))
     attn_two = send(two, DOWN_Z)
     attn_three = send(three, UP_Z)
-    entry_near, entry_far = call(
-        entry_product_kernel, (first_own, second_own, w_heads), [low_rows] * 2
-    )
-    entry_far = far_sum(entry_far, entry_core, (in_one,))
-    entry_y = send(entry_far, SWAP_Y)
+    (one,) = split(in_pieces[1], in_two, (quarter,))
+    in_one = send(one, DOWN_Z)
     output, output_heads, power_sums = call(
         functools.partial(output_kernel, rows),
         (valid, chip[4], out_core, out_y, middle, stream, b_mlp_out, attn_power, middle_sums),
@@ -1227,7 +1317,6 @@
         [((piece, width), BF16)] * 2,
     )
     attn_one = send(one, DOWN_Z)
-    in_total = add_last(in_pieces[0], in_one, in_three)
     gradient, heads, small = call(
         functools.partial(entry_back_kernel, rows),
         (valid, entry_near, entry_core, entry_y, stream, grad_middle)
@@ -1240,47 +1329,46 @@
     def add_small(received, gate=()):
         return call(add_wide_kernel, (small, received), [(small.shape, F32)], gate=gate)[0]
 
-    in_across, in_core = send(in_total, SWAP_X), send(in_total, SWAP_C)
     heads_after = send(jnp.concatenate([output_heads, heads]), PREVIOUS)
-    small = add_small(send(small, SWAP_C), (in_core,))
+    small = add_small(send(small, SWAP_C))
     small_y = send(small, SWAP_Y)
-    (out_whole,) = call(
-        swapped_sum_kernel, (out_total, out_across), [((2 * quarter, width), BF16)]
-    )
-    out_core = send(out_whole, SWAP_C)
-    attn_total = add_last(zero, attn_one, attn_three, (heads_after,))
+    attn_total = add_last(zero, attn_one, attn_three, (out_across,))
     attn_across, attn_core = send(attn_total, SWAP_X), send(attn_total, SWAP_C)
-    small = add_small(small_y, (out_core, attn_core))
+    small = add_small(small_y, (attn_core, heads_after))
     small_z = send(small, FLIP_Z[1])
     output_rows, gradient_rows = call(
         exit_kernel,
         (output, gradient, heads_after),
         [((rows, width), F32)] * 2,
-        scratch=[pltpu.VMEM((half, width), F32)],
-    )
-    small = add_small(small_z, (in_across,))
+        scratch=[pltpu.VMEM((half, width), F32)], final=True)
+    small = add_small(small_z)
     small_z = send(small, FLIP_Z[2])
-    in_last = send(in_across, SWAP_C)
-    (grad_w_mlp_out,) = call(
-        mlp_out_gradient_kernel, (out_whole, out_core), [((hidden_local, width), F32)]
-    )
-    small = add_small(small_z, (attn_across,))
+    in_total = add_last(in_pieces[0], in_one, in_three)
+    in_across, in_core = send(in_total, SWAP_X), send(in_total, SWAP_C)
+    (out_whole,) = call(
+        swapped_sum_kernel,
+        (out_total, out_across),
+        [((2 * quarter, width), BF16)],
+        gate=(attn_across,),
+    )
+    out_core = send(out_whole, SWAP_C)
+    attn_last = send(attn_across, SWAP_C)
+    small = add_small(small_z, (in_core,))
     small_x = send(small, SWAP_X)
-    attn_last = send(attn_across, SWAP_C)
-    (grad_w_mlp_in,) = call(
-        mlp_in_gradient_kernel,
-        (in_total, in_across, in_core, in_last),
-        [((width, hidden_local), F32)],
-    )
     attn_grads = call(
         attention_gradients_kernel,
         (attn_total, attn_across, attn_core, attn_last),
         [((2 * DH, width), F32)] * 4
-        + [((2 * DH,), F32), ((2 * DH,), F32), ((hidden_local,), F32)],
-    )
+        + [((2 * DH,), F32), ((2 * DH,), F32), ((hidden_local,), F32)], final=True)
+    in_last = send(in_across, SWAP_C)
+    (grad_w_mlp_out,) = call(
+        mlp_out_gradient_kernel, (out_whole, out_core), [((hidden_local, width), F32)], final=True)
+    (grad_w_mlp_in,) = call(
+        mlp_in_gradient_kernel,
+        (in_total, in_across, in_core, in_last),
+        [((width, hidden_local), F32)], final=True)
     *vectors, powers = call(
-        sums_kernel, (small, small_x), [((width,), F32)] * 6 + [((2 * DH,), F32)]
-    )
+        sums_kernel, (small, small_x), [((width,), F32)] * 6 + [((2 * DH,), F32)], final=True)
     stream_rms = jnp.sqrt(powers[:4] / (jnp.maximum(powers[4], 1.0) * D))
     return (
         output_rows,

time: 279 us -> 239 us (0.86)
  waiting for transfers between devices: 131 us -> 92.6 us
  local copies, waits for them, and re-layouts: 5.98 us -> 0.67 us
    ppermute x59 -> x60, waiting for transfers between devices: 131 us -> 92.6 us  [send(): found = lax.ppermute(values, AXES, pairs)]
    unnamed x46 -> x34, local copies, waits for them, and re-layouts: 5.4 us -> 0.09 us
    ppermute x59 -> x60, starting transfers between devices: 66 us -> 67.8 us  [send(): found = lax.ppermute(values, AXES, pairs)]
    pallas_call x46 -> x47, Pallas kernels: 70 us -> 71.6 us  [kernel_call(): pl.pallas_call(kernel, in_specs=list(specs) + [VMEM] * extra, out_specs=[...]
  transfers between devices with their start and end apart: 59 -> 60, of which waited for: 24 -> 21; matrix products, arithmetic and copies ran while one was open for 0% -> 0% of each run, Pallas kernels for 23% -> 28%
where the time goes in v3:
time: 239 us; the launch traced here: 235 us
  waiting for transfers between devices  92.6 us (39%)
  Pallas kernels  71.6 us (30%)
  starting transfers between devices  67.8 us (28%)
    ppermute x60, waiting for transfers between devices, send(): found = lax.ppermute(values, AXES, pairs)  92.6 us
    pallas_call x47, Pallas kernels, kernel_call(): pl.pallas_call(kernel, in_specs=list(specs) + [VMEM] * extra, out_specs=[...  71.6 us
    ppermute x60, starting transfers between devices, send(): found = lax.ppermute(values, AXES, pairs)  67.8 us
  transfers between devices with their start and end apart: 60, of which 21 were waited for; matrix products, arithmetic and copies ran while one was open for 0% of the time, Pallas kernels for 28%

profile of v3, /device:TPU:0, one launch (start us, length us, event | category | flops | bytes accessed | tf_op | source)
XLA Modules:
  0.0 235.2 jit_solution(9056478902293814350)
XLA Ops:
  2.2 3.1 %collective-permute-start.1 = (bf16[144,1024]{1,0:T(8,128)(2,1)S(1)}, bf16[144,1024]{1,0:T(8,128)(2,1)S(1)}, u32[]{:S(2)}, u32[]{:S(2)}) collective-permute-start(bf16[144,1024]{1,0:T(8,128)(2,1)S(1)} %get-tuple-element.116.refs_2_.refs_4_.refs_11_), channel_id=1, source_target_pairs={{0,2},{1,3},{2,4},{3,5},{4,6},{5,7},{6,0},{7,1},{8,10},{9,11},{10,... | collective-permute-start | bytes 884744 | tf_op jit(solution)/shard_map/ppermute | solution.py:1095
  5.4 3.6 %collective-permute-start = (bf16[16,1024]{1,0:T(8,128)(2,1)S(1)}, bf16[16,1024]{1,0:T(8,128)(2,1)S(1)}, u32[]{:S(2)}, u32[]{:S(2)}) collective-permute-start(bf16[16,1024]{1,0:T(8,128)(2,1)S(1)} %shard_map.314.refs_2_), channel_id=1, source_target_pairs={{0,1},{1,2},{2,3},{3,4},{4,5},{5,6},{6,7},{8,9},{9,10},{10,11},{11... | collective-permute-start | bytes 98312 | tf_op jit(solution)/shard_map/ppermute | solution.py:1095
  10.5 3.8 %collective-permute-done.1.refs_7_.refs_6_.refs_12_ = bf16[144,1024]{1,0:T(8,128)(2,1)S(1)} collective-permute-done((bf16[144,1024]{1,0:T(8,128)(2,1)S(1)}, bf16[144,1024]{1,0:T(8,128)(2,1)S(1)}, u32[]{:S(2)}, u32[]{:S(2)}) %collective-permute-start.1) | collective-permute-done | bytes 294944 | tf_op jit(solution)/shard_map/ppermute | solution.py:1095
  21.0 11.6 %collective-permute-done.2.refs_2_.refs_1_.refs_5_ = bf16[304,1024]{1,0:T(8,128)(2,1)S(1)} collective-permute-done((bf16[304,1024]{1,0:T(8,128)(2,1)S(1)}, bf16[304,1024]{1,0:T(8,128)(2,1)S(1)}, u32[]{:S(2)}, u32[]{:S(2)}) %collective-permute-start.2) | collective-permute-done | bytes 622624 | tf_op jit(solution)/shard_map/ppermute | solution.py:1095
  34.8 2.2 collective-permute-start.5
  36.9 5.3 %collective-permute-done.10.refs_8_.refs_6_ = bf16[256,1024]{1,0:T(8,128)(2,1)S(1)} collective-permute-done((bf16[256,1024]{1,0:T(8,128)(2,1)S(1)}, bf16[256,1024]{1,0:T(8,128)(2,1)S(1)}, u32[]{:S(2)}, u32[]{:S(2)}) %collective-permute-start.10) | collective-permute-done | bytes 524320 | tf_op jit(solution)/shard_map/ppermute | solution.py:1095
  42.9 5.3 %shard_map.320 = (bf16[608,384]{1,0:T(8,128)(2,1)S(1)}, bf16[608,384]{1,0:T(8,128)(2,1)S(1)}, bf16[2,608,608]{2,1,0:T(8,128)(2,1)S(1)}, bf16[2,608,608]{2,1,0:T(...) custom-call(bf16[304,1024]{1,0:T(8,128)(2,1)S(1)} %get-tuple-element, ...), custom_call_target="tpu_custom_call" | custom-call | flops 6000000000 | bytes 65536 | tf_op jit(solution)/shard_map/pallas_call | solution.py:439
  48.3 6.6 %collective-permute-done.5.refs_2_.refs_13_ = bf16[288,1024]{1,0:T(8,128)(2,1)S(1)} collective-permute-done((bf16[288,1024]{1,0:T(8,128)(2,1)S(1)}, bf16[288,1024]{1,0:T(8,128)(2,1)S(1)}, u32[]{:S(2)}, u32[]{:S(2)}) %collective-permute-start.5) | collective-permute-done | bytes 589856 | tf_op jit(solution)/shard_map/ppermute | solution.py:1095
  55.4 3.1 %shard_map.321 = (bf16[608,384]{1,0:T(8,128)(2,1)S(1)}, bf16[2,608,608]{2,1,0:T(8,128)(2,1)S(1)}, bf16[608,128]{1,0:T(8,128)(2,1)S(1)}, bf16[608,1024]{1,0:T(8,1...) custom-call(bf16[304,1024]{1,0:T(8,128)(2,1)S(1)} %collective-permute-done.3.refs_2, ...), custom_call_target="tpu_custom_call" | custom-call | flops 10000000 | bytes 65536 | tf_op jit(solution)/shard_map/pallas_call | solution.py:439
  59.0 3.1 %shard_map.322 = (bf16[608,384]{1,0:T(8,128)(2,1)S(1)}, bf16[2,608,608]{2,1,0:T(8,128)(2,1)S(1)}, bf16[608,128]{1,0:T(8,128)(2,1)S(1)}, bf16[304,1024]{1,0:T(8,128)(2,1)S(1)}, bf16[304,1024]{1,0:T(8,128)(2,1)S(1)}) custom-call(bf16[304,1024]{1,0:T(8,128)(2,1)S(1)} %get-tuple-element.118.refs_0_.refs_4_, ...), custom_call_target="tpu_custom_call" | custom-call | flops 30000001024 | bytes 65536 | tf_op jit(solution)/shard_map/pallas_call | solution.py:439
  64.4 4.1 %collective-permute-done.15.refs_10_.refs_7_ = bf16[256,1024]{1,0:T(8,128)(2,1)S(1)} collective-permute-done((bf16[256,1024]{1,0:T(8,128)(2,1)S(1)}, bf16[256,1024]{1,0:T(8,128)(2,1)S(1)}, u32[]{:S(2)}, u32[]{:S(2)}) %collective-permute-start.15) | collective-permute-done | bytes 524320 | tf_op jit(solution)/shard_map/ppermute | solution.py:1095
  68.5 3.9 %collective-permute-start.18 = (bf16[512,1024]{1,0:T(8,128)(2,1)S(1)}, bf16[512,1024]{1,0:T(8,128)(2,1)S(1)}, u32[]{:S(2)}, u32[]{:S(2)}) collective-permute-start(bf16[512,1024]{1,0:T(8,128)(2,1)S(1)} %shard_map.324.refs_9_), channel_id=1, source_target_pairs={{0,6},{1,7},{2,0},{3,1},{4,2},{5,3},{6,4},{7,5},{8,14},{9,15},{10,... | collective-permute-start | bytes 3145736 | tf_op jit(solution)/shard_map/ppermute | solution.py:1095
  72.4 5.9 %collective-permute-done.13.refs_3_ = bf16[160,1024]{1,0:T(8,128)(2,1)S(1)} collective-permute-done((bf16[160,1024]{1,0:T(8,128)(2,1)S(1)}, bf16[160,1024]{1,0:T(8,128)(2,1)S(1)}, u32[]{:S(2)}, u32[]{:S(2)}) %collective-permute-start.13) | collective-permute-done | bytes 327712 | tf_op jit(solution)/shard_map/ppermute | solution.py:1095
  81.8 13.2 %collective-permute-done.22.refs_0_.refs_4_ = bf16[304,1024]{1,0:T(8,128)(2,1)S(1)} collective-permute-done((bf16[304,1024]{1,0:T(8,128)(2,1)S(1)}, bf16[304,1024]{1,0:T(8,128)(2,1)S(1)}, u32[]{:S(2)}, u32[]{:S(2)}) %collective-permute-start.22) | collective-permute-done | bytes 622624 | tf_op jit(solution)/shard_map/ppermute | solution.py:1095
  95.1 5.7 %shard_map.327 = (bf16[608,1024]{1,0:T(8,128)(2,1)S(1)}, bf16[608,1024]{1,0:T(8,128)(2,1)S(1)}, bf16[304,1024]{1,0:T(8,128)(2,1)S(1)}, bf16[304,1024]{1,0:T(8,12...) custom-call(bf16[304,1024]{1,0:T(8,128)(2,1)S(1)} %get-tuple-element.136.refs_0_.re, ...), custom_call_target="tpu_custom_call" | custom-call | flops 10000000000 | bytes 65536 | tf_op jit(solution)/shard_map/pallas_call | solution.py:439
  101.4 5.7 %shard_map.328 = (bf16[608,1024]{1,0:T(8,128)(2,1)S(1)}, bf16[608,1024]{1,0:T(8,128)(2,1)S(1)}, bf16[304,1024]{1,0:T(8,128)(2,1)S(1)}, bf16[304,1024]{1,0:T(8,12...) custom-call(bf16[304,1024]{1,0:T(8,128)(2,1)S(1)} %collective-permute-done.22.refs_, ...), custom_call_target="tpu_custom_call" | custom-call | flops 10000000 | bytes 65536 | tf_op jit(solution)/shard_map/pallas_call | solution.py:439
  110.8 5.3 %shard_map.330 = (bf16[256,1024]{1,0:T(8,128)(2,1)S(1)}, bf16[256,1024]{1,0:T(8,128)(2,1)S(1)}, bf16[256,1024]{1,0:T(8,128)(2,1)S(1)}, bf16[256,1024]{1,0:T(8,128)(2,1)S(1)}) custom-call(bf16[608,1024]{1,0:T(8,128)(2,1)S(1)} %get-tuple-element.153.refs_0_, bf16[608,1024]{1,0:T(8,128)(2,1)S(1)} %get-tuple-element.154.refs_1_, ...), custom_call_target="tpu_custom_call" | custom-call | flops 10000000000 | bytes 65536 | tf_op jit(solution)/shard_map/pallas_call | solution.py:439
  116.1 8.2 %collective-permute-start.31 = (bf16[256,1024]{1,0:T(8,128)(2,1)S(1)}, bf16[256,1024]{1,0:T(8,128)(2,1)S(1)}, u32[]{:S(2)}, u32[]{:S(2)}) collective-permute-start(bf16[256,1024]{1,0:T(8,128)(2,1)S(1)} %get-tuple-element.165), channel_id=1, source_target_pairs={{0,6},{1,7},{2,0},{3,1},{4,2},{5,3},{6,4},{7,5},{8,14},{9,15},{10,... | collective-permute-start | bytes 1572872 | tf_op jit(solution)/shard_map/ppermute | solution.py:1095
  124.4 5.1 %shard_map.331 = (bf16[512,1024]{1,0:T(8,128)(2,1)S(1)}, bf16[512,1024]{1,0:T(8,128)(2,1)S(1)}) custom-call(bf16[608,1024]{1,0:T(8,128)(2,1)S(1)} %get-tuple-element.151.refs_0_, bf16[608,1024]{1,0:T(8,128)(2,1)S(1)} %get-tuple-element.152.refs_1_, bf16[304,1024]{1,0:T(8,128)(2,1)S(1)} %get-tuple-element.136.refs_0_.refs_2_, ...), custom_call_target="tpu_custom_call" | custom-call | flops 10000000000 | bytes 65536 | tf_op jit(solution)/shard_map/pallas_call | solution.py:439
  132.5 15.0 %collective-permute-done.28.refs_1_ = bf16[304,1024]{1,0:T(8,128)(2,1)S(1)} collective-permute-done((bf16[304,1024]{1,0:T(8,128)(2,1)S(1)}, bf16[304,1024]{1,0:T(8,128)(2,1)S(1)}, u32[]{:S(2)}, u32[]{:S(2)}) %collective-permute-start.28) | collective-permute-done | bytes 622624 | tf_op jit(solution)/shard_map/ppermute | solution.py:1095
  147.6 4.5 %collective-permute-start.34 = (bf16[256,1024]{1,0:T(8,128)(2,1)S(1)}, bf16[256,1024]{1,0:T(8,128)(2,1)S(1)}, u32[]{:S(2)}, u32[]{:S(2)}) collective-permute-start(bf16[256,1024]{1,0:T(8,128)(2,1)S(1)} %shard_map.334.refs_17_), channel_id=1, source_target_pairs={{0,6},{1,7},{2,0},{3,1},{4,2},{5,3},{6,4},{7,5},{8,14},{9,15},{10,... | collective-permute-start | bytes 1572872 | tf_op jit(solution)/shard_map/ppermute | solution.py:1095
  152.1 8.1 %shard_map.335 = (bf16[608,384]{1,0:T(8,128)(2,1)S(1)}, bf16[608,384]{1,0:T(8,128)(2,1)S(1)}, bf16[288,1024]{1,0:T(8,128)(2,1)S(1)}, bf16[288,1024]{1,0:T(8,128)(2,1)S(1)}) custom-call(bf16[304,1024]{1,0:T(8,128)(2,1)S(1)} %get-tuple-element.158.refs_0_, bf16[304,1024]{1,0:T(8,128)(2,1)S(1)} %collective-permute-done.28.refs_1_, ...), custom_call_target="tpu_custom_call" | custom-call | flops 10000000000 | bytes 65536 | tf_op jit(solution)/shard_map/pallas_call | solution.py:439
  164.0 8.3 %shard_map.337 = (bf16[608,384]{1,0:T(8,128)(2,1)S(1)}, bf16[608,384]{1,0:T(8,128)(2,1)S(1)}, bf16[288,1024]{1,0:T(8,128)(2,1)S(1)}, bf16[288,1024]{1,0:T(8,128)(2,1)S(1)}) custom-call(bf16[304,1024]{1,0:T(8,128)(2,1)S(1)} %get-tuple-element.158.refs_0_, bf16[304,1024]{1,0:T(8,128)(2,1)S(1)} %collective-permute-done.28.refs_1_, ...), custom_call_target="tpu_custom_call" | custom-call | flops 6000000000 | bytes 65536 | tf_op jit(solution)/shard_map/pallas_call | solution.py:439
  173.9 4.3 %collective-permute-start.36 = (bf16[128,1024]{1,0:T(8,128)(2,1)S(1)}, bf16[128,1024]{1,0:T(8,128)(2,1)S(1)}, u32[]{:S(2)}, u32[]{:S(2)}) collective-permute-start(bf16[128,1024]{1,0:T(8,128)(2,1)S(1)} %get-tuple-element.175), channel_id=1, source_target_pairs={{0,6},{1,7},{2,0},{3,1},{4,2},{5,3},{6,4},{7,5},{8,14},{9,15},{10,... | collective-permute-start | bytes 786440 | tf_op jit(solution)/shard_map/ppermute | solution.py:1095
  183.8 3.9 %collective-permute-start.42 = (bf16[144,1024]{1,0:T(8,128)(2,1)S(1)}, bf16[144,1024]{1,0:T(8,128)(2,1)S(1)}, u32[]{:S(2)}, u32[]{:S(2)}) collective-permute-start(bf16[144,1024]{1,0:T(8,128)(2,1)S(1)} %get-tuple-element.191), channel_id=1, source_target_pairs={{0,6},{1,7},{2,0},{3,1},{4,2},{5,3},{6,4},{7,5},{8,14},{9,15},{10,... | collective-permute-start | bytes 884744 | tf_op jit(solution)/shard_map/ppermute | solution.py:1095
  187.8 3.3 %collective-permute-done.39.refs_10_.refs_2_ = bf16[128,1024]{1,0:T(8,128)(2,1)S(1)} collective-permute-done((bf16[128,1024]{1,0:T(8,128)(2,1)S(1)}, bf16[128,1024]{1,0:T(8,128)(2,1)S(1)}, u32[]{:S(2)}, u32[]{:S(2)}) %collective-permute-start.39) | collective-permute-done | bytes 262176 | tf_op jit(solution)/shard_map/ppermute | solution.py:1095
  193.4 4.2 %collective-permute-done.42.refs_2_ = bf16[144,1024]{1,0:T(8,128)(2,1)S(1)} collective-permute-done((bf16[144,1024]{1,0:T(8,128)(2,1)S(1)}, bf16[144,1024]{1,0:T(8,128)(2,1)S(1)}, u32[]{:S(2)}, u32[]{:S(2)}) %collective-permute-start.42) | collective-permute-done | bytes 294944 | tf_op jit(solution)/shard_map/ppermute | solution.py:1095
  197.7 3.7 %collective-permute-start.47 = (bf16[144,1024]{1,0:T(8,128)(2,1)S(1)}, bf16[144,1024]{1,0:T(8,128)(2,1)S(1)}, u32[]{:S(2)}, u32[]{:S(2)}) collective-permute-start(bf16[144,1024]{1,0:T(8,128)(2,1)S(1)} %get-tuple-element.197), channel_id=1, source_target_pairs={{0,6},{1,7},{2,0},{3,1},{4,2},{5,3},{6,4},{7,5},{8,14},{9,15},{10,... | collective-permute-start | bytes 884744 | tf_op jit(solution)/shard_map/ppermute | solution.py:1095
  201.4 2.4 %collective-permute-done.43.refs_9_.refs_2_ = bf16[144,1024]{1,0:T(8,128)(2,1)S(1)} collective-permute-done((bf16[144,1024]{1,0:T(8,128)(2,1)S(1)}, bf16[144,1024]{1,0:T(8,128)(2,1)S(1)}, u32[]{:S(2)}, u32[]{:S(2)}) %collective-permute-start.43) | collective-permute-done | bytes 294944 | tf_op jit(solution)/shard_map/ppermute | solution.py:1095
  214.3 2.8 %collective-permute-done.49.refs_4_.refs_1_.refs_3_ = f32[8,1024]{1,0:T(8,128)S(1)} collective-permute-done((f32[8,1024]{1,0:T(8,128)S(1)}, f32[8,1024]{1,0:T(8,128)S(1)}, u32[]{:S(2)}, u32[]{:S(2)}) %collective-permute-start.49) | collective-permute-done | bytes 32800 | tf_op jit(solution)/shard_map/ppermute | solution.py:1095
  218.9 5.0 %collective-permute-done.50.refs_3_.refs_1_ = bf16[144,1024]{1,0:T(8,128)(2,1)S(1)} collective-permute-done((bf16[144,1024]{1,0:T(8,128)(2,1)S(1)}, bf16[144,1024]{1,0:T(8,128)(2,1)S(1)}, u32[]{:S(2)}, u32[]{:S(2)}) %collective-permute-start.50) | collective-permute-done | bytes 294944 | tf_op jit(solution)/shard_map/ppermute | solution.py:1095
  224.3 3.1 %shard_map.351 = (f32[289,1024]{1,0:T(8,128)}, f32[289,1024]{1,0:T(8,128)}) custom-call(f32[304,1024]{1,0:T(8,128)S(1)} %get-tuple-element.186.refs_0_, f32[304,1024]{1,0:T(8,128)S(1)} %get-tuple-element.194.refs_1_, f32[16,1024]{1,0:T(8,128)S(1)} %collective-permute-done.44.refs_2_, f32[8,1024]{1,0:T(8,128)S(1)} %shard_map.350.refs_3_.refs_0_.refs_2_, ...), custom_call_target="tpu_custom_call" | custom-call | flops 10000000000 | bytes 65536 | tf_op jit(solution)/shard_map/pallas_call | solution.py:439
  (172 shorter events, 59.9 us)
Async XLA Ops:
  16.2 16.4 %collective-permute-start.2 = (bf16[304,1024]{1,0:T(8,128)(2,1)S(1)}, bf16[304,1024]{1,0:T(8,128)(2,1)S(1)}, u32[]{:S(2)}, u32[]{:S(2)}) collective-permute-start(bf16[304,1024]{1,0:T(8,128)(2,1)S(1)} %get-tuple-element.118.refs_0_.refs_4_), channel_id=1, source_target_pairs={{0,1},{1,0},{2,3},{3,2},{4,5},{5,4},{6,7},{7,6},{8,9},{9,8},{10,11... | collective-permute-start | bytes 1867784 | tf_op jit(solution)/shard_map/ppermute | solution.py:1095
  17.7 14.9 %collective-permute-start.8 = (bf16[144,1024]{1,0:T(8,128)(2,1)S(1)}, bf16[144,1024]{1,0:T(8,128)(2,1)S(1)}, u32[]{:S(2)}, u32[]{:S(2)}) collective-permute-start(bf16[144,1024]{1,0:T(8,128)(2,1)S(1)} %collective-permute-done.1.refs_7_.refs_6_.refs_12_), channel_id=1, source_target_pairs={{0,16},{1,17},{2,18},{3,19},{4,20},{5,21},{6,22},{7,23},{8,24},{9,... | collective-permute-start | bytes 884744 | tf_op jit(solution)/shard_map/ppermute | solution.py:1095
  19.2 13.4 %collective-permute-start.6 = (bf16[144,1024]{1,0:T(8,128)(2,1)S(1)}, bf16[144,1024]{1,0:T(8,128)(2,1)S(1)}, u32[]{:S(2)}, u32[]{:S(2)}) collective-permute-start(bf16[144,1024]{1,0:T(8,128)(2,1)S(1)} %collective-permute-done.1.refs_7_.refs_6_.refs_12_), channel_id=1, source_target_pairs={{0,2},{1,3},{2,4},{3,5},{4,6},{5,7},{6,0},{7,1},{8,10},{9,11},{10,... | collective-permute-start | bytes 884744 | tf_op jit(solution)/shard_map/ppermute | solution.py:1095
  19.3 22.9 %collective-permute-start.10 = (bf16[256,1024]{1,0:T(8,128)(2,1)S(1)}, bf16[256,1024]{1,0:T(8,128)(2,1)S(1)}, u32[]{:S(2)}, u32[]{:S(2)}) collective-permute-start(bf16[256,1024]{1,0:T(8,128)(2,1)S(1)} %shard_map.317.refs_1_), channel_id=1, source_target_pairs={{0,2},{1,3},{2,4},{3,5},{4,6},{5,7},{6,0},{7,1},{8,10},{9,11},{10,... | collective-permute-start | bytes 1572872 | tf_op jit(solution)/shard_map/ppermute | solution.py:1095
  32.7 22.7 %collective-permute-start.9 = (bf16[304,1024]{1,0:T(8,128)(2,1)S(1)}, bf16[304,1024]{1,0:T(8,128)(2,1)S(1)}, u32[]{:S(2)}, u32[]{:S(2)}) collective-permute-start(bf16[304,1024]{1,0:T(8,128)(2,1)S(1)} %shard_map.319.refs_8_), channel_id=1, source_target_pairs={{0,8},{1,9},{2,10},{3,11},{4,12},{5,13},{6,14},{7,15},{8,0},{9,1},... | collective-permute-start | bytes 1867784 | tf_op jit(solution)/shard_map/ppermute | solution.py:1095
  33.2 25.3 %collective-permute-start.12 = (bf16[304,1024]{1,0:T(8,128)(2,1)S(1)}, bf16[304,1024]{1,0:T(8,128)(2,1)S(1)}, u32[]{:S(2)}, u32[]{:S(2)}) collective-permute-start(bf16[304,1024]{1,0:T(8,128)(2,1)S(1)} %shard_map.319.refs_8_), channel_id=1, source_target_pairs={{0,1},{1,0},{2,3},{3,2},{4,5},{5,4},{6,7},{7,6},{8,9},{9,8},{10,11... | collective-permute-start | bytes 1867784 | tf_op jit(solution)/shard_map/ppermute | solution.py:1095
  34.8 20.1 %collective-permute-start.5 = (bf16[288,1024]{1,0:T(8,128)(2,1)S(1)}, bf16[288,1024]{1,0:T(8,128)(2,1)S(1)}, u32[]{:S(2)}, u32[]{:S(2)}) collective-permute-start(bf16[288,1024]{1,0:T(8,128)(2,1)S(1)} %get-tuple-element.119), channel_id=1, source_target_pairs={{0,6},{1,7},{2,0},{3,1},{4,2},{5,3},{6,4},{7,5},{8,14},{9,15},{10,... | collective-permute-start | bytes 1769480 | tf_op jit(solution)/shard_map/ppermute | solution.py:1095
  42.2 13.2 %collective-permute-start.7 = (bf16[144,1024]{1,0:T(8,128)(2,1)S(1)}, bf16[144,1024]{1,0:T(8,128)(2,1)S(1)}, u32[]{:S(2)}, u32[]{:S(2)}) collective-permute-start(bf16[144,1024]{1,0:T(8,128)(2,1)S(1)} %collective-permute-done.6.refs_2_.refs_3_.refs_14_), channel_id=1, source_target_pairs={{0,16},{1,17},{2,18},{3,19},{4,20},{5,21},{6,22},{7,23},{8,24},{9,... | collective-permute-start | bytes 884744 | tf_op jit(solution)/shard_map/ppermute | solution.py:1095
  42.7 37.6 %collective-permute-start.19 = (bf16[256,1024]{1,0:T(8,128)(2,1)S(1)}, bf16[256,1024]{1,0:T(8,128)(2,1)S(1)}, u32[]{:S(2)}, u32[]{:S(2)}) collective-permute-start(bf16[256,1024]{1,0:T(8,128)(2,1)S(1)} %collective-permute-done.10.refs_8_.refs_6_), channel_id=1, source_target_pairs={{0,2},{1,3},{2,4},{3,5},{4,6},{5,7},{6,0},{7,1},{8,10},{9,11},{10,... | collective-permute-start | bytes 1572872 | tf_op jit(solution)/shard_map/ppermute | solution.py:1095
  54.8 13.7 %collective-permute-start.15 = (bf16[256,1024]{1,0:T(8,128)(2,1)S(1)}, bf16[256,1024]{1,0:T(8,128)(2,1)S(1)}, u32[]{:S(2)}, u32[]{:S(2)}) collective-permute-start(bf16[256,1024]{1,0:T(8,128)(2,1)S(1)} %collective-permute-done.10.refs_8_.refs_6_), channel_id=1, source_target_pairs={{0,16},{1,17},{2,18},{3,19},{4,20},{5,21},{6,22},{7,23},{8,24},{9,... | collective-permute-start | bytes 1572872 | tf_op jit(solution)/shard_map/ppermute | solution.py:1095
  58.5 13.9 %collective-permute-start.16 = (bf16[304,1024]{1,0:T(8,128)(2,1)S(1)}, bf16[304,1024]{1,0:T(8,128)(2,1)S(1)}, u32[]{:S(2)}, u32[]{:S(2)}) collective-permute-start(bf16[304,1024]{1,0:T(8,128)(2,1)S(1)} %collective-permute-done.12.refs_3_.refs_2_.refs_4_), channel_id=1, source_target_pairs={{0,8},{1,9},{2,10},{3,11},{4,12},{5,13},{6,14},{7,15},{8,0},{9,1},... | collective-permute-start | bytes 1867784 | tf_op jit(solution)/shard_map/ppermute | solution.py:1095
  62.8 15.5 %collective-permute-start.13 = (bf16[160,1024]{1,0:T(8,128)(2,1)S(1)}, bf16[160,1024]{1,0:T(8,128)(2,1)S(1)}, u32[]{:S(2)}, u32[]{:S(2)}) collective-permute-start(bf16[160,1024]{1,0:T(8,128)(2,1)S(1)} %get-tuple-element.133), channel_id=1, source_target_pairs={{0,1},{1,0},{2,3},{3,2},{4,5},{5,4},{6,7},{7,6},{8,9},{9,8},{10,11... | collective-permute-start | bytes 983048 | tf_op jit(solution)/shard_map/ppermute | solution.py:1095
  68.5 26.5 %collective-permute-start.18 = (bf16[512,1024]{1,0:T(8,128)(2,1)S(1)}, bf16[512,1024]{1,0:T(8,128)(2,1)S(1)}, u32[]{:S(2)}, u32[]{:S(2)}) collective-permute-start(bf16[512,1024]{1,0:T(8,128)(2,1)S(1)} %shard_map.324.refs_9_), channel_id=1, source_target_pairs={{0,6},{1,7},{2,0},{3,1},{4,2},{5,3},{6,4},{7,5},{8,14},{9,15},{10,... | collective-permute-start | bytes 3145736 | tf_op jit(solution)/shard_map/ppermute | solution.py:1095
  79.8 15.2 %collective-permute-start.22 = (bf16[304,1024]{1,0:T(8,128)(2,1)S(1)}, bf16[304,1024]{1,0:T(8,128)(2,1)S(1)}, u32[]{:S(2)}, u32[]{:S(2)}) collective-permute-start(bf16[304,1024]{1,0:T(8,128)(2,1)S(1)} %get-tuple-element.136.refs_0_.refs_2_), channel_id=1, source_target_pairs={{0,1},{1,0},{2,3},{3,2},{4,5},{5,4},{6,7},{7,6},{8,9},{9,8},{10,11... | collective-permute-start | bytes 1867784 | tf_op jit(solution)/shard_map/ppermute | solution.py:1095
  80.3 14.7 %collective-permute-start.17 = (bf16[304,1024]{1,0:T(8,128)(2,1)S(1)}, bf16[304,1024]{1,0:T(8,128)(2,1)S(1)}, u32[]{:S(2)}, u32[]{:S(2)}) collective-permute-start(bf16[304,1024]{1,0:T(8,128)(2,1)S(1)} %get-tuple-element.136.refs_0_.refs_2_), channel_id=1, source_target_pairs={{0,8},{1,9},{2,10},{3,11},{4,12},{5,13},{6,14},{7,15},{8,0},{9,1},... | collective-permute-start | bytes 1867784 | tf_op jit(solution)/shard_map/ppermute | solution.py:1095
  80.3 14.7 %collective-permute-start.20 = (bf16[256,1024]{1,0:T(8,128)(2,1)S(1)}, bf16[256,1024]{1,0:T(8,128)(2,1)S(1)}, u32[]{:S(2)}, u32[]{:S(2)}) collective-permute-start(bf16[256,1024]{1,0:T(8,128)(2,1)S(1)} %collective-permute-done.19.refs_2_.refs_9_), channel_id=1, source_target_pairs={{0,16},{1,17},{2,18},{3,19},{4,20},{5,21},{6,22},{7,23},{8,24},{9,... | collective-permute-start | bytes 1572872 | tf_op jit(solution)/shard_map/ppermute | solution.py:1095
  109.4 20.2 %collective-permute-start.27 = (bf16[304,1024]{1,0:T(8,128)(2,1)S(1)}, bf16[304,1024]{1,0:T(8,128)(2,1)S(1)}, u32[]{:S(2)}, u32[]{:S(2)}) collective-permute-start(bf16[304,1024]{1,0:T(8,128)(2,1)S(1)} %shard_map.329.refs_6_), channel_id=1, source_target_pairs={{0,1},{1,0},{2,3},{3,2},{4,5},{5,4},{6,7},{7,6},{8,9},{9,8},{10,11... | collective-permute-start | bytes 1867784 | tf_op jit(solution)/shard_map/ppermute | solution.py:1095
  116.1 31.3 %collective-permute-start.31 = (bf16[256,1024]{1,0:T(8,128)(2,1)S(1)}, bf16[256,1024]{1,0:T(8,128)(2,1)S(1)}, u32[]{:S(2)}, u32[]{:S(2)}) collective-permute-start(bf16[256,1024]{1,0:T(8,128)(2,1)S(1)} %get-tuple-element.165), channel_id=1, source_target_pairs={{0,6},{1,7},{2,0},{3,1},{4,2},{5,3},{6,4},{7,5},{8,14},{9,15},{10,... | collective-permute-start | bytes 1572872 | tf_op jit(solution)/shard_map/ppermute | solution.py:1095
  124.4 38.4 %collective-permute-start.35 = (bf16[256,1024]{1,0:T(8,128)(2,1)S(1)}, bf16[256,1024]{1,0:T(8,128)(2,1)S(1)}, u32[]{:S(2)}, u32[]{:S(2)}) collective-permute-start(bf16[256,1024]{1,0:T(8,128)(2,1)S(1)} %get-tuple-element.172), channel_id=1, source_target_pairs={{0,2},{1,3},{2,4},{3,5},{4,6},{5,7},{6,0},{7,1},{8,10},{9,11},{10,... | collective-permute-start | bytes 1572872 | tf_op jit(solution)/shard_map/ppermute | solution.py:1095
  129.5 44.2 %collective-permute-start.33 = (bf16[512,1024]{1,0:T(8,128)(2,1)S(1)}, bf16[512,1024]{1,0:T(8,128)(2,1)S(1)}, u32[]{:S(2)}, u32[]{:S(2)}) collective-permute-start(bf16[512,1024]{1,0:T(8,128)(2,1)S(1)} %get-tuple-element.167), channel_id=1, source_target_pairs={{0,16},{1,17},{2,18},{3,19},{4,20},{5,21},{6,22},{7,23},{8,24},{9,... | collective-permute-start | bytes 3145736 | tf_op jit(solution)/shard_map/ppermute | solution.py:1095
  130.9 16.5 %collective-permute-start.29 = (bf16[304,1024]{1,0:T(8,128)(2,1)S(1)}, bf16[304,1024]{1,0:T(8,128)(2,1)S(1)}, u32[]{:S(2)}, u32[]{:S(2)}) collective-permute-start(bf16[304,1024]{1,0:T(8,128)(2,1)S(1)} %get-tuple-element.158.refs_0_), channel_id=1, source_target_pairs={{0,8},{1,9},{2,10},{3,11},{4,12},{5,13},{6,14},{7,15},{8,0},{9,1},... | collective-permute-start | bytes 1867784 | tf_op jit(solution)/shard_map/ppermute | solution.py:1095
  131.0 16.4 %collective-permute-start.28 = (bf16[304,1024]{1,0:T(8,128)(2,1)S(1)}, bf16[304,1024]{1,0:T(8,128)(2,1)S(1)}, u32[]{:S(2)}, u32[]{:S(2)}) collective-permute-start(bf16[304,1024]{1,0:T(8,128)(2,1)S(1)} %get-tuple-element.158.refs_0_), channel_id=1, source_target_pairs={{0,1},{1,0},{2,3},{3,2},{4,5},{5,4},{6,7},{7,6},{8,9},{9,8},{10,11... | collective-permute-start | bytes 1867784 | tf_op jit(solution)/shard_map/ppermute | solution.py:1095
  147.6 16.3 %collective-permute-start.34 = (bf16[256,1024]{1,0:T(8,128)(2,1)S(1)}, bf16[256,1024]{1,0:T(8,128)(2,1)S(1)}, u32[]{:S(2)}, u32[]{:S(2)}) collective-permute-start(bf16[256,1024]{1,0:T(8,128)(2,1)S(1)} %shard_map.334.refs_17_), channel_id=1, source_target_pairs={{0,6},{1,7},{2,0},{3,1},{4,2},{5,3},{6,4},{7,5},{8,14},{9,15},{10,... | collective-permute-start | bytes 1572872 | tf_op jit(solution)/shard_map/ppermute | solution.py:1095
  160.2 23.5 %collective-permute-start.37 = (bf16[288,1024]{1,0:T(8,128)(2,1)S(1)}, bf16[288,1024]{1,0:T(8,128)(2,1)S(1)}, u32[]{:S(2)}, u32[]{:S(2)}) collective-permute-start(bf16[288,1024]{1,0:T(8,128)(2,1)S(1)} %get-tuple-element.177), channel_id=1, source_target_pairs={{0,16},{1,17},{2,18},{3,19},{4,20},{5,21},{6,22},{7,23},{8,24},{9,... | collective-permute-start | bytes 1769480 | tf_op jit(solution)/shard_map/ppermute | solution.py:1095
  161.7 17.7 %collective-permute-start.32 = (bf16[304,1024]{1,0:T(8,128)(2,1)S(1)}, bf16[304,1024]{1,0:T(8,128)(2,1)S(1)}, u32[]{:S(2)}, u32[]{:S(2)}) collective-permute-start(bf16[304,1024]{1,0:T(8,128)(2,1)S(1)} %shard_map.336.refs_17_), channel_id=1, source_target_pairs={{0,1},{1,0},{2,3},{3,2},{4,5},{5,4},{6,7},{7,6},{8,9},{9,8},{10,11... | collective-permute-start | bytes 1867784 | tf_op jit(solution)/shard_map/ppermute | solution.py:1095
  172.2 21.1 %collective-permute-start.41 = (bf16[288,1024]{1,0:T(8,128)(2,1)S(1)}, bf16[288,1024]{1,0:T(8,128)(2,1)S(1)}, u32[]{:S(2)}, u32[]{:S(2)}) collective-permute-start(bf16[288,1024]{1,0:T(8,128)(2,1)S(1)} %get-tuple-element.190), channel_id=1, source_target_pairs={{0,16},{1,17},{2,18},{3,19},{4,20},{5,21},{6,22},{7,23},{8,24},{9,... | collective-permute-start | bytes 1769480 | tf_op jit(solution)/shard_map/ppermute | solution.py:1095
  173.9 13.8 %collective-permute-start.36 = (bf16[128,1024]{1,0:T(8,128)(2,1)S(1)}, bf16[128,1024]{1,0:T(8,128)(2,1)S(1)}, u32[]{:S(2)}, u32[]{:S(2)}) collective-permute-start(bf16[128,1024]{1,0:T(8,128)(2,1)S(1)} %get-tuple-element.175), channel_id=1, source_target_pairs={{0,6},{1,7},{2,0},{3,1},{4,2},{5,3},{6,4},{7,5},{8,14},{9,15},{10,... | collective-permute-start | bytes 786440 | tf_op jit(solution)/shard_map/ppermute | solution.py:1095
  178.3 12.8 %collective-permute-start.39 = (bf16[128,1024]{1,0:T(8,128)(2,1)S(1)}, bf16[128,1024]{1,0:T(8,128)(2,1)S(1)}, u32[]{:S(2)}, u32[]{:S(2)}) collective-permute-start(bf16[128,1024]{1,0:T(8,128)(2,1)S(1)} %get-tuple-element.185), channel_id=1, source_target_pairs={{0,2},{1,3},{2,4},{3,5},{4,6},{5,7},{6,0},{7,1},{8,10},{9,11},{10,... | collective-permute-start | bytes 786440 | tf_op jit(solution)/shard_map/ppermute | solution.py:1095
  182.6 21.2 %collective-permute-start.40 = (bf16[304,1024]{1,0:T(8,128)(2,1)S(1)}, bf16[304,1024]{1,0:T(8,128)(2,1)S(1)}, u32[]{:S(2)}, u32[]{:S(2)}) collective-permute-start(bf16[304,1024]{1,0:T(8,128)(2,1)S(1)} %shard_map.341.refs_2_), channel_id=1, source_target_pairs={{0,1},{1,0},{2,3},{3,2},{4,5},{5,4},{6,7},{7,6},{8,9},{9,8},{10,11... | collective-permute-start | bytes 1867784 | tf_op jit(solution)/shard_map/ppermute | solution.py:1095
  183.8 13.7 %collective-permute-start.42 = (bf16[144,1024]{1,0:T(8,128)(2,1)S(1)}, bf16[144,1024]{1,0:T(8,128)(2,1)S(1)}, u32[]{:S(2)}, u32[]{:S(2)}) collective-permute-start(bf16[144,1024]{1,0:T(8,128)(2,1)S(1)} %get-tuple-element.191), channel_id=1, source_target_pairs={{0,6},{1,7},{2,0},{3,1},{4,2},{5,3},{6,4},{7,5},{8,14},{9,15},{10,... | collective-permute-start | bytes 884744 | tf_op jit(solution)/shard_map/ppermute | solution.py:1095
  187.7 16.1 %collective-permute-start.43 = (bf16[144,1024]{1,0:T(8,128)(2,1)S(1)}, bf16[144,1024]{1,0:T(8,128)(2,1)S(1)}, u32[]{:S(2)}, u32[]{:S(2)}) collective-permute-start(bf16[144,1024]{1,0:T(8,128)(2,1)S(1)} %get-tuple-element.184.refs_2_), channel_id=1, source_target_pairs={{0,2},{1,3},{2,4},{3,5},{4,6},{5,7},{6,0},{7,1},{8,10},{9,11},{10,... | collective-permute-start | bytes 884744 | tf_op jit(solution)/shard_map/ppermute | solution.py:1095
  192.7 15.5 %collective-permute-start.48 = (bf16[256,1024]{1,0:T(8,128)(2,1)S(1)}, bf16[256,1024]{1,0:T(8,128)(2,1)S(1)}, u32[]{:S(2)}, u32[]{:S(2)}) collective-permute-start(bf16[256,1024]{1,0:T(8,128)(2,1)S(1)} %shard_map.345.refs_3_.refs_0_), channel_id=1, source_target_pairs={{0,16},{1,17},{2,18},{3,19},{4,20},{5,21},{6,22},{7,23},{8,24},{9,... | collective-permute-start | bytes 1572872 | tf_op jit(solution)/shard_map/ppermute | solution.py:1095
  (45 other events, 374.9 us)

commit v4 on v3

--- a/solution.py
+++ b/solution.py
@@ -334,58 +334,74 @@
     0: 6,
     1: 1,
     2: 0.01,
-    3: 30,
-    4: 1,
+    3: 1,
+    4: 0.01,
     6: 60,
     7: 6,
     8: 0.01,
     11: 6,
+    12: 10,
+    13: 1,
+    14: 10,
     15: 0.01,
+    16: 30,
+    17: 6,
     18: 10,
     19: 0.01,
     23: 0.01,
     24: 6,
     25: 0.01,
-    27: 60,
+    26: 1,
+    27: 30,
     28: 3,
-    29: 3,
+    29: 0.01,
     30: 3,
-    33: 1,
+    31: 3,
+    33: 6,
     34: 3,
     35: 0.01,
-    36: 0.01,
+    36: 1,
     37: 10,
     39: 0.01,
-    40: 10,
+    40: 1,
     44: 1,
     45: 0.01,
     46: 0.01,
 }
 EARLY = {
+    2: (2,),
     4: (6,),
+    5: (0, 7),
+    6: (8,),
     7: (2,),
     8: (6,),
     10: (11,),
+    12: (11,),
     13: (15,),
     14: (21,),
+    15: (14,),
+    17: (26,),
     18: (25,),
     20: (26,),
-    25: (33,),
     27: (36,),
     31: (39,),
-    36: (45,),
     37: (46,),
     38: (52,),
     39: (51,),
     42: (52,),
     43: (58,),
-    44: (55,),
+    44: (55, 57),
+    45: (44, 58),
     46: (52,),
 }
 LATE = {
     4: (1, 0),
+    5: (0, 1),
+    8: (0,),
+    12: (1,),
     13: (1,),
     14: (0,),
+    21: (0,),
     29: (0,),
     32: (0,),
     37: (1, 0),

time: 239 us -> 235 us (0.983)
  waiting for transfers between devices: 92.6 us -> 82 us
  starting transfers between devices: 67.8 us -> 75.6 us
    ppermute x60, waiting for transfers between devices: 92.6 us -> 82 us  [send(): found = lax.ppermute(values, AXES, pairs)]
    ppermute x60, starting transfers between devices: 67.8 us -> 75.6 us  [send(): found = lax.ppermute(values, AXES, pairs)]
  transfers between devices with their start and end apart: 60 -> 60, of which waited for: 21 -> 27; matrix products, arithmetic and copies ran while one was open for 0% -> 0% of each run, Pallas kernels for 28% -> 29%
where the time goes in v4:
time: 235 us; the launch traced here: 232 us
  waiting for transfers between devices  82 us (35%)
  starting transfers between devices  75.6 us (32%)
  Pallas kernels  71.4 us (30%)
    ppermute x60, waiting for transfers between devices, send(): found = lax.ppermute(values, AXES, pairs)  82 us
    ppermute x60, starting transfers between devices, send(): found = lax.ppermute(values, AXES, pairs)  75.6 us
    pallas_call x47, Pallas kernels, kernel_call(): pl.pallas_call(kernel, in_specs=list(specs) + [VMEM] * extra, out_specs=[...  71.4 us
  transfers between devices with their start and end apart: 60, of which 27 were waited for; matrix products, arithmetic and copies ran while one was open for 0% of the time, Pallas kernels for 29%

profile of v4, /device:TPU:0, one launch (start us, length us, event | category | flops | bytes accessed | tf_op | source)
XLA Modules:
  0.0 232.2 jit_solution(5225575668518154242)
XLA Ops:
  2.2 3.1 %collective-permute-start.1 = (bf16[144,1024]{1,0:T(8,128)(2,1)S(1)}, bf16[144,1024]{1,0:T(8,128)(2,1)S(1)}, u32[]{:S(2)}, u32[]{:S(2)}) collective-permute-start(bf16[144,1024]{1,0:T(8,128)(2,1)S(1)} %get-tuple-element.116.refs_2_.refs_4_.refs_11_), channel_id=1, source_target_pairs={{0,2},{1,3},{2,4},{3,5},{4,6},{5,7},{6,0},{7,1},{8,10},{9,11},{10,... | collective-permute-start | bytes 884744 | tf_op jit(solution)/shard_map/ppermute | solution.py:1111
  5.4 3.6 %collective-permute-start = (bf16[16,1024]{1,0:T(8,128)(2,1)S(1)}, bf16[16,1024]{1,0:T(8,128)(2,1)S(1)}, u32[]{:S(2)}, u32[]{:S(2)}) collective-permute-start(bf16[16,1024]{1,0:T(8,128)(2,1)S(1)} %shard_map.314.refs_2_), channel_id=1, source_target_pairs={{0,1},{1,2},{2,3},{3,4},{4,5},{5,6},{6,7},{8,9},{9,10},{10,11},{11... | collective-permute-start | bytes 98312 | tf_op jit(solution)/shard_map/ppermute | solution.py:1111
  10.8 3.6 %collective-permute-done.1.refs_7_.refs_2_.refs_6_.refs_12_ = bf16[144,1024]{1,0:T(8,128)(2,1)S(1)} collective-permute-done((bf16[144,1024]{1,0:T(8,128)(2,1)S(1)}, bf16[144,1024]{1,0:T(8,128)(2,1)S(1)}, u32[]{:S(2)}, u32[]{:S(2)}) %collective-permute-start.1) | collective-permute-done | bytes 294944 | tf_op jit(solution)/shard_map/ppermute | solution.py:1111
  19.9 9.5 %collective-permute-done.6.refs_3_.refs_14_ = bf16[144,1024]{1,0:T(8,128)(2,1)S(1)} collective-permute-done((bf16[144,1024]{1,0:T(8,128)(2,1)S(1)}, bf16[144,1024]{1,0:T(8,128)(2,1)S(1)}, u32[]{:S(2)}, u32[]{:S(2)}) %collective-permute-start.6) | collective-permute-done | bytes 294944 | tf_op jit(solution)/shard_map/ppermute | solution.py:1111
  32.6 8.1 %collective-permute-done.9.refs_3_.refs_8_.refs_6_ = bf16[256,1024]{1,0:T(8,128)(2,1)S(1)} collective-permute-done((bf16[256,1024]{1,0:T(8,128)(2,1)S(1)}, bf16[256,1024]{1,0:T(8,128)(2,1)S(1)}, u32[]{:S(2)}, u32[]{:S(2)}) %collective-permute-start.9) | collective-permute-done | bytes 524320 | tf_op jit(solution)/shard_map/ppermute | solution.py:1111
  44.9 5.3 %shard_map.320 = (bf16[608,384]{1,0:T(8,128)(2,1)S(1)}, bf16[608,384]{1,0:T(8,128)(2,1)S(1)}, bf16[2,608,608]{2,1,0:T(8,128)(2,1)S(1)}, bf16[2,608,608]{2,1,0:T(...) custom-call(bf16[304,1024]{1,0:T(8,128)(2,1)S(1)} %get-tuple-element, ...), custom_call_target="tpu_custom_call" | custom-call | flops 6000000000 | bytes 65536 | tf_op jit(solution)/shard_map/pallas_call | solution.py:455
  50.3 2.3 %collective-permute-done.5.refs_2_.refs_13_ = bf16[288,1024]{1,0:T(8,128)(2,1)S(1)} collective-permute-done((bf16[288,1024]{1,0:T(8,128)(2,1)S(1)}, bf16[288,1024]{1,0:T(8,128)(2,1)S(1)}, u32[]{:S(2)}, u32[]{:S(2)}) %collective-permute-start.5) | collective-permute-done | bytes 589856 | tf_op jit(solution)/shard_map/ppermute | solution.py:1111
  52.6 3.1 %shard_map.321 = (bf16[608,384]{1,0:T(8,128)(2,1)S(1)}, bf16[2,608,608]{2,1,0:T(8,128)(2,1)S(1)}, bf16[608,128]{1,0:T(8,128)(2,1)S(1)}, bf16[608,1024]{1,0:T(8,1...) custom-call(bf16[304,1024]{1,0:T(8,128)(2,1)S(1)} %collective-permute-done.3.refs_2, ...), custom_call_target="tpu_custom_call" | custom-call | flops 10000000 | bytes 65536 | tf_op jit(solution)/shard_map/pallas_call | solution.py:455
  55.7 3.1 %shard_map.322 = (bf16[608,384]{1,0:T(8,128)(2,1)S(1)}, bf16[2,608,608]{2,1,0:T(8,128)(2,1)S(1)}, bf16[608,128]{1,0:T(8,128)(2,1)S(1)}, bf16[304,1024]{1,0:T(8,128)(2,1)S(1)}, bf16[304,1024]{1,0:T(8,128)(2,1)S(1)}) custom-call(bf16[304,1024]{1,0:T(8,128)(2,1)S(1)} %get-tuple-element.118.refs_0_.refs_4_, ...), custom_call_target="tpu_custom_call" | custom-call | flops 30000001024 | bytes 65536 | tf_op jit(solution)/shard_map/pallas_call | solution.py:455
  61.2 10.9 %collective-permute-start.17 = (bf16[512,1024]{1,0:T(8,128)(2,1)S(1)}, bf16[512,1024]{1,0:T(8,128)(2,1)S(1)}, u32[]{:S(2)}, u32[]{:S(2)}) collective-permute-start(bf16[512,1024]{1,0:T(8,128)(2,1)S(1)} %shard_map.324.refs_9_), channel_id=1, source_target_pairs={{0,6},{1,7},{2,0},{3,1},{4,2},{5,3},{6,4},{7,5},{8,14},{9,15},{10,... | collective-permute-start | bytes 3145736 | tf_op jit(solution)/shard_map/ppermute | solution.py:1111
  72.1 3.4 %collective-permute-done.13.refs_3_ = bf16[160,1024]{1,0:T(8,128)(2,1)S(1)} collective-permute-done((bf16[160,1024]{1,0:T(8,128)(2,1)S(1)}, bf16[160,1024]{1,0:T(8,128)(2,1)S(1)}, u32[]{:S(2)}, u32[]{:S(2)}) %collective-permute-start.13) | collective-permute-done | bytes 327712 | tf_op jit(solution)/shard_map/ppermute | solution.py:1111
  79.3 13.3 %collective-permute-done.21.refs_0_.refs_4_ = bf16[304,1024]{1,0:T(8,128)(2,1)S(1)} collective-permute-done((bf16[304,1024]{1,0:T(8,128)(2,1)S(1)}, bf16[304,1024]{1,0:T(8,128)(2,1)S(1)}, u32[]{:S(2)}, u32[]{:S(2)}) %collective-permute-start.21) | collective-permute-done | bytes 622624 | tf_op jit(solution)/shard_map/ppermute | solution.py:1111
  93.7 5.7 %shard_map.327 = (bf16[608,1024]{1,0:T(8,128)(2,1)S(1)}, bf16[608,1024]{1,0:T(8,128)(2,1)S(1)}, bf16[304,1024]{1,0:T(8,128)(2,1)S(1)}, bf16[304,1024]{1,0:T(8,12...) custom-call(bf16[304,1024]{1,0:T(8,128)(2,1)S(1)} %get-tuple-element.136.refs_0_.re, ...), custom_call_target="tpu_custom_call" | custom-call | flops 10000000000 | bytes 65536 | tf_op jit(solution)/shard_map/pallas_call | solution.py:455
  100.0 5.7 %shard_map.328 = (bf16[608,1024]{1,0:T(8,128)(2,1)S(1)}, bf16[608,1024]{1,0:T(8,128)(2,1)S(1)}, bf16[304,1024]{1,0:T(8,128)(2,1)S(1)}, bf16[304,1024]{1,0:T(8,12...) custom-call(bf16[304,1024]{1,0:T(8,128)(2,1)S(1)} %collective-permute-done.21.refs_, ...), custom_call_target="tpu_custom_call" | custom-call | flops 10000000 | bytes 65536 | tf_op jit(solution)/shard_map/pallas_call | solution.py:455
  109.6 5.3 %shard_map.330 = (bf16[256,1024]{1,0:T(8,128)(2,1)S(1)}, bf16[256,1024]{1,0:T(8,128)(2,1)S(1)}, bf16[256,1024]{1,0:T(8,128)(2,1)S(1)}, bf16[256,1024]{1,0:T(8,128)(2,1)S(1)}) custom-call(bf16[608,1024]{1,0:T(8,128)(2,1)S(1)} %get-tuple-element.153.refs_0_, bf16[608,1024]{1,0:T(8,128)(2,1)S(1)} %get-tuple-element.154.refs_1_, ...), custom_call_target="tpu_custom_call" | custom-call | flops 6000000000 | bytes 65536 | tf_op jit(solution)/shard_map/pallas_call | solution.py:455
  114.9 7.9 %collective-permute-start.31 = (bf16[256,1024]{1,0:T(8,128)(2,1)S(1)}, bf16[256,1024]{1,0:T(8,128)(2,1)S(1)}, u32[]{:S(2)}, u32[]{:S(2)}) collective-permute-start(bf16[256,1024]{1,0:T(8,128)(2,1)S(1)} %get-tuple-element.165), channel_id=1, source_target_pairs={{0,6},{1,7},{2,0},{3,1},{4,2},{5,3},{6,4},{7,5},{8,14},{9,15},{10,... | collective-permute-start | bytes 1572872 | tf_op jit(solution)/shard_map/ppermute | solution.py:1111
  122.8 5.1 %shard_map.331 = (bf16[512,1024]{1,0:T(8,128)(2,1)S(1)}, bf16[512,1024]{1,0:T(8,128)(2,1)S(1)}) custom-call(bf16[608,1024]{1,0:T(8,128)(2,1)S(1)} %get-tuple-element.151.refs_0_, bf16[608,1024]{1,0:T(8,128)(2,1)S(1)} %get-tuple-element.152.refs_1_, bf16[304,1024]{1,0:T(8,128)(2,1)S(1)} %get-tuple-element.136.refs_0_.refs_2_, ...), custom_call_target="tpu_custom_call" | custom-call | flops 10000000000 | bytes 65536 | tf_op jit(solution)/shard_map/pallas_call | solution.py:455
  132.5 14.9 %collective-permute-done.28.refs_1_ = bf16[304,1024]{1,0:T(8,128)(2,1)S(1)} collective-permute-done((bf16[304,1024]{1,0:T(8,128)(2,1)S(1)}, bf16[304,1024]{1,0:T(8,128)(2,1)S(1)}, u32[]{:S(2)}, u32[]{:S(2)}) %collective-permute-start.28) | collective-permute-done | bytes 622624 | tf_op jit(solution)/shard_map/ppermute | solution.py:1111
  147.5 3.9 %collective-permute-start.34 = (bf16[256,1024]{1,0:T(8,128)(2,1)S(1)}, bf16[256,1024]{1,0:T(8,128)(2,1)S(1)}, u32[]{:S(2)}, u32[]{:S(2)}) collective-permute-start(bf16[256,1024]{1,0:T(8,128)(2,1)S(1)} %shard_map.334.refs_17_), channel_id=1, source_target_pairs={{0,6},{1,7},{2,0},{3,1},{4,2},{5,3},{6,4},{7,5},{8,14},{9,15},{10,... | collective-permute-start | bytes 1572872 | tf_op jit(solution)/shard_map/ppermute | solution.py:1111
  151.4 8.0 %shard_map.335 = (bf16[608,384]{1,0:T(8,128)(2,1)S(1)}, bf16[608,384]{1,0:T(8,128)(2,1)S(1)}, bf16[288,1024]{1,0:T(8,128)(2,1)S(1)}, bf16[288,1024]{1,0:T(8,128)(2,1)S(1)}) custom-call(bf16[304,1024]{1,0:T(8,128)(2,1)S(1)} %get-tuple-element.158.refs_0_, bf16[304,1024]{1,0:T(8,128)(2,1)S(1)} %collective-permute-done.28.refs_1_, ...), custom_call_target="tpu_custom_call" | custom-call | flops 10000000000 | bytes 65536 | tf_op jit(solution)/shard_map/pallas_call | solution.py:455
  163.2 8.3 %shard_map.337 = (bf16[608,384]{1,0:T(8,128)(2,1)S(1)}, bf16[608,384]{1,0:T(8,128)(2,1)S(1)}, bf16[288,1024]{1,0:T(8,128)(2,1)S(1)}, bf16[288,1024]{1,0:T(8,128)(2,1)S(1)}) custom-call(bf16[304,1024]{1,0:T(8,128)(2,1)S(1)} %get-tuple-element.158.refs_0_, bf16[304,1024]{1,0:T(8,128)(2,1)S(1)} %collective-permute-done.28.refs_1_, ...), custom_call_target="tpu_custom_call" | custom-call | flops 6000000000 | bytes 65536 | tf_op jit(solution)/shard_map/pallas_call | solution.py:455
  172.8 4.3 %collective-permute-start.36 = (bf16[128,1024]{1,0:T(8,128)(2,1)S(1)}, bf16[128,1024]{1,0:T(8,128)(2,1)S(1)}, u32[]{:S(2)}, u32[]{:S(2)}) collective-permute-start(bf16[128,1024]{1,0:T(8,128)(2,1)S(1)} %get-tuple-element.175), channel_id=1, source_target_pairs={{0,6},{1,7},{2,0},{3,1},{4,2},{5,3},{6,4},{7,5},{8,14},{9,15},{10,... | collective-permute-start | bytes 786440 | tf_op jit(solution)/shard_map/ppermute | solution.py:1111
  179.5 1.8 collective-permute-done.38.refs_1_.refs_2_
  182.6 3.9 %collective-permute-start.42 = (bf16[144,1024]{1,0:T(8,128)(2,1)S(1)}, bf16[144,1024]{1,0:T(8,128)(2,1)S(1)}, u32[]{:S(2)}, u32[]{:S(2)}) collective-permute-start(bf16[144,1024]{1,0:T(8,128)(2,1)S(1)} %get-tuple-element.191), channel_id=1, source_target_pairs={{0,6},{1,7},{2,0},{3,1},{4,2},{5,3},{6,4},{7,5},{8,14},{9,15},{10,... | collective-permute-start | bytes 884744 | tf_op jit(solution)/shard_map/ppermute | solution.py:1111
  186.5 3.5 %collective-permute-done.39.refs_10_.refs_2_ = bf16[128,1024]{1,0:T(8,128)(2,1)S(1)} collective-permute-done((bf16[128,1024]{1,0:T(8,128)(2,1)S(1)}, bf16[128,1024]{1,0:T(8,128)(2,1)S(1)}, u32[]{:S(2)}, u32[]{:S(2)}) %collective-permute-start.39) | collective-permute-done | bytes 262176 | tf_op jit(solution)/shard_map/ppermute | solution.py:1111
  192.5 3.9 %collective-permute-done.42.refs_2_ = bf16[144,1024]{1,0:T(8,128)(2,1)S(1)} collective-permute-done((bf16[144,1024]{1,0:T(8,128)(2,1)S(1)}, bf16[144,1024]{1,0:T(8,128)(2,1)S(1)}, u32[]{:S(2)}, u32[]{:S(2)}) %collective-permute-start.42) | collective-permute-done | bytes 294944 | tf_op jit(solution)/shard_map/ppermute | solution.py:1111
  196.6 3.8 %collective-permute-start.47 = (bf16[144,1024]{1,0:T(8,128)(2,1)S(1)}, bf16[144,1024]{1,0:T(8,128)(2,1)S(1)}, u32[]{:S(2)}, u32[]{:S(2)}) collective-permute-start(bf16[144,1024]{1,0:T(8,128)(2,1)S(1)} %get-tuple-element.197), channel_id=1, source_target_pairs={{0,6},{1,7},{2,0},{3,1},{4,2},{5,3},{6,4},{7,5},{8,14},{9,15},{10,... | collective-permute-start | bytes 884744 | tf_op jit(solution)/shard_map/ppermute | solution.py:1111
  200.4 2.3 collective-permute-done.43.refs_9_.refs_2_
  206.5 2.0 collective-permute-done.47.refs_1_.refs_3_
  209.5 2.0 collective-permute-start.49
  214.1 2.2 collective-permute-start.53
  220.5 3.1 %shard_map.351 = (f32[289,1024]{1,0:T(8,128)}, f32[289,1024]{1,0:T(8,128)}) custom-call(f32[304,1024]{1,0:T(8,128)S(1)} %get-tuple-element.186.refs_0_, f32[304,1024]{1,0:T(8,128)S(1)} %get-tuple-element.194.refs_1_, f32[16,1024]{1,0:T(8,128)S(1)} %collective-permute-done.44.refs_2_, f32[8,1024]{1,0:T(8,128)S(1)} %shard_map.350.refs_3_.refs_0_.refs_2_, ...), custom_call_target="tpu_custom_call" | custom-call | flops 10000000000 | bytes 65536 | tf_op jit(solution)/shard_map/pallas_call | solution.py:455
  (162 shorter events, 63.4 us)
Async XLA Ops:
  2.2 12.1 %collective-permute-start.1 = (bf16[144,1024]{1,0:T(8,128)(2,1)S(1)}, bf16[144,1024]{1,0:T(8,128)(2,1)S(1)}, u32[]{:S(2)}, u32[]{:S(2)}) collective-permute-start(bf16[144,1024]{1,0:T(8,128)(2,1)S(1)} %get-tuple-element.116.refs_2_.refs_4_.refs_11_), channel_id=1, source_target_pairs={{0,2},{1,3},{2,4},{3,5},{4,6},{5,7},{6,0},{7,1},{8,10},{9,11},{10,... | collective-permute-start | bytes 884744 | tf_op jit(solution)/shard_map/ppermute | solution.py:1111
  16.1 16.4 %collective-permute-start.2 = (bf16[304,1024]{1,0:T(8,128)(2,1)S(1)}, bf16[304,1024]{1,0:T(8,128)(2,1)S(1)}, u32[]{:S(2)}, u32[]{:S(2)}) collective-permute-start(bf16[304,1024]{1,0:T(8,128)(2,1)S(1)} %get-tuple-element.118.refs_0_.refs_4_), channel_id=1, source_target_pairs={{0,1},{1,0},{2,3},{3,2},{4,5},{5,4},{6,7},{7,6},{8,9},{9,8},{10,11... | collective-permute-start | bytes 1867784 | tf_op jit(solution)/shard_map/ppermute | solution.py:1111
  18.2 22.5 %collective-permute-start.9 = (bf16[256,1024]{1,0:T(8,128)(2,1)S(1)}, bf16[256,1024]{1,0:T(8,128)(2,1)S(1)}, u32[]{:S(2)}, u32[]{:S(2)}) collective-permute-start(bf16[256,1024]{1,0:T(8,128)(2,1)S(1)} %shard_map.317.refs_1_), channel_id=1, source_target_pairs={{0,2},{1,3},{2,4},{3,5},{4,6},{5,7},{6,0},{7,1},{8,10},{9,11},{10,... | collective-permute-start | bytes 1572872 | tf_op jit(solution)/shard_map/ppermute | solution.py:1111
  30.9 21.7 %collective-permute-start.5 = (bf16[288,1024]{1,0:T(8,128)(2,1)S(1)}, bf16[288,1024]{1,0:T(8,128)(2,1)S(1)}, u32[]{:S(2)}, u32[]{:S(2)}) collective-permute-start(bf16[288,1024]{1,0:T(8,128)(2,1)S(1)} %get-tuple-element.119), channel_id=1, source_target_pairs={{0,6},{1,7},{2,0},{3,1},{4,2},{5,3},{6,4},{7,5},{8,14},{9,15},{10,... | collective-permute-start | bytes 1769480 | tf_op jit(solution)/shard_map/ppermute | solution.py:1111
  31.3 11.9 %collective-permute-start.8 = (bf16[144,1024]{1,0:T(8,128)(2,1)S(1)}, bf16[144,1024]{1,0:T(8,128)(2,1)S(1)}, u32[]{:S(2)}, u32[]{:S(2)}) collective-permute-start(bf16[144,1024]{1,0:T(8,128)(2,1)S(1)} %collective-permute-done.1.refs_7_.refs_2_.refs_6_.refs_12_), channel_id=1, source_target_pairs={{0,16},{1,17},{2,18},{3,19},{4,20},{5,21},{6,22},{7,23},{8,24},{9,... | collective-permute-start | bytes 884744 | tf_op jit(solution)/shard_map/ppermute | solution.py:1111
  40.8 18.0 %collective-permute-start.12 = (bf16[304,1024]{1,0:T(8,128)(2,1)S(1)}, bf16[304,1024]{1,0:T(8,128)(2,1)S(1)}, u32[]{:S(2)}, u32[]{:S(2)}) collective-permute-start(bf16[304,1024]{1,0:T(8,128)(2,1)S(1)} %shard_map.319.refs_8_), channel_id=1, source_target_pairs={{0,8},{1,9},{2,10},{3,11},{4,12},{5,13},{6,14},{7,15},{8,0},{9,1},... | collective-permute-start | bytes 1867784 | tf_op jit(solution)/shard_map/ppermute | solution.py:1111
  40.8 18.0 %collective-permute-start.11 = (bf16[304,1024]{1,0:T(8,128)(2,1)S(1)}, bf16[304,1024]{1,0:T(8,128)(2,1)S(1)}, u32[]{:S(2)}, u32[]{:S(2)}) collective-permute-start(bf16[304,1024]{1,0:T(8,128)(2,1)S(1)} %shard_map.319.refs_8_), channel_id=1, source_target_pairs={{0,1},{1,0},{2,3},{3,2},{4,5},{5,4},{6,7},{7,6},{8,9},{9,8},{10,11... | collective-permute-start | bytes 1867784 | tf_op jit(solution)/shard_map/ppermute | solution.py:1111
  43.2 34.4 %collective-permute-start.18 = (bf16[256,1024]{1,0:T(8,128)(2,1)S(1)}, bf16[256,1024]{1,0:T(8,128)(2,1)S(1)}, u32[]{:S(2)}, u32[]{:S(2)}) collective-permute-start(bf16[256,1024]{1,0:T(8,128)(2,1)S(1)} %collective-permute-done.9.refs_3_.refs_8_.refs_6_), channel_id=1, source_target_pairs={{0,2},{1,3},{2,4},{3,5},{4,6},{5,7},{6,0},{7,1},{8,10},{9,11},{10,... | collective-permute-start | bytes 1572872 | tf_op jit(solution)/shard_map/ppermute | solution.py:1111
  43.4 28.7 %collective-permute-start.15 = (bf16[256,1024]{1,0:T(8,128)(2,1)S(1)}, bf16[256,1024]{1,0:T(8,128)(2,1)S(1)}, u32[]{:S(2)}, u32[]{:S(2)}) collective-permute-start(bf16[256,1024]{1,0:T(8,128)(2,1)S(1)} %collective-permute-done.9.refs_3_.refs_8_.refs_6_), channel_id=1, source_target_pairs={{0,16},{1,17},{2,18},{3,19},{4,20},{5,21},{6,22},{7,23},{8,24},{9,... | collective-permute-start | bytes 1572872 | tf_op jit(solution)/shard_map/ppermute | solution.py:1111
  59.0 13.1 %collective-permute-start.14 = (bf16[144,1024]{1,0:T(8,128)(2,1)S(1)}, bf16[144,1024]{1,0:T(8,128)(2,1)S(1)}, u32[]{:S(2)}, u32[]{:S(2)}) collective-permute-start(bf16[144,1024]{1,0:T(8,128)(2,1)S(1)} %get-tuple-element.134.refs_1_), channel_id=1, source_target_pairs={{0,1},{1,0},{2,3},{3,2},{4,5},{5,4},{6,7},{7,6},{8,9},{9,8},{10,11... | collective-permute-start | bytes 884744 | tf_op jit(solution)/shard_map/ppermute | solution.py:1111
  59.7 15.8 %collective-permute-start.13 = (bf16[160,1024]{1,0:T(8,128)(2,1)S(1)}, bf16[160,1024]{1,0:T(8,128)(2,1)S(1)}, u32[]{:S(2)}, u32[]{:S(2)}) collective-permute-start(bf16[160,1024]{1,0:T(8,128)(2,1)S(1)} %get-tuple-element.133), channel_id=1, source_target_pairs={{0,1},{1,0},{2,3},{3,2},{4,5},{5,4},{6,7},{7,6},{8,9},{9,8},{10,11... | collective-permute-start | bytes 983048 | tf_op jit(solution)/shard_map/ppermute | solution.py:1111
  61.2 32.6 %collective-permute-start.17 = (bf16[512,1024]{1,0:T(8,128)(2,1)S(1)}, bf16[512,1024]{1,0:T(8,128)(2,1)S(1)}, u32[]{:S(2)}, u32[]{:S(2)}) collective-permute-start(bf16[512,1024]{1,0:T(8,128)(2,1)S(1)} %shard_map.324.refs_9_), channel_id=1, source_target_pairs={{0,6},{1,7},{2,0},{3,1},{4,2},{5,3},{6,4},{7,5},{8,14},{9,15},{10,... | collective-permute-start | bytes 3145736 | tf_op jit(solution)/shard_map/ppermute | solution.py:1111
  76.9 15.7 %collective-permute-start.21 = (bf16[304,1024]{1,0:T(8,128)(2,1)S(1)}, bf16[304,1024]{1,0:T(8,128)(2,1)S(1)}, u32[]{:S(2)}, u32[]{:S(2)}) collective-permute-start(bf16[304,1024]{1,0:T(8,128)(2,1)S(1)} %get-tuple-element.136.refs_0_.refs_2_), channel_id=1, source_target_pairs={{0,1},{1,0},{2,3},{3,2},{4,5},{5,4},{6,7},{7,6},{8,9},{9,8},{10,11... | collective-permute-start | bytes 1867784 | tf_op jit(solution)/shard_map/ppermute | solution.py:1111
  77.6 15.0 %collective-permute-start.16 = (bf16[304,1024]{1,0:T(8,128)(2,1)S(1)}, bf16[304,1024]{1,0:T(8,128)(2,1)S(1)}, u32[]{:S(2)}, u32[]{:S(2)}) collective-permute-start(bf16[304,1024]{1,0:T(8,128)(2,1)S(1)} %get-tuple-element.136.refs_0_.refs_2_), channel_id=1, source_target_pairs={{0,8},{1,9},{2,10},{3,11},{4,12},{5,13},{6,14},{7,15},{8,0},{9,1},... | collective-permute-start | bytes 1867784 | tf_op jit(solution)/shard_map/ppermute | solution.py:1111
  77.6 15.0 %collective-permute-start.19 = (bf16[256,1024]{1,0:T(8,128)(2,1)S(1)}, bf16[256,1024]{1,0:T(8,128)(2,1)S(1)}, u32[]{:S(2)}, u32[]{:S(2)}) collective-permute-start(bf16[256,1024]{1,0:T(8,128)(2,1)S(1)} %collective-permute-done.18.refs_2_.refs_9_), channel_id=1, source_target_pairs={{0,16},{1,17},{2,18},{3,19},{4,20},{5,21},{6,22},{7,23},{8,24},{9,... | collective-permute-start | bytes 1572872 | tf_op jit(solution)/shard_map/ppermute | solution.py:1111
  79.1 21.0 %collective-permute-start.23 = (bf16[304,1024]{1,0:T(8,128)(2,1)S(1)}, bf16[304,1024]{1,0:T(8,128)(2,1)S(1)}, u32[]{:S(2)}, u32[]{:S(2)}) collective-permute-start(bf16[304,1024]{1,0:T(8,128)(2,1)S(1)} %collective-permute-done.11.refs_3_.refs_2_.refs_4_), channel_id=1, source_target_pairs={{0,8},{1,9},{2,10},{3,11},{4,12},{5,13},{6,14},{7,15},{8,0},{9,1},... | collective-permute-start | bytes 1867784 | tf_op jit(solution)/shard_map/ppermute | solution.py:1111
  108.0 21.5 %collective-permute-start.27 = (bf16[304,1024]{1,0:T(8,128)(2,1)S(1)}, bf16[304,1024]{1,0:T(8,128)(2,1)S(1)}, u32[]{:S(2)}, u32[]{:S(2)}) collective-permute-start(bf16[304,1024]{1,0:T(8,128)(2,1)S(1)} %shard_map.329.refs_6_), channel_id=1, source_target_pairs={{0,1},{1,0},{2,3},{3,2},{4,5},{5,4},{6,7},{7,6},{8,9},{9,8},{10,11... | collective-permute-start | bytes 1867784 | tf_op jit(solution)/shard_map/ppermute | solution.py:1111
  114.9 32.5 %collective-permute-start.31 = (bf16[256,1024]{1,0:T(8,128)(2,1)S(1)}, bf16[256,1024]{1,0:T(8,128)(2,1)S(1)}, u32[]{:S(2)}, u32[]{:S(2)}) collective-permute-start(bf16[256,1024]{1,0:T(8,128)(2,1)S(1)} %get-tuple-element.165), channel_id=1, source_target_pairs={{0,6},{1,7},{2,0},{3,1},{4,2},{5,3},{6,4},{7,5},{8,14},{9,15},{10,... | collective-permute-start | bytes 1572872 | tf_op jit(solution)/shard_map/ppermute | solution.py:1111
  122.8 38.6 %collective-permute-start.35 = (bf16[256,1024]{1,0:T(8,128)(2,1)S(1)}, bf16[256,1024]{1,0:T(8,128)(2,1)S(1)}, u32[]{:S(2)}, u32[]{:S(2)}) collective-permute-start(bf16[256,1024]{1,0:T(8,128)(2,1)S(1)} %get-tuple-element.172), channel_id=1, source_target_pairs={{0,2},{1,3},{2,4},{3,5},{4,6},{5,7},{6,0},{7,1},{8,10},{9,11},{10,... | collective-permute-start | bytes 1572872 | tf_op jit(solution)/shard_map/ppermute | solution.py:1111
  128.0 44.6 %collective-permute-start.33 = (bf16[512,1024]{1,0:T(8,128)(2,1)S(1)}, bf16[512,1024]{1,0:T(8,128)(2,1)S(1)}, u32[]{:S(2)}, u32[]{:S(2)}) collective-permute-start(bf16[512,1024]{1,0:T(8,128)(2,1)S(1)} %get-tuple-element.167), channel_id=1, source_target_pairs={{0,16},{1,17},{2,18},{3,19},{4,20},{5,21},{6,22},{7,23},{8,24},{9,... | collective-permute-start | bytes 3145736 | tf_op jit(solution)/shard_map/ppermute | solution.py:1111
  130.9 20.5 %collective-permute-start.29 = (bf16[304,1024]{1,0:T(8,128)(2,1)S(1)}, bf16[304,1024]{1,0:T(8,128)(2,1)S(1)}, u32[]{:S(2)}, u32[]{:S(2)}) collective-permute-start(bf16[304,1024]{1,0:T(8,128)(2,1)S(1)} %get-tuple-element.158.refs_0_), channel_id=1, source_target_pairs={{0,8},{1,9},{2,10},{3,11},{4,12},{5,13},{6,14},{7,15},{8,0},{9,1},... | collective-permute-start | bytes 1867784 | tf_op jit(solution)/shard_map/ppermute | solution.py:1111
  130.9 16.4 %collective-permute-start.28 = (bf16[304,1024]{1,0:T(8,128)(2,1)S(1)}, bf16[304,1024]{1,0:T(8,128)(2,1)S(1)}, u32[]{:S(2)}, u32[]{:S(2)}) collective-permute-start(bf16[304,1024]{1,0:T(8,128)(2,1)S(1)} %get-tuple-element.158.refs_0_), channel_id=1, source_target_pairs={{0,1},{1,0},{2,3},{3,2},{4,5},{5,4},{6,7},{7,6},{8,9},{9,8},{10,11... | collective-permute-start | bytes 1867784 | tf_op jit(solution)/shard_map/ppermute | solution.py:1111
  147.5 15.7 %collective-permute-start.34 = (bf16[256,1024]{1,0:T(8,128)(2,1)S(1)}, bf16[256,1024]{1,0:T(8,128)(2,1)S(1)}, u32[]{:S(2)}, u32[]{:S(2)}) collective-permute-start(bf16[256,1024]{1,0:T(8,128)(2,1)S(1)} %shard_map.334.refs_17_), channel_id=1, source_target_pairs={{0,6},{1,7},{2,0},{3,1},{4,2},{5,3},{6,4},{7,5},{8,14},{9,15},{10,... | collective-permute-start | bytes 1572872 | tf_op jit(solution)/shard_map/ppermute | solution.py:1111
  159.4 23.0 %collective-permute-start.37 = (bf16[288,1024]{1,0:T(8,128)(2,1)S(1)}, bf16[288,1024]{1,0:T(8,128)(2,1)S(1)}, u32[]{:S(2)}, u32[]{:S(2)}) collective-permute-start(bf16[288,1024]{1,0:T(8,128)(2,1)S(1)} %get-tuple-element.177), channel_id=1, source_target_pairs={{0,16},{1,17},{2,18},{3,19},{4,20},{5,21},{6,22},{7,23},{8,24},{9,... | collective-permute-start | bytes 1769480 | tf_op jit(solution)/shard_map/ppermute | solution.py:1111
  160.5 17.8 %collective-permute-start.32 = (bf16[304,1024]{1,0:T(8,128)(2,1)S(1)}, bf16[304,1024]{1,0:T(8,128)(2,1)S(1)}, u32[]{:S(2)}, u32[]{:S(2)}) collective-permute-start(bf16[304,1024]{1,0:T(8,128)(2,1)S(1)} %shard_map.336.refs_17_), channel_id=1, source_target_pairs={{0,1},{1,0},{2,3},{3,2},{4,5},{5,4},{6,7},{7,6},{8,9},{9,8},{10,11... | collective-permute-start | bytes 1867784 | tf_op jit(solution)/shard_map/ppermute | solution.py:1111
  171.5 20.9 %collective-permute-start.41 = (bf16[288,1024]{1,0:T(8,128)(2,1)S(1)}, bf16[288,1024]{1,0:T(8,128)(2,1)S(1)}, u32[]{:S(2)}, u32[]{:S(2)}) collective-permute-start(bf16[288,1024]{1,0:T(8,128)(2,1)S(1)} %get-tuple-element.190), channel_id=1, source_target_pairs={{0,16},{1,17},{2,18},{3,19},{4,20},{5,21},{6,22},{7,23},{8,24},{9,... | collective-permute-start | bytes 1769480 | tf_op jit(solution)/shard_map/ppermute | solution.py:1111
  172.8 13.6 %collective-permute-start.36 = (bf16[128,1024]{1,0:T(8,128)(2,1)S(1)}, bf16[128,1024]{1,0:T(8,128)(2,1)S(1)}, u32[]{:S(2)}, u32[]{:S(2)}) collective-permute-start(bf16[128,1024]{1,0:T(8,128)(2,1)S(1)} %get-tuple-element.175), channel_id=1, source_target_pairs={{0,6},{1,7},{2,0},{3,1},{4,2},{5,3},{6,4},{7,5},{8,14},{9,15},{10,... | collective-permute-start | bytes 786440 | tf_op jit(solution)/shard_map/ppermute | solution.py:1111
  177.1 12.9 %collective-permute-start.39 = (bf16[128,1024]{1,0:T(8,128)(2,1)S(1)}, bf16[128,1024]{1,0:T(8,128)(2,1)S(1)}, u32[]{:S(2)}, u32[]{:S(2)}) collective-permute-start(bf16[128,1024]{1,0:T(8,128)(2,1)S(1)} %get-tuple-element.185), channel_id=1, source_target_pairs={{0,2},{1,3},{2,4},{3,5},{4,6},{5,7},{6,0},{7,1},{8,10},{9,11},{10,... | collective-permute-start | bytes 786440 | tf_op jit(solution)/shard_map/ppermute | solution.py:1111
  181.5 21.2 %collective-permute-start.40 = (bf16[304,1024]{1,0:T(8,128)(2,1)S(1)}, bf16[304,1024]{1,0:T(8,128)(2,1)S(1)}, u32[]{:S(2)}, u32[]{:S(2)}) collective-permute-start(bf16[304,1024]{1,0:T(8,128)(2,1)S(1)} %shard_map.341.refs_2_), channel_id=1, source_target_pairs={{0,1},{1,0},{2,3},{3,2},{4,5},{5,4},{6,7},{7,6},{8,9},{9,8},{10,11... | collective-permute-start | bytes 1867784 | tf_op jit(solution)/shard_map/ppermute | solution.py:1111
  182.6 13.8 %collective-permute-start.42 = (bf16[144,1024]{1,0:T(8,128)(2,1)S(1)}, bf16[144,1024]{1,0:T(8,128)(2,1)S(1)}, u32[]{:S(2)}, u32[]{:S(2)}) collective-permute-start(bf16[144,1024]{1,0:T(8,128)(2,1)S(1)} %get-tuple-element.191), channel_id=1, source_target_pairs={{0,6},{1,7},{2,0},{3,1},{4,2},{5,3},{6,4},{7,5},{8,14},{9,15},{10,... | collective-permute-start | bytes 884744 | tf_op jit(solution)/shard_map/ppermute | solution.py:1111
  186.5 16.2 %collective-permute-start.43 = (bf16[144,1024]{1,0:T(8,128)(2,1)S(1)}, bf16[144,1024]{1,0:T(8,128)(2,1)S(1)}, u32[]{:S(2)}, u32[]{:S(2)}) collective-permute-start(bf16[144,1024]{1,0:T(8,128)(2,1)S(1)} %get-tuple-element.184.refs_2_), channel_id=1, source_target_pairs={{0,2},{1,3},{2,4},{3,5},{4,6},{5,7},{6,0},{7,1},{8,10},{9,11},{10,... | collective-permute-start | bytes 884744 | tf_op jit(solution)/shard_map/ppermute | solution.py:1111
  191.6 14.9 %collective-permute-start.48 = (bf16[256,1024]{1,0:T(8,128)(2,1)S(1)}, bf16[256,1024]{1,0:T(8,128)(2,1)S(1)}, u32[]{:S(2)}, u32[]{:S(2)}) collective-permute-start(bf16[256,1024]{1,0:T(8,128)(2,1)S(1)} %shard_map.345.refs_3_.refs_0_), channel_id=1, source_target_pairs={{0,16},{1,17},{2,18},{3,19},{4,20},{5,21},{6,22},{7,23},{8,24},{9,... | collective-permute-start | bytes 1572872 | tf_op jit(solution)/shard_map/ppermute | solution.py:1111
  (40 other events, 279.3 us)
